TPU v7x, 128 devices: a whole 4x4x4 slice. The times are simulated.
128 devices in a mesh: ctx: 16 (over y, x_hi, core), tp: 8 (over z, x_lo).
Axes of the slice: x: 4 (x_hi: 2, x_lo: 2; x = x_hi * 2 + x_lo), y: 4, z: 4, core: 2. Of those that a mesh axis runs over, the one named last changes fastest.
Arguments:
- hidden_in: bfloat16 [8192, 4096], P(('ctx', 'tp')), may hold values from -24 to 24
- cotangent: bfloat16 [8192, 4096], P(('ctx', 'tp')), may hold values from -24 to 24
- norm_gain: float32 [4096], replicated, may hold values from 0.1 to 1.9
- in_weight: bfloat16 [4096, 3, 4096], P(None, None, 'tp'), may hold values from -0.09375 to 0.09375
- filter_taps: float32 [3, 3, 4096], P(None, None, 'tp'), may hold values from -3 to 3
- inner_taps: float32 [7, 4096], P(None, 'tp'), may hold values from -3 to 3
- out_weight: bfloat16 [4096, 4096], P('tp'), may hold values from -0.09375 to 0.09375
Outputs:
- layer_out: bfloat16 [8192, 4096], P(('ctx', 'tp'))
- grad_input: bfloat16 [8192, 4096], P(('ctx', 'tp'))
- grad_in_weight: bfloat16 [4096, 3, 4096], P('ctx', None, 'tp')
- grad_out_weight: bfloat16 [4096, 4096], P('tp', 'ctx')
- grad_filter: float32 [3, 3, 4096], P(None, None, 'tp')
- grad_inner: float32 [7, 4096], P(None, 'tp')
All inputs are finite; a program needn't handle non-finite values.
Results may differ from a plain program's by a relative error of at most 0.025.
Values may be sent and summed in bfloat16 or wider, within the bound.
A program may use at most 192 MiB of HBM per device.

v0:
```python
import jax
import jax.numpy as jnp
from jax import lax
from jax.sharding import PartitionSpec as P


def passed_along(value, axis, steps):
    count = lax.axis_size(axis)
    first, last = (max(0, -steps), min(count, count - steps))
    return lax.ppermute(value, axis, [(source, source + steps) for source in range(first, last)])


def normed(values, gain):
    floats = values.astype(jnp.float32)
    factor = lax.rsqrt(jnp.mean(floats * floats, axis=-1, keepdims=True) + 1e-05)
    return floats * factor * gain


def taps_causal(extended, taps, number):
    count = taps.shape[0]
    summed = jnp.zeros((number,) + extended.shape[1:], jnp.float32)
    for tap_index in range(count):
        begin = count - 1 - tap_index
        summed = summed + taps[tap_index] * extended[begin : begin + number]
    return summed


def taps_ahead(extended, taps, number):
    count = taps.shape[0]
    summed = jnp.zeros((number,) + extended.shape[1:], jnp.float32)
    for tap_index in range(count):
        summed = summed + taps[tap_index] * extended[tap_index : tap_index + number]
    return summed


def lagged_sums(grads, extended, number, count):
    pieces = []
    for tap_index in range(count):
        begin = count - 1 - tap_index
        pieces.append(jnp.sum(grads * extended[begin : begin + number], axis=0))
    return jnp.stack(pieces)


def local(hidden_in, cotangent, norm_gain, in_weight, filter_taps, inner_taps, out_weight):
    rows_local = hidden_in.shape[0]
    model_width = hidden_in.shape[1]
    channels = in_weight.shape[2]
    block_rows = rows_local * lax.axis_size("tp")
    loss_scale = (block_rows * lax.axis_size("ctx")) ** (-0.5)
    short_edge = filter_taps.shape[0] - 1
    inner_edge = inner_taps.shape[0] - 1
    reach = short_edge + inner_edge
    normal_rows = normed(hidden_in, norm_gain).astype(jnp.bfloat16)
    flat_in = in_weight.reshape(model_width, 3 * channels)
    gathered = lax.all_gather(normal_rows, "tp", axis=0, tiled=True)
    projected = jnp.dot(gathered, flat_in, preferred_element_type=jnp.float32).astype(jnp.bfloat16)
    projected = projected.reshape(block_rows, 3, channels)
    earlier = passed_along(projected[block_rows - reach :], "ctx", 1)
    blended = taps_causal(
        jnp.concatenate([earlier, projected]), filter_taps, block_rows + inner_edge
    )
    features = blended[inner_edge:]
    before = blended[:inner_edge, 1] * blended[:inner_edge, 2]
    shifted_in = jnp.concatenate([earlier[inner_edge:], projected])
    query_vals = features[:, 0]
    key_vals = features[:, 1]
    value_vals = features[:, 2]
    wide_prods = jnp.concatenate([before, key_vals * value_vals])
    gate_vals = taps_causal(wide_prods, inner_taps, block_rows)
    mixed = (query_vals * gate_vals).astype(jnp.bfloat16)
    rows_part = mixed
    branch = lax.psum_scatter(
        jnp.dot(rows_part, out_weight, preferred_element_type=jnp.float32).astype(jnp.bfloat16),
        "tp",
        scatter_dimension=0,
        tiled=True,
    ).astype(jnp.float32)
    layer_out = (hidden_in.astype(jnp.float32) + branch).astype(jnp.bfloat16)
    grad_all = lax.all_gather(cotangent, "tp", axis=0, tiled=True)
    grad_mixed = lax.dot_general(
        grad_all, out_weight, (((1,), (1,)), ((), ())), preferred_element_type=jnp.float32
    )
    out_partial = (
        lax.dot_general(
            mixed, grad_all, (((0,), (0,)), ((), ())), preferred_element_type=jnp.float32
        )
        * loss_scale
    )
    grad_out_weight = lax.psum_scatter(
        out_partial.astype(jnp.bfloat16), "ctx", scatter_dimension=1, tiled=True
    )
    grad_query = grad_mixed * gate_vals
    grad_gates = grad_mixed * query_vals
    head_prod = taps_ahead(grad_gates[:reach], inner_taps, short_edge)
    head_feat = jnp.stack(
        [
            grad_query[:short_edge],
            head_prod * value_vals[:short_edge],
            head_prod * key_vals[:short_edge],
        ],
        axis=1,
    )
    next_gates, next_feat = passed_along((grad_gates[:inner_edge], head_feat), "ctx", -1)
    grad_products = taps_ahead(jnp.concatenate([grad_gates, next_gates]), inner_taps, block_rows)
    grad_features = jnp.stack(
        [grad_query, grad_products * value_vals, grad_products * key_vals], axis=1
    )
    filter_part = lagged_sums(grad_features, shifted_in, block_rows, short_edge + 1) * loss_scale
    inner_part = lagged_sums(grad_gates, wide_prods, block_rows, inner_edge + 1) * loss_scale
    grad_filter, grad_inner = (
        lax.psum(filter_part.astype(jnp.bfloat16), "ctx").astype(jnp.float32),
        lax.psum(inner_part.astype(jnp.bfloat16), "ctx").astype(jnp.float32),
    )
    grad_proj = taps_ahead(
        jnp.concatenate([grad_features, next_feat]), filter_taps, block_rows
    ).astype(jnp.bfloat16)
    flat_grad = grad_proj.reshape(block_rows, 3 * channels)
    rows_part = flat_grad
    grad_normed = lax.psum_scatter(
        lax.dot_general(
            rows_part, flat_in, (((1,), (1,)), ((), ())), preferred_element_type=jnp.float32
        ).astype(jnp.bfloat16),
        "tp",
        scatter_dimension=0,
        tiled=True,
    ).astype(jnp.float32)
    _, pullback = jax.vjp(lambda values: normed(values, norm_gain), hidden_in.astype(jnp.float32))
    grad_input = (cotangent.astype(jnp.float32) + pullback(grad_normed)[0]).astype(jnp.bfloat16)
    in_partial = lax.dot_general(
        gathered, flat_grad, (((0,), (0,)), ((), ())), preferred_element_type=jnp.float32
    )
    scaled_in = (in_partial * loss_scale).reshape(model_width, 3, channels)
    grad_in_weight = lax.psum_scatter(
        scaled_in.astype(jnp.bfloat16), "ctx", scatter_dimension=0, tiled=True
    )
    return (layer_out, grad_input, grad_in_weight, grad_out_weight, grad_filter, grad_inner)


def solution(mesh):
    placed = (
        P(("ctx", "tp"), None),
        P(("ctx", "tp"), None),
        P(),
        P(None, None, "tp"),
        P(None, None, "tp"),
        P(None, "tp"),
        P("tp", None),
    )
    return jax.shard_map(
        local,
        mesh=mesh,
        in_specs=placed,
        out_specs=(
            P(("ctx", "tp"), None),
            P(("ctx", "tp"), None),
            P("ctx", None, "tp"),
            P("tp", "ctx"),
            P(None, None, "tp"),
            P(None, "tp"),
        ),
        check_vma=False,
    )
```

profile of v0, /device:TPU:0, one launch (start us, length us, event | category | flops | bytes accessed | tf_op | source)
XLA Modules:
  0.0 638.5 jit_solution(6486723572044766842)
XLA Ops:
  7.2 0.0 all-gather.3.cloned.1.call-start
  7.2 1.2 fusion.8
  8.5 2.0 fusion.10
  10.5 0.0 all-gather.3.cloned.1.call-update
  10.5 0.0 all-gather.5.cloned.1.call-start
  10.6 0.7 all-gather.5.cloned.1.call-update
  11.3 0.0 copy-start.5
  11.3 0.0 reduce-scatter.7.cloned.1.call-start
  11.3 16.9 %copy.17 = bf16[4096,3,512]{0,2,1:T(8,128)(2,1)} copy(bf16[4096,3,512]{2,0,1:T(8,128)(2,1)} %param.10) | data formatting | bytes 25165824 | tf_op args[3]
  28.3 0.0 copy-done.5
  28.3 75.8 %all-gather.3.cloned.1.call-done = bf16[512,4096]{1,0:T(8,128)(2,1)} async-done(((bf16[64,4096]{1,0:T(8,128)(2,1)}), bf16[512,4096]{1,0:T(8,128)(2,1)}) %all-gather.3.cloned.1.call-update) | async-done | bytes 4194320 | tf_op jit(solution)/shard_map/all_gather | solution.py:55
  104.1 11.0 %convolution_convert_fusion.1 = bf16[512,1536]{1,0:T(8,128)(2,1)S(1)} fusion(bf16[512,4096]{1,0:T(8,128)(2,1)} %all-gather.3.cloned.1.call-done, bf16[4096,1536]{0,1:T(8,128)(2,1)} %bitcast.88), kind=kOutput, calls=%fused_computation.15 | convolution fusion | flops 6443237376 | bytes 18350080 | tf_op jit(solution)/shard_map/dot_general | solution.py:56
  115.0 0.0 copy-start.1
  115.1 1.5 collective-permute-start
  116.6 0.0 copy-done.6
  116.6 0.7 copy.18
  117.3 1.6 copy.19
  118.9 0.0 collective-permute-done
  118.9 0.0 copy-done.1
  118.9 3.3 multiply_add_fusion
  122.3 1.2 fusion.36
  123.5 73.3 %all-gather.5.cloned.1.call-done = bf16[512,4096]{1,0:T(8,128)(2,1)} async-done(((bf16[64,4096]{1,0:T(8,128)(2,1)}), bf16[512,4096]{1,0:T(8,128)(2,1)}) %all-gather.5.cloned.1.call-update) | async-done | bytes 4194320 | tf_op jit(solution)/shard_map/all_gather | solution.py:79
  196.8 9.4 %multiply_reduce_fusion.3 = (f32[512]{0:T(512)S(1)}, f32[512]{0:T(512)S(1)}, f32[512]{0:T(512)S(1)}, f32[512]{0:T(512)S(1)}, f32[512]{0:T(512)S(1)}, /*index=5*/...) fusion(f32[512,512]{1,0:T(8,128)} %fusion.36, f32[6,512]{1,0:T(8,128)S(1)} %fusion.38, ...), kind=kOutput, calls=%fused_computation.78 | convolution fusion | flops 2152985088 | bytes 12609536 | tf_op jit(solution)/shard_map/dot_general | solution.py:80
  206.2 1.3 collective-permute-start.1
  207.6 1.7 collective-permute-done.1
  209.3 0.0 copy-done.3
  209.3 2.1 multiply_bitcast_fusion.1
  211.4 1.5 collective-permute-start.2
  212.9 0.0 slice-start
  212.9 1.3 multiply_bitcast_fusion
  214.3 2.9 collective-permute-done.2
  217.1 0.3 pad_maximum_fusion
  217.4 0.0 copy-done
  217.4 0.0 slice-start.2
  217.5 2.1 pad_maximum_fusion.1
  219.6 1.1 copy-done.2
  220.7 0.0 slice-done
  220.7 0.0 slice-done.2
  220.7 8.2 %bitcast_convert_fusion = bf16[512,4096]{1,0:T(8,128)(2,1)} fusion(bf16[512,3,512]{2,0,1:T(8,128)(2,1)S(1)} %get-tuple-element.27, bf16[4096,3,512]{2,0,1:T(8,128)(2,1)S(1)} %bitcast.87), kind=kOutput, calls=%fused_computation.1 | convolution fusion | flops 6444548096 | bytes 18350080 | tf_op jit(solution)/shard_map/dot_general | solution.py:120
  229.0 0.0 reduce-scatter.7.cloned.1.call-update
  229.0 0.0 reduce-scatter.5.cloned.1.call-start
  229.0 6.7 %convolution_convert_fusion = bf16[512,4096]{1,0:T(8,128)(2,1)} fusion(bf16[512,512]{1,0:T(8,128)(2,1)} %get-tuple-element.25, bf16[512,4096]{1,0:T(8,128)(2,1)} %param.13), kind=kOutput, calls=%fused_computation.3 | convolution fusion | flops 2149580800 | bytes 8912896 | tf_op jit(solution)/shard_map/dot_general | solution.py:73
  235.7 0.0 reduce-scatter.5.cloned.1.call-update
  235.7 0.0 reduce-scatter.11.cloned.1.call-start
  235.8 6.8 %multiply_convert_fusion.1 = bf16[512,4096]{1,0:T(8,128)(2,1)} fusion(bf16[512,512]{1,0:T(8,128)(2,1)} %get-tuple-element.25, bf16[512,4096]{1,0:T(8,128)(2,1)} %all-gather.5.cloned.1.call-done), kind=kOutput, calls=%fused_computation.2 | convolution fusion | flops 2151677952 | bytes 8912896 | tf_op jit(solution)/shard_map/dot_general | solution.py:84
  242.6 0.0 reduce-scatter.11.cloned.1.call-update
  242.6 0.3 reduce-scatter.9.cloned.1.call-start
  242.9 2.7 copy.20
  245.6 11.5 %multiply_convert_fusion = bf16[4096,1536]{0,1:T(8,128)(2,1)} fusion(bf16[512,1536]{0,1:T(8,128)(2,1)} %bitcast.94, bf16[512,4096]{1,0:T(8,128)(2,1)} %all-gather.3.cloned.1.call-done), kind=kOutput, calls=%fused_computation | convolution fusion | flops 6455033856 | bytes 18350080 | tf_op jit(solution)/shard_map/dot_general | solution.py:129
  257.1 16.7 %copy.21 = bf16[4096,3,512]{2,0,1:T(8,128)(2,1)} copy(bf16[4096,3,512]{0,2,1:T(8,128)(2,1)} %bitcast.89) | data formatting | bytes 25165824 | tf_op jit(solution)/shard_map/convert_element_type | solution.py:134
  273.8 0.0 reduce-scatter.9.cloned.1.call-update
  273.9 2.4 copy.22
  276.3 2.4 copy.23
  278.7 0.0 copy-start.4
  278.7 1.8 multiply_reduce_fusion.2
  280.5 71.5 %all-reduce = (bf16[3,3,512]{2,1,0:T(4,128)(2,1)S(1)}, bf16[7,512]{1,0:T(8,128)(2,1)S(1)}) all-reduce(bf16[3,3,512]{2,1,0:T(4,128)(2,1)S(1)} %fusion.37, bf16[7,512]{1,0:T(8,128)(2,1)S(1)} %multiply_convert_fusion.3), channel_id=1, replica_groups=mesh['ctx'=16,'tp'=8] {'ctx'}, use_global_device_ids=true, to_apply=%region_9.0 | all-reduce | flops 8192 | bytes 32768 | tf_op jit(solution)/shard_map/psum | solution.py:111
  352.0 0.6 convert_element_type.100
  352.6 0.6 convert_element_type.102
  353.3 0.0 copy-done.4
  353.3 1.5 fusion.12
  354.8 65.7 %reduce-scatter.5.cloned.1.call-done = bf16[64,4096]{1,0:T(8,128)(2,1)} async-done(((bf16[512,4096]{1,0:T(8,128)(2,1)}), bf16[64,4096]{1,0:T(8,128)(2,1)}) %reduce-scatter.5.cloned.1.call-update) | async-done | bytes 524304 | tf_op jit(solution)/shard_map/reduce_scatter | solution.py:72
  420.5 2.9 fusion.7
  423.4 81.8 %reduce-scatter.11.cloned.1.call-done = bf16[512,256]{1,0:T(8,128)(2,1)} async-done(((bf16[512,4096]{1,0:T(8,128)(2,1)}), bf16[512,256]{1,0:T(8,128)(2,1)}) %reduce-scatter.11.cloned.1.call-update) | async-done | bytes 262160 | tf_op jit(solution)/shard_map/reduce_scatter | solution.py:89
  505.2 126.4 %reduce-scatter.9.cloned.1.call-done = bf16[256,3,512]{2,0,1:T(8,128)(2,1)} async-done(((bf16[4096,3,512]{2,0,1:T(8,128)(2,1)}), bf16[256,3,512]{2,0,1:T(8,128)(2,1)}) %reduce-scatter.9.cloned.1.call-update) | async-done | bytes 786448 | tf_op jit(solution)/shard_map/reduce_scatter | solution.py:133
  (23 shorter events, 0.2 us)
Async XLA Ops:
  7.2 96.9 %all-gather.3.cloned.1.call-start = ((), (), s32[]{:S(2)}) async-start(), calls=%async_computation.4 | async-start | bytes 4718592 | tf_op jit(solution)/shard_map/all_gather | solution.py:55
  10.5 186.2 %all-gather.5.cloned.1.call-start = ((), (), s32[]{:S(2)}) async-start(), calls=%async_computation.6 | async-start | bytes 4718592 | tf_op jit(solution)/shard_map/all_gather | solution.py:79
  11.3 17.0 %copy-start.5 = (f32[3,3,512]{2,1,0:T(4,128)S(1)}, f32[3,3,512]{2,1,0:T(4,128)}, u32[]{:S(2)}) copy-start(f32[3,3,512]{2,1,0:T(4,128)} %param.11) | copy-start | bytes 55300
  11.3 342.0 %reduce-scatter.7.cloned.1.call-start = ((), (), s32[]{:S(2)}) async-start(), calls=%async_computation.7 | async-start | bytes 4718592 | tf_op jit(solution)/shard_map/reduce_scatter | solution.py:119
  104.1 12.5 %copy-start.6 = (f32[7,512]{1,0:T(8,128)S(1)}, f32[7,512]{1,0:T(8,128)}, u32[]{:S(2)}) copy-start(f32[7,512]{1,0:T(8,128)} %param.12) | copy-start | bytes 43012
  115.0 3.9 copy-start.1
  115.1 3.9 collective-permute-start
  196.8 12.5 %copy-start.3 = (f32[512,512]{1,0:T(8,128)S(1)}, f32[512,512]{1,0:T(8,128)}, u32[]{:S(2)}) copy-start(f32[512,512]{1,0:T(8,128)} %fusion.36) | copy-start | bytes 3145732
  206.2 3.1 collective-permute-start.1
  211.4 5.7 collective-permute-start.2
  212.9 7.8 %slice-start = ((s8[12582912]{0:T(1024)(128)(4,1)}), s8[4194304]{0:T(1024)(128)(4,1)S(1)}, s32[]{:S(2)}) async-start(s8[12582912]{0:T(1024)(128)(4,1)} %bitcast.86), calls=%async_computation.10 | async-start | bytes 8388608
  214.3 3.2 copy-start
  217.1 3.6 slice-start.1
  217.4 3.3 slice-start.2
  219.6 1.2 copy-start.2
  229.0 191.5 %reduce-scatter.5.cloned.1.call-start = ((), (), s32[]{:S(2)}) async-start(), calls=%async_computation.5 | async-start | bytes 4718592 | tf_op jit(solution)/shard_map/reduce_scatter | solution.py:72
  235.7 269.5 %reduce-scatter.11.cloned.1.call-start = ((), (), s32[]{:S(2)}) async-start(), calls=%async_computation.9 | async-start | bytes 4456448 | tf_op jit(solution)/shard_map/reduce_scatter | solution.py:89
  242.6 389.0 %reduce-scatter.9.cloned.1.call-start = ((), (), s32[]{:S(2)}) async-start(), calls=%async_computation.8 | async-start | bytes 13369344 | tf_op jit(solution)/shard_map/reduce_scatter | solution.py:133
  278.7 74.6 %copy-start.4 = (f32[4096]{0:T(1024)S(1)}, f32[4096]{0:T(1024)}, u32[]{:S(2)}) copy-start(f32[4096]{0:T(1024)} %param.9) | copy-start | bytes 49156
Sparse Core Ops, SparseCore 0:
  10.7 93.3 all-gather.2
  105.7 91.0 all-gather.4
  229.1 97.6 reduce-scatter.6
  329.1 91.3 reduce-scatter.4
  424.9 80.2 reduce-scatter.10
  510.6 121.0 reduce-scatter.8
where the time goes:
time: 640 us; the launch traced here: 638 us
  waiting for transfers between devices  428 us (67%)
  blocking collectives  71.5 us (11%)
  matrix products  53.6 us (8%)
  local copies, waits for them, and re-layouts  44.7 us (7%)
  other arithmetic  21.1 us (3%)
  between operations  14.4 us (2%)
    reduce_scatter x1, waiting for transfers between devices, local(): lax.psum_scatter(scaled_in.astype(jnp.bfloat16), 'ctx', scatter_dimension...  126 us
    reduce_scatter x1, waiting for transfers between devices, local(): lax.psum_scatter(out_partial.astype(jnp.bfloat16), 'ctx', scatter_dimensi...  81.8 us
    all_gather x1, waiting for transfers between devices, local(): gathered = lax.all_gather(normal_rows, 'tp', axis=0, tiled=True)  75.8 us
    all_gather x1, waiting for transfers between devices, local(): grad_all = lax.all_gather(cotangent, 'tp', axis=0, tiled=True)  73.3 us
    psum x1, blocking collectives, local(): lax.psum(filter_part.astype(jnp.bfloat16), 'ctx').astype(jnp.float32)  71.5 us
    reduce_scatter x1, waiting for transfers between devices, local(): lax.psum_scatter(jnp.dot(rows_part, out_weight, preferred_element_type=jn...  65.7 us
    unnamed x21, local copies, waits for them, and re-layouts  18.1 us
    convert_element_type x1, local copies, waits for them, and re-layouts, local(): scaled_in.astype(jnp.bfloat16)  16.7 us
  transfers between devices with their start and end apart: 9, of which 7 were waited for; matrix products, arithmetic and copies ran while one was open for 15% of the time, Pallas kernels for 0%

commit v1 on v0

--- a/solution.py
+++ b/solution.py
@@ -1,7 +1,12 @@
 import jax
 import jax.numpy as jnp
 from jax import lax
+from jax.experimental import pallas as pl
+from jax.experimental.pallas import tpu as pltpu
 from jax.sharding import PartitionSpec as P
+
+MESH = pl.DeviceIdType.MESH
+DELTAS = (2, 1, 3, 0)
 
 
 def passed_along(value, axis, steps):
@@ -39,6 +44,412 @@
         begin = count - 1 - tap_index
         pieces.append(jnp.sum(grads * extended[begin : begin + number], axis=0))
     return jnp.stack(pieces)
+
+
+class Place:
+    def __init__(self):
+        ctx, tp = lax.axis_index("ctx"), lax.axis_index("tp")
+        self.y, self.x_hi, self.core = ctx // 4, (ctx // 2) % 2, ctx % 2
+        self.z, self.x_lo = tp // 2, tp % 2
+        self.ctx, self.tp = ctx, tp
+
+    def sibling(self):
+        return (self.y * 4 + self.x_hi * 2 + 1 - self.core, self.tp)
+
+    def along_y(self, step):
+        return (((self.y + step) % 4) * 4 + self.x_hi * 2 + self.core, self.tp)
+
+    def along_z(self, step):
+        return (self.ctx, ((self.z + step) % 4) * 2 + self.x_lo)
+
+    def along_x(self, step):
+        x = (self.x_hi * 2 + self.x_lo + step) % 4
+        return (self.y * 4 + (x // 2) * 2 + self.core, self.z * 2 + x % 2)
+
+    def partner(self):
+        return (self.ctx, self.z * 2 + 1 - self.x_lo)
+
+    def block(self, step, same):
+        x_lo = self.x_lo if same else 1 - self.x_lo
+        return ((self.z + step) % 4) * 2 + x_lo
+
+
+def remote(source, target, send, recv, device):
+    return pltpu.make_async_remote_copy(
+        src_ref=source, dst_ref=target, send_sem=send, recv_sem=recv, device_id=device, device_id_type=MESH
+    )
+
+
+def greet(devices):
+    barrier = pltpu.get_barrier_semaphore()
+    for device in devices:
+        pl.semaphore_signal(barrier, inc=1, device_id=device, device_id_type=MESH)
+    pl.semaphore_wait(barrier, len(devices))
+
+
+def tile(index, size):
+    return pl.ds(pl.multiple_of(index * size, size), size)
+
+
+def reduce_kernel(
+    scale,
+    acts_hbm, turned_hbm, in_w_hbm, out_w_hbm, norm_hbm, cot_hbm,
+    branch_ref, gnorm_ref, shard_ref,
+    acts, turned, in_w, out_w, norms, cots,
+    sib_out, sums, y_in, x_pass, x_in, parts, tp_in,
+    load_sem, in_w_sem, col_sem, sib_send, sib_recv, y_send, y_recv, x_send, x_recv, tp_send, tp_recv,
+):
+    here = Place()
+    tokens, width = norm_hbm.shape
+    chans = out_w_hbm.shape[0]
+    cut = width // 16
+    rows_all = turned_hbm.shape[0]
+    half = rows_all // 2
+    block = tokens // 8
+    upper, lower = pl.ds(0, half), pl.ds(half, half)
+    step_in = in_w.shape[2]
+    steps_in = width // step_in
+
+    def target(index, core):
+        y = (here.y + DELTAS[index % 4]) % 4
+        x_hi = 1 - here.x_hi if index < 4 else here.x_hi
+        return y * 4 + x_hi * 2 + core
+
+    order = []
+    for index in range(8):
+        order.append(target(index, 1 - here.core))
+        order.append(target(index, here.core))
+
+    def loads(position):
+        cols = tile(order[position], cut)
+        return (
+            pltpu.make_async_copy(norm_hbm.at[:, cols], norms.at[:, cols], col_sem.at[0, position]),
+            pltpu.make_async_copy(cot_hbm.at[:, cols], cots.at[:, cols], col_sem.at[1, position]),
+        )
+
+    def in_load(step, slot):
+        return pltpu.make_async_copy(in_w_hbm.at[:, tile(step, step_in), :], in_w.at[slot], in_w_sem.at[slot])
+
+    turned_load = pltpu.make_async_copy(turned_hbm, turned, load_sem.at[0])
+    acts_load = pltpu.make_async_copy(acts_hbm, acts, load_sem.at[1])
+    out_load = pltpu.make_async_copy(out_w_hbm, out_w, load_sem.at[2])
+    turned_load.start()
+    for copy in loads(0) + loads(1) + loads(2):
+        copy.start()
+    acts_load.start()
+    out_load.start()
+    for position in range(3, 16):
+        for copy in loads(position):
+            copy.start()
+    in_load(0, 0).start()
+    in_load(1, 1).start()
+
+    greet(
+        [here.sibling(), here.along_y(1), here.along_y(-1), here.along_z(1), here.along_z(-1),
+         here.along_x(1), here.along_x(-1)]
+    )
+    sends = []
+
+    def go(copy):
+        copy.start()
+        sends.append(copy)
+
+    def product(position, write):
+        for copy in loads(position):
+            copy.wait()
+        cols = tile(order[position], cut)
+
+        def one(index, source):
+            rows = tile(index, chans)
+            value = jnp.dot(turned[rows, :], source[:, cols], preferred_element_type=jnp.float32)
+            write(rows, value * scale)
+
+        def loop(index, carry):
+            one(index, norms)
+            return carry
+
+        lax.fori_loop(0, rows_all // chans - 1, loop, 0)
+        one(rows_all // chans - 1, cots)
+
+    def sib_copy(index):
+        slot = index % 4
+        return remote(sib_out.at[slot], sums.at[index], sib_send.at[index], sib_recv.at[index], here.sibling())
+
+    def for_sibling(index):
+        if index >= 4:
+            sib_copy(index - 4).wait_send()
+
+        def write(rows, value):
+            sib_out[index % 4, rows, :] = value.astype(jnp.bfloat16)
+
+        product(2 * index, write)
+        sib_copy(index).start()
+
+    def for_self(index):
+        sib_copy(index).wait_recv()
+
+        def write(rows, value):
+            held = sums[index, rows, :].astype(jnp.float32)
+            sums[index, rows, :] = (held + value).astype(jnp.bfloat16)
+
+        product(2 * index + 1, write)
+
+    def y_copy(group, slot):
+        index, rows, step = (
+            (0, upper, 1), (0, lower, -1), (1, lower, 1), (2, upper, -1), (1, upper, 1), (2, lower, -1)
+        )[slot]
+        return remote(
+            sums.at[group * 4 + index, rows], y_in.at[group, slot],
+            y_send.at[group, slot], y_recv.at[group, slot], here.along_y(step),
+        )
+
+    def add_rows(ref, base, length, others, size=128):
+        def loop(index, carry):
+            at = tile(index, size)
+            rows = pl.ds(pl.multiple_of(base + index * size, size), size)
+            total = ref[rows, :].astype(jnp.float32)
+            for other in others:
+                total = total + other[at, :].astype(jnp.float32)
+            ref[rows, :] = total.astype(jnp.bfloat16)
+            return carry
+
+        lax.fori_loop(0, length // size, loop, 0)
+
+    def y_pass(group):
+        y_copy(group, 0).wait_recv()
+        add_rows(sums.at[group * 4 + 1], 0, half, [y_in.at[group, 0]])
+        go(y_copy(group, 4))
+        y_copy(group, 1).wait_recv()
+        add_rows(sums.at[group * 4 + 2], half, half, [y_in.at[group, 1]])
+        go(y_copy(group, 5))
+
+    def y_done(group):
+        for slot in (3, 4, 2, 5):
+            y_copy(group, slot).wait_recv()
+
+    def x_copy(side):
+        rows, step = ((upper, 1), (lower, -1))[side]
+        return remote(sums.at[3, rows], x_pass.at[side], x_send.at[side], x_recv.at[side], here.along_x(step))
+
+    def x_forward(side):
+        return remote(
+            x_pass.at[side], x_in.at[side], x_send.at[2 + side], x_recv.at[2 + side], here.along_x((1, -1)[side])
+        )
+
+    quarter = block // 2
+
+    def tp_copy(which, slot):
+        part, held = parts.at[which], tp_in.at[which]
+        source, place, device = (
+            lambda: (part.at[tile(here.block(2, False), block)], held.at[0], here.partner()),
+            lambda: (part.at[tile(here.block(1, False), block)], held.at[1], here.along_z(1)),
+            lambda: (part.at[tile(here.block(-1, False), block)], held.at[2], here.along_z(-1)),
+            lambda: (
+                part.at[pl.ds(pl.multiple_of(here.block(2, True) * block, block), quarter)],
+                held.at[3, pl.ds(0, quarter)], here.along_z(1)),
+            lambda: (
+                part.at[pl.ds(pl.multiple_of(here.block(2, True) * block + quarter, quarter), quarter)],
+                held.at[3, pl.ds(quarter, quarter)], here.along_z(-1)),
+            lambda: (part.at[tile(here.block(1, True), block)], held.at[4], here.along_z(1)),
+            lambda: (part.at[tile(here.block(-1, True), block)], held.at[5], here.along_z(-1)),
+            lambda: (part.at[tile(here.block(0, False), block)], held.at[6], here.partner()),
+        )[slot]()
+        return remote(source, place, tp_send.at[which, slot], tp_recv.at[which, slot], device)
+
+    def tp_begin(which):
+        for slot in range(3):
+            go(tp_copy(which, slot))
+
+    def tp_halves(which):
+        tp_copy(which, 0).wait_recv()
+        add_rows(parts.at[which], here.block(2, True) * block, block, [tp_in.at[which, 0]], 16)
+        go(tp_copy(which, 3))
+        go(tp_copy(which, 4))
+
+    def tp_direct(which):
+        tp_copy(which, 3).wait_recv()
+        add_rows(parts.at[which], here.block(1, True) * block, quarter, [tp_in.at[which, 3, pl.ds(0, quarter)]], 16)
+        go(tp_copy(which, 5))
+        tp_copy(which, 4).wait_recv()
+        add_rows(
+            parts.at[which], here.block(-1, True) * block + quarter, quarter,
+            [tp_in.at[which, 3, pl.ds(quarter, quarter)]], 16)
+        go(tp_copy(which, 6))
+
+    def tp_last(which):
+        tp_copy(which, 1).wait_recv()
+        tp_copy(which, 2).wait_recv()
+        add_rows(parts.at[which], here.block(0, False) * block, block, [tp_in.at[which, 1], tp_in.at[which, 2]], 16)
+        go(tp_copy(which, 7))
+
+    def tp_finish(which, result):
+        for slot in (5, 6, 7):
+            tp_copy(which, slot).wait_recv()
+
+        def loop(index, carry):
+            at = tile(index, 16)
+            rows = pl.ds(pl.multiple_of(here.tp * block + index * 16, 16), 16)
+            total = parts[which, rows, :].astype(jnp.float32)
+            for slot in (4, 5, 6):
+                total = total + tp_in[which, slot, at, :].astype(jnp.float32)
+            result[at, :] = total
+            return carry
+
+        lax.fori_loop(0, block // 16, loop, 0)
+
+    def branch_product():
+        def loop(index, carry):
+            cols = tile(index, chans)
+            value = jnp.dot(
+                acts[:, pl.ds(3 * chans, chans)], out_w[:, cols], preferred_element_type=jnp.float32
+            )
+            parts[0, :, cols] = value.astype(jnp.bfloat16)
+            return carry
+
+        lax.fori_loop(0, width // chans, loop, 0)
+
+    def gnorm_product():
+        def loop(step, carry):
+            slot = step % 2
+            in_load(step, slot).wait()
+
+            def inner(index, carry):
+                rows = tile(index, tokens // 2)
+                value = jnp.zeros((tokens // 2, step_in), jnp.float32)
+                for kind in range(3):
+                    value = value + lax.dot_general(
+                        acts[rows, pl.ds(kind * chans, chans)], in_w[slot, kind],
+                        (((1,), (1,)), ((), ())), preferred_element_type=jnp.float32,
+                    )
+                parts[1, rows, tile(step, step_in)] = value.astype(jnp.bfloat16)
+                return carry
+
+            lax.fori_loop(0, 2, inner, 0)
+
+            @pl.when(step + 2 < steps_in)
+            def _():
+                in_load(step + 2, slot).start()
+
+            return carry
+
+        lax.fori_loop(0, steps_in, loop, 0)
+
+    turned_load.wait()
+    for_sibling(0)
+    for_sibling(1)
+    for_self(0)
+    go(y_copy(0, 0))
+    go(y_copy(0, 1))
+    acts_load.wait()
+    out_load.wait()
+    branch_product()
+    tp_begin(0)
+    for_sibling(2)
+    for_self(1)
+    go(y_copy(0, 2))
+    for_sibling(3)
+    for_self(2)
+    go(y_copy(0, 3))
+    for_sibling(4)
+    for_self(3)
+    tp_halves(0)
+    gnorm_product()
+    tp_begin(1)
+    y_pass(0)
+    for_sibling(5)
+    for_self(4)
+    go(y_copy(1, 0))
+    go(y_copy(1, 1))
+    for_sibling(6)
+    for_self(5)
+    go(y_copy(1, 2))
+    for_sibling(7)
+    for_self(6)
+    go(y_copy(1, 3))
+    for_self(7)
+    tp_direct(0)
+    tp_last(0)
+    y_done(0)
+    add_rows(sums.at[3], 0, half, [y_in.at[0, 3], y_in.at[0, 4]])
+    go(x_copy(0))
+    add_rows(sums.at[3], half, half, [y_in.at[0, 2], y_in.at[0, 5]])
+    go(x_copy(1))
+    tp_halves(1)
+    y_pass(1)
+    tp_direct(1)
+    tp_last(1)
+    for side in range(2):
+        x_copy(side).wait_recv()
+        go(x_forward(side))
+    tp_finish(0, branch_ref)
+    tp_finish(1, gnorm_ref)
+    x_forward(0).wait_recv()
+    x_forward(1).wait_recv()
+    y_done(1)
+
+    def last(begin, others):
+        def loop(index, carry):
+            at = tile(index, 128)
+            rows = pl.ds(pl.multiple_of(begin + index * 128, 128), 128)
+            total = sums[7, rows, :].astype(jnp.float32)
+            for other in others:
+                total = total + other[at, :].astype(jnp.float32)
+            shard_ref[rows, :] = total.astype(jnp.bfloat16)
+            return carry
+
+        lax.fori_loop(0, half // 128, loop, 0)
+
+    last(0, [y_in.at[1, 3], y_in.at[1, 4], x_in.at[0]])
+    last(half, [y_in.at[1, 2], y_in.at[1, 5], x_in.at[1]])
+    for index in range(4, 8):
+        sib_copy(index).wait_send()
+    for copy in sends:
+        copy.wait_send()
+
+
+def reduced(acts, turned, in_weight, out_weight, norms, cots, scale):
+    tokens, width = norms.shape
+    chans = out_weight.shape[0]
+    rows_all = turned.shape[0]
+    cut = width // 16
+    block = tokens // 8
+    half = rows_all // 2
+    any_space = pl.BlockSpec(memory_space=pl.ANY)
+    vmem_space = pl.BlockSpec(memory_space=pltpu.VMEM)
+    bf16 = jnp.bfloat16
+    dma = pltpu.SemaphoreType.DMA
+    body = lambda *refs: reduce_kernel(scale, *refs)
+    return pl.pallas_call(
+        body,
+        out_shape=(
+            jax.ShapeDtypeStruct((block, width), jnp.float32),
+            jax.ShapeDtypeStruct((block, width), jnp.float32),
+            jax.ShapeDtypeStruct((rows_all, cut), bf16),
+        ),
+        in_specs=[any_space] * 6,
+        out_specs=(vmem_space, vmem_space, vmem_space),
+        scratch_shapes=[
+            pltpu.VMEM(acts.shape, bf16),
+            pltpu.VMEM(turned.shape, bf16),
+            pltpu.VMEM((2, 3, 512, chans), bf16),
+            pltpu.VMEM(out_weight.shape, bf16),
+            pltpu.VMEM(norms.shape, bf16),
+            pltpu.VMEM(cots.shape, bf16),
+            pltpu.VMEM((4, rows_all, cut), bf16),
+            pltpu.VMEM((8, rows_all, cut), bf16),
+            pltpu.VMEM((2, 6, half, cut), bf16),
+            pltpu.VMEM((2, half, cut), bf16),
+            pltpu.VMEM((2, half, cut), bf16),
+            pltpu.VMEM((2, tokens, width), bf16),
+            pltpu.VMEM((2, 7, block, width), bf16),
+            dma((3,)), dma((2,)), dma((2, 16)),
+            dma((8,)), dma((8,)), dma((2, 6)), dma((2, 6)), dma((4,)), dma((4,)), dma((2, 8)), dma((2, 8)),
+        ],
+        compiler_params=pltpu.CompilerParams(
+            collective_id=0, has_side_effects=True, vmem_limit_bytes=63 * 2**20
+        ),
+        name="reduce_all",
+    )(acts, turned, in_weight, out_weight, norms, cots)
 
 
 def local(hidden_in, cotangent, norm_gain, in_weight, filter_taps, inner_taps, out_weight):
@@ -68,26 +479,9 @@
     wide_prods = jnp.concatenate([before, key_vals * value_vals])
     gate_vals = taps_causal(wide_prods, inner_taps, block_rows)
     mixed = (query_vals * gate_vals).astype(jnp.bfloat16)
-    rows_part = mixed
-    branch = lax.psum_scatter(
-        jnp.dot(rows_part, out_weight, preferred_element_type=jnp.float32).astype(jnp.bfloat16),
-        "tp",
-        scatter_dimension=0,
-        tiled=True,
-    ).astype(jnp.float32)
-    layer_out = (hidden_in.astype(jnp.float32) + branch).astype(jnp.bfloat16)
     grad_all = lax.all_gather(cotangent, "tp", axis=0, tiled=True)
     grad_mixed = lax.dot_general(
         grad_all, out_weight, (((1,), (1,)), ((), ())), preferred_element_type=jnp.float32
-    )
-    out_partial = (
-        lax.dot_general(
-            mixed, grad_all, (((0,), (0,)), ((), ())), preferred_element_type=jnp.float32
-        )
-        * loss_scale
-    )
-    grad_out_weight = lax.psum_scatter(
-        out_partial.astype(jnp.bfloat16), "ctx", scatter_dimension=1, tiled=True
     )
     grad_query = grad_mixed * gate_vals
     grad_gates = grad_mixed * query_vals
@@ -114,25 +508,16 @@
     grad_proj = taps_ahead(
         jnp.concatenate([grad_features, next_feat]), filter_taps, block_rows
     ).astype(jnp.bfloat16)
-    flat_grad = grad_proj.reshape(block_rows, 3 * channels)
-    rows_part = flat_grad
-    grad_normed = lax.psum_scatter(
-        lax.dot_general(
-            rows_part, flat_in, (((1,), (1,)), ((), ())), preferred_element_type=jnp.float32
-        ).astype(jnp.bfloat16),
-        "tp",
-        scatter_dimension=0,
-        tiled=True,
-    ).astype(jnp.float32)
+    acts = jnp.concatenate([grad_proj.reshape(block_rows, 3 * channels), mixed], axis=1)
+    branch, grad_normed, shard = reduced(
+        acts, acts.T, jnp.transpose(in_weight, (1, 0, 2)), out_weight, gathered, grad_all, loss_scale
+    )
+    layer_out = (hidden_in.astype(jnp.float32) + branch).astype(jnp.bfloat16)
     _, pullback = jax.vjp(lambda values: normed(values, norm_gain), hidden_in.astype(jnp.float32))
     grad_input = (cotangent.astype(jnp.float32) + pullback(grad_normed)[0]).astype(jnp.bfloat16)
-    in_partial = lax.dot_general(
-        gathered, flat_grad, (((0,), (0,)), ((), ())), preferred_element_type=jnp.float32
-    )
-    scaled_in = (in_partial * loss_scale).reshape(model_width, 3, channels)
-    grad_in_weight = lax.psum_scatter(
-        scaled_in.astype(jnp.bfloat16), "ctx", scatter_dimension=0, tiled=True
-    )
+    cut = shard.shape[1]
+    grad_in_weight = jnp.transpose(shard[: 3 * channels].reshape(3, channels, cut), (2, 0, 1))
+    grad_out_weight = shard[3 * channels :]
     return (layer_out, grad_input, grad_in_weight, grad_out_weight, grad_filter, grad_inner)
 
 

time: 640 us -> 442 us (0.69)
  waiting for transfers between devices: 428 us -> 151 us
  Pallas kernels: 0 us -> 100 us
  matrix products: 53.6 us -> 19.6 us
  other arithmetic: 21.1 us -> 45 us
  local copies, waits for them, and re-layouts: 44.7 us -> 36.9 us
    reduce_scatter x4 -> x0, waiting for transfers between devices: 274 us -> none  [the longest x1 126 us: local(): lax.psum_scatter(scaled_in.astype(jnp.bfloat16), 'ctx', scatter_dimension...]
    pallas_call x0 -> x1, Pallas kernels: none -> 100 us  [reduced(): pl.pallas_call(body, out_shape=(jax.ShapeDtypeStruct((block, width), jnp....]
    dot_general x4 -> x0, matrix products: 33.2 us -> none  [the longest x1 11.5 us: local(): lax.dot_general(gathered, flat_grad, (((0,), (0,)), ((), ())), preferred_...]
    convert_element_type x2 -> x0, local copies, waits for them, and re-layouts: 19.4 us -> none  [the longest x1 16.7 us: local(): scaled_in.astype(jnp.bfloat16)]
    another operation x3, other arithmetic: 5.5 us -> 23.2 us  [local(): jnp.stack([grad_query, grad_products * value_vals, grad_products * key_va...]
    unnamed x21 -> x63, local copies, waits for them, and re-layouts: 18.1 us -> 19.4 us
  transfers between devices with their start and end apart: 9 -> 5, of which waited for: 7 -> 3; matrix products, arithmetic and copies ran while one was open for 15% -> 11% of each run, Pallas kernels for 0% -> 0%
where the time goes in v1:
time: 442 us; the launch traced here: 441 us
  waiting for transfers between devices  151 us (34%)
  Pallas kernels  100 us (23%)
  blocking collectives  69 us (16%)
  other arithmetic  45 us (10%)
  local copies, waits for them, and re-layouts  36.9 us (8%)
  matrix products  19.6 us (4%)
  between operations  14.5 us (3%)
    pallas_call x1, Pallas kernels, reduced(): pl.pallas_call(body, out_shape=(jax.ShapeDtypeStruct((block, width), jnp....  100 us
    all_gather x1, waiting for transfers between devices, local(): gathered = lax.all_gather(normal_rows, 'tp', axis=0, tiled=True)  75.2 us
    all_gather x1, waiting for transfers between devices, local(): grad_all = lax.all_gather(cotangent, 'tp', axis=0, tiled=True)  75.2 us
    psum x1, blocking collectives, local(): lax.psum(filter_part.astype(jnp.bfloat16), 'ctx').astype(jnp.float32)  69 us
    another operation x3, other arithmetic, local(): jnp.stack([grad_query, grad_products * value_vals, grad_products * key_va...  23.2 us
    unnamed x63, local copies, waits for them, and re-layouts  19.4 us
    dot_general x1, matrix products, local(): jnp.dot(gathered, flat_in, preferred_element_type=jnp.float32)  11 us
  transfers between devices with their start and end apart: 5, of which 3 were waited for; matrix products, arithmetic and copies ran while one was open for 11% of the time, Pallas kernels for 0%

profile of v1, /device:TPU:0, one launch (start us, length us, event | category | flops | bytes accessed | tf_op | source)
XLA Modules:
  0.0 440.8 jit_solution(2698435249039343098)
XLA Ops:
  7.2 0.0 all-gather.5.cloned.1.call-start
  7.2 1.2 fusion.29
  8.5 0.5 copy-done.29
  9.0 0.6 copy-done.27
  9.5 2.0 fusion.31
  11.6 0.0 all-gather.5.cloned.1.call-update
  11.6 0.0 all-gather.3.cloned.1.call-start
  11.6 0.7 all-gather.3.cloned.1.call-update
  12.3 0.0 copy-start.16
  12.3 17.0 %copy.28 = bf16[4096,3,512]{0,2,1:T(8,128)(2,1)} copy(bf16[4096,3,512]{2,0,1:T(8,128)(2,1)} %param.10) | data formatting | bytes 25165824 | tf_op args[3]
  29.3 0.6 slice_bitcast_fusion.8
  29.9 75.2 %all-gather.5.cloned.1.call-done.refs_4_ = bf16[512,4096]{1,0:T(8,128)(2,1)} async-done(((bf16[64,4096]{1,0:T(8,128)(2,1)}), bf16[512,4096]{1,0:T(8,128)(2,1)}) %all-gather.5.cloned.1.call-update) | async-done | bytes 4194320 | tf_op jit(solution)/shard_map/all_gather | solution.py:466
  105.1 11.0 %convolution_convert_fusion = bf16[512,1536]{1,0:T(8,128)(2,1)S(1)} fusion(bf16[512,4096]{1,0:T(8,128)(2,1)} %all-gather.5.cloned.1.call-done.refs_4_, bf16[4096,1536]{0,1:T(8,128)(2,1)} %bitcast.84), kind=kOutput, calls=%fused_computation.21 | convolution fusion | flops 6443237376 | bytes 18350080 | tf_op jit(solution)/shard_map/dot_general | solution.py:467
  116.1 1.1 copy.29
  117.2 1.5 collective-permute-start
  118.8 0.6 fusion.55
  119.4 0.7 copy.30
  120.1 0.2 collective-permute-done
  120.3 3.7 multiply_add_fusion
  124.0 0.8 fusion.47
  124.8 1.1 copy-done
  125.9 0.6 fusion.35
  126.6 75.2 %all-gather.3.cloned.1.call-done.refs_5_ = bf16[512,4096]{1,0:T(8,128)(2,1)} async-done(((bf16[64,4096]{1,0:T(8,128)(2,1)}), bf16[512,4096]{1,0:T(8,128)(2,1)}) %all-gather.3.cloned.1.call-update) | async-done | bytes 4194320 | tf_op jit(solution)/shard_map/all_gather | solution.py:482
  201.8 8.6 %multiply_reduce_fusion.3 = (f32[512]{0:T(512)}, f32[512]{0:T(512)}, f32[512]{0:T(512)}, f32[512]{0:T(512)}, f32[512]{0:T(512)}, /*index=5*/f32[512]{0:T(512)}, ...) fusion(f32[512,512]{0,1:T(8,128)S(1)} %fusion.35, f32[6,512]{0,1:T(8,128)S(1)} %copy-done.12, ...), kind=kOutput, calls=%fused_computation.82 | convolution fusion | flops 2152985088 | bytes 12609536 | tf_op jit(solution)/shard_map/dot_general | solution.py:483
  210.5 1.5 collective-permute-start.1
  212.1 2.0 fusion.40
  214.0 1.1 fusion.38
  215.1 0.8 stack.82
  215.9 0.6 multiply_convert_fusion.1
  216.5 0.7 copy.34
  217.2 0.7 copy.35
  217.9 0.9 slice.288
  218.8 0.0 collective-permute-done.1
  218.8 13.9 %multiply_bitcast_fusion.1 = (f32[512,1,512]{0,2,1:T(8,128)}, f32[512,512]{0,1:T(8,128)}, f32[512,512]{0,1:T(8,128)S(1)}, f32[512,512]{0,1:T(8,128)}) fusion(f32[518,3,512]{0,2,1:T(8,128)} %copy-done, f32[6,512]{0,1:T(8,128)S(1)} %collective-permute-done.1, f32[512,512]{0,1:T(8,128)} %copy-done.3, f32[512]{0:T(512)} %bitcast.102, f32[512]{0:T(512)} %bitcast.104, ...), kind=kLoop, calls=%fused_computation.91 | loop fusion | flops 10485760 | bytes 8427520 | tf_op jit(solution)/shard_map/stack | solution.py:499
  232.8 0.1 copy.33
  232.9 0.0 copy-done.25
  232.9 1.3 collective-permute-start.2
  234.2 4.1 multiply_bitcast_fusion
  238.3 0.0 collective-permute-done.2
  238.3 0.3 copy.36
  238.6 0.0 copy-start.10
  238.6 0.0 copy-start.14
  238.6 2.0 pad_maximum_fusion
  240.7 0.1 copy-done.2
  240.8 0.1 copy-done.10
  240.9 5.2 %pad_maximum_fusion.1 = (f32[512,3,512]{0,2,1:T(8,128)}, bf16[512,3,512]{0,2,1:T(8,128)(2,1)S(1)}, f32[3,512]{1,0:T(4,128)S(1)}, f32[3,512]{1,0:T(4,128)S(1)}) fusion(f32[512,1,512]{0,2,1:T(8,128)S(1)} %copy-done.1, f32[512,1,512]{0,2,1:T(8,128)S(1)} %copy-done.2, f32[512,1,512]{0,2,1:T(8,128)S(1)} %bitcast.86, f32[514,3,512]{0,2,1:T(8,128)S(1)} %pad_maximum_fusion, ...), kind=kLoop, calls=%fused_computation.7 | loop fusion | flops 15725568 | bytes 15765504 | tf_op jit(solution)/shard_map/stack | solution.py:499
  246.1 0.0 copy-done.9
  246.1 1.7 fusion.50
  247.8 2.5 copy.37.refs_0_
  250.3 100.1 %reduce_all.1 = (f32[64,4096]{1,0:T(8,128)}, f32[64,4096]{1,0:T(8,128)}, bf16[2048,256]{1,0:T(8,128)(2,1)}) custom-call(bf16[512,2048]{1,0:T(8,128)(2,1)} %copy.37.refs_0_, bf16[2048,512]{1,0:T(8,128)(2,1)} %get-tuple-element.36.refs_1_, bf16[3,4096,512]{2,1,0:T(8,128)(2,1)} %bitcast.80, bf16[512,4096]{1,0:T(8,128)(2,1)} %refs_3_.1, ...), custom_call_target="tpu_custom_call" | custom-call | tf_op jit(solution)/shard_map/reduce_all/pallas_call | solution.py:422
  350.4 1.7 slice.241
  352.1 2.1 slice.240
  354.2 2.4 copy.39
  356.5 0.0 copy-start.15
  356.6 0.0 copy-start.13
  356.6 1.8 multiply_reduce_fusion.2
  358.4 0.0 copy-start.6
  358.4 0.0 copy-start.8
  358.5 69.0 %all-reduce = (bf16[3,3,512]{2,1,0:T(4,128)(2,1)S(1)}, bf16[7,512]{1,0:T(8,128)(2,1)S(1)}) all-reduce(bf16[3,3,512]{2,1,0:T(4,128)(2,1)S(1)} %fusion.48, bf16[7,512]{1,0:T(8,128)(2,1)S(1)} %copy-done.15), channel_id=1, replica_groups=mesh['ctx'=16,'tp'=8] {'ctx'}, use_global_device_ids=true, to_apply=%region_5.0 | all-reduce | flops 8192 | bytes 32768 | tf_op jit(solution)/shard_map/psum | solution.py:505
  427.5 0.6 convert_element_type.72
  428.1 0.6 convert_element_type.74
  428.7 1.6 fusion.33
  430.3 2.3 copy.38
  432.7 1.4 fusion.28
  (56 shorter events, 0.2 us)
Async XLA Ops:
  7.2 98.0 %all-gather.5.cloned.1.call-start = ((), (), s32[]{:S(2)}) async-start(), calls=%async_computation.1 | async-start | bytes 4718592 | tf_op jit(solution)/shard_map/all_gather | solution.py:466
  8.5 0.5 copy-start.29
  9.0 0.6 copy-start.27
  11.6 190.2 %all-gather.3.cloned.1.call-start = ((), (), s32[]{:S(2)}) async-start(), calls=%async_computation | async-start | bytes 4718592 | tf_op jit(solution)/shard_map/all_gather | solution.py:482
  12.3 17.0 %copy-start.16 = (f32[3,3,512]{2,1,0:T(4,128)S(1)}, f32[3,3,512]{2,1,0:T(4,128)}, u32[]{:S(2)}) copy-start(f32[3,3,512]{2,1,0:T(4,128)} %param.11) | copy-start | bytes 55300
  105.1 13.6 %copy-start.26 = (f32[7,512]{1,0:T(8,128)S(1)}, f32[7,512]{1,0:T(8,128)}, u32[]{:S(2)}) copy-start(f32[7,512]{1,0:T(8,128)} %param.12) | copy-start | bytes 43012
  116.1 7.9 %copy-start.5 = (bf16[512,1536]{1,0:T(8,128)(2,1)}, bf16[512,1536]{1,0:T(8,128)(2,1)S(1)}, u32[]{:S(2)}) copy-start(bf16[512,1536]{1,0:T(8,128)(2,1)S(1)} %convolution_convert_fusion) | copy-start | bytes 4718596
  117.2 3.0 collective-permute-start
  124.0 1.9 copy-start
  125.9 75.8 %copy-start.12 = (f32[6,512]{0,1:T(8,128)S(1)}, f32[6,512]{0,1:T(8,128)}, u32[]{:S(2)}) copy-start(f32[6,512]{0,1:T(8,128)} %fusion.47) | copy-start | bytes 36868
  126.5 83.9 %copy-start.7 = (f32[512,512]{0,1:T(8,128)}, f32[512,512]{0,1:T(8,128)S(1)}, u32[]{:S(2)}) copy-start(f32[512,512]{0,1:T(8,128)S(1)} %fusion.35) | copy-start | bytes 3145732
  201.8 10.2 %copy-start.17 = (f32[1,512]{1,0:T(1,128)S(1)}, f32[1,512]{1,0:T(1,128)}, u32[]{:S(2)}) copy-start(f32[1,512]{1,0:T(1,128)} %get-tuple-element.43) | copy-start | bytes 6148
  201.8 10.2 %copy-start.18 = (f32[1,512]{1,0:T(1,128)S(1)}, f32[1,512]{1,0:T(1,128)}, u32[]{:S(2)}) copy-start(f32[1,512]{1,0:T(1,128)} %get-tuple-element.44) | copy-start | bytes 6148
  201.8 10.2 %copy-start.19 = (f32[1,512]{1,0:T(1,128)S(1)}, f32[1,512]{1,0:T(1,128)}, u32[]{:S(2)}) copy-start(f32[1,512]{1,0:T(1,128)} %get-tuple-element.45) | copy-start | bytes 6148
  201.8 10.2 %copy-start.20 = (f32[1,512]{1,0:T(1,128)S(1)}, f32[1,512]{1,0:T(1,128)}, u32[]{:S(2)}) copy-start(f32[1,512]{1,0:T(1,128)} %get-tuple-element.46) | copy-start | bytes 6148
  201.8 10.2 %copy-start.21 = (f32[1,512]{1,0:T(1,128)S(1)}, f32[1,512]{1,0:T(1,128)}, u32[]{:S(2)}) copy-start(f32[1,512]{1,0:T(1,128)} %get-tuple-element.47) | copy-start | bytes 6148
  201.8 10.2 %copy-start.22 = (f32[1,512]{1,0:T(1,128)S(1)}, f32[1,512]{1,0:T(1,128)}, u32[]{:S(2)}) copy-start(f32[1,512]{1,0:T(1,128)} %get-tuple-element.48) | copy-start | bytes 6148
  201.8 10.2 %copy-start.23 = (f32[1,512]{1,0:T(1,128)S(1)}, f32[1,512]{1,0:T(1,128)}, u32[]{:S(2)}) copy-start(f32[1,512]{1,0:T(1,128)} %get-tuple-element.49) | copy-start | bytes 6148
  210.5 1.5 copy-start.3
  210.5 8.3 %collective-permute-start.1 = (f32[6,512]{0,1:T(8,128)S(1)}, f32[6,512]{0,1:T(8,128)S(1)}, u32[]{:S(2)}, u32[]{:S(2)}) collective-permute-start(f32[6,512]{0,1:T(8,128)S(1)} %slice.265), channel_id=1, source_target_pairs={{8,0},{16,8},{24,16},{32,24},{40,32},{48,40},{56,48},{64,56},{72,6... | collective-permute-start | bytes 36872 | tf_op jit(solution)/shard_map/ppermute | solution.py:15
  218.8 14.1 %copy-start.24 = (f32[2,1,512]{2,0,1:T(2,128)S(1)}, f32[2,1,512]{2,0,1:T(2,128)}, u32[]{:S(2)}) copy-start(f32[2,1,512]{2,0,1:T(2,128)} %copy.34) | copy-start | bytes 12292
  218.8 14.1 %copy-start.25 = (f32[2,1,512]{2,0,1:T(2,128)S(1)}, f32[2,1,512]{2,0,1:T(2,128)}, u32[]{:S(2)}) copy-start(f32[2,1,512]{2,0,1:T(2,128)} %copy.35) | copy-start | bytes 12292
  232.9 5.4 %collective-permute-start.2 = (f32[2,3,512]{2,0,1:T(2,128)S(1)}, f32[2,3,512]{2,0,1:T(2,128)S(1)}, u32[]{:S(2)}, u32[]{:S(2)}) collective-permute-start(f32[2,3,512]{2,0,1:T(2,128)S(1)} %pad_maximum_fusion.7), channel_id=1, source_target_pairs={{8,0},{16,8},{24,16},{32,24},{40,32},{48,40},{56,48},{64,56},{72,6... | collective-permute-start | bytes 36872 | tf_op jit(solution)/shard_map/ppermute | solution.py:15
  238.6 2.1 copy-start.1
  238.6 2.2 copy-start.2
  238.6 2.2 copy-start.10
  238.6 2.2 copy-start.14
  240.9 5.2 %copy-start.9 = (bf16[512,512]{0,1:T(8,128)(2,1)S(1)}, bf16[512,512]{0,1:T(8,128)(2,1)}, u32[]{:S(2)}) copy-start(bf16[512,512]{0,1:T(8,128)(2,1)} %get-tuple-element.31) | copy-start | bytes 1572868
  356.5 1.9 copy-start.15
  356.6 72.1 %copy-start.13 = (f32[4096]{0:T(1024)S(1)}, f32[4096]{0:T(1024)}, u32[]{:S(2)}) copy-start(f32[4096]{0:T(1024)} %param.9) | copy-start | bytes 49156
  356.6 73.7 %copy-start.30 = (f32[64]{0:T(128)S(1)}, f32[64]{0:T(128)}, u32[]{:S(2)}) copy-start(f32[64]{0:T(128)} %copy-done.29) | copy-start | bytes 772
  356.6 76.0 %copy-start.28 = (f32[64]{0:T(128)S(1)}, f32[64]{0:T(128)}, u32[]{:S(2)}) copy-start(f32[64]{0:T(128)} %copy-done.27) | copy-start | bytes 772
  358.4 74.3 %copy-start.4 = (bf16[64,4096]{1,0:T(8,128)(2,1)S(1)}, bf16[64,4096]{1,0:T(8,128)(2,1)}, u32[]{:S(2)}) copy-start(bf16[64,4096]{1,0:T(8,128)(2,1)} %param.7) | copy-start | bytes 1572868
  358.4 74.3 %copy-start.6 = (f32[64,4096]{1,0:T(8,128)S(1)}, f32[64,4096]{1,0:T(8,128)}, u32[]{:S(2)}) copy-start(f32[64,4096]{1,0:T(8,128)} %get-tuple-element.10) | copy-start | bytes 3145732
  358.4 74.2 %copy-start.8 = (bf16[64,4096]{1,0:T(8,128)(2,1)S(1)}, bf16[64,4096]{1,0:T(8,128)(2,1)}, u32[]{:S(2)}) copy-start(bf16[64,4096]{1,0:T(8,128)(2,1)} %param.8) | copy-start | bytes 1572868
  358.4 74.2 %copy-start.11 = (f32[64,4096]{1,0:T(8,128)S(1)}, f32[64,4096]{1,0:T(8,128)}, u32[]{:S(2)}) copy-start(f32[64,4096]{1,0:T(8,128)} %get-tuple-element.9) | copy-start | bytes 3145732
Sparse Core Ops, SparseCore 0:
  11.7 93.3 all-gather.4
  106.8 94.9 all-gather.2

commit v2 on v1

--- a/solution.py
+++ b/solution.py
@@ -9,43 +9,6 @@
 DELTAS = (2, 1, 3, 0)
 
 
-def passed_along(value, axis, steps):
-    count = lax.axis_size(axis)
-    first, last = (max(0, -steps), min(count, count - steps))
-    return lax.ppermute(value, axis, [(source, source + steps) for source in range(first, last)])
-
-
-def normed(values, gain):
-    floats = values.astype(jnp.float32)
-    factor = lax.rsqrt(jnp.mean(floats * floats, axis=-1, keepdims=True) + 1e-05)
-    return floats * factor * gain
-
-
-def taps_causal(extended, taps, number):
-    count = taps.shape[0]
-    summed = jnp.zeros((number,) + extended.shape[1:], jnp.float32)
-    for tap_index in range(count):
-        begin = count - 1 - tap_index
-        summed = summed + taps[tap_index] * extended[begin : begin + number]
-    return summed
-
-
-def taps_ahead(extended, taps, number):
-    count = taps.shape[0]
-    summed = jnp.zeros((number,) + extended.shape[1:], jnp.float32)
-    for tap_index in range(count):
-        summed = summed + taps[tap_index] * extended[tap_index : tap_index + number]
-    return summed
-
-
-def lagged_sums(grads, extended, number, count):
-    pieces = []
-    for tap_index in range(count):
-        begin = count - 1 - tap_index
-        pieces.append(jnp.sum(grads * extended[begin : begin + number], axis=0))
-    return jnp.stack(pieces)
-
-
 class Place:
     def __init__(self):
         ctx, tp = lax.axis_index("ctx"), lax.axis_index("tp")
@@ -66,6 +29,9 @@
         x = (self.x_hi * 2 + self.x_lo + step) % 4
         return (self.y * 4 + (x // 2) * 2 + self.core, self.z * 2 + x % 2)
 
+    def along_ctx(self, step):
+        return ((self.ctx + step) % 16, self.tp)
+
     def partner(self):
         return (self.ctx, self.z * 2 + 1 - self.x_lo)
 
@@ -91,13 +57,297 @@
     return pl.ds(pl.multiple_of(index * size, size), size)
 
 
+def gather_kernel(
+    scale, tokens,
+    hidden, cot, gain, taps, in_w_hbm, out_w_hbm,
+    norm_out, cot_out, acts, turned, lag_out,
+    both, in_w, out_w, proj, query, gates, grads, prods, lags,
+    load_sem, send_sem, recv_sem, edge_send, edge_recv, out_sem,
+):
+    here = Place()
+    block, width = hidden.shape
+    chans = out_w_hbm.shape[0]
+    half = block // 2
+    group = 2 * block
+    wide, span = 72, 64
+    bf16, f32 = jnp.bfloat16, jnp.float32
+
+    in_loads = [pltpu.make_async_copy(in_w_hbm.at[kind], in_w.at[kind], load_sem.at[kind]) for kind in range(3)]
+    out_load = pltpu.make_async_copy(out_w_hbm, out_w, load_sem.at[3])
+    for copy in in_loads + [out_load]:
+        copy.start()
+
+    barrier = pltpu.get_barrier_semaphore()
+    devices = [here.partner(), here.along_z(1), here.along_z(-1), here.along_ctx(1), here.along_ctx(-1)]
+    for device in devices:
+        pl.semaphore_signal(barrier, inc=1, device_id=device, device_id_type=MESH)
+
+    def normalise(index, carry):
+        at = tile(index, 16)
+        rows = pl.ds(pl.multiple_of(here.tp * block + index * 16, 16), 16)
+        floats = hidden[at, :].astype(f32)
+        factor = lax.rsqrt(jnp.mean(floats * floats, axis=-1, keepdims=True) + 1e-05)
+        both[0, rows, :] = (floats * factor * gain[...]).astype(bf16)
+        both[1, rows, :] = cot[at, :]
+        return carry
+
+    lax.fori_loop(0, block // 16, normalise, 0)
+    pl.semaphore_wait(barrier, len(devices))
+    sends = []
+
+    def go(copy):
+        copy.start()
+        sends.append(copy)
+
+    def rows_of(step, same, begin=0, size=block):
+        return pl.ds(pl.multiple_of(here.block(step, same) * block + begin, size), size)
+
+    def gather(which, slot):
+        rows, device = (
+            lambda: (rows_of(0, True), here.partner()),
+            lambda: (rows_of(0, True), here.along_z(1)),
+            lambda: (rows_of(0, True), here.along_z(-1)),
+            lambda: (rows_of(0, False), here.along_z(1)),
+            lambda: (rows_of(0, False), here.along_z(-1)),
+            lambda: (rows_of(-1, True, 0, half), here.along_z(1)),
+            lambda: (rows_of(1, True, half, half), here.along_z(-1)),
+            lambda: (rows_of(2, True), here.partner()),
+        )[slot]()
+        held = both.at[which, rows]
+        go(remote(held, held, send_sem.at[which, slot], recv_sem.at[which, slot], device))
+
+    def arrived(which, slot):
+        rows = (
+            lambda: rows_of(0, False),
+            lambda: rows_of(-1, True),
+            lambda: rows_of(1, True),
+            lambda: rows_of(-1, False),
+            lambda: rows_of(1, False),
+            lambda: rows_of(2, True, 0, half),
+            lambda: rows_of(2, True, half, half),
+            lambda: rows_of(2, False),
+        )[slot]()
+        held = both.at[which, rows]
+        remote(held, held, send_sem.at[which, slot], recv_sem.at[which, slot], here.partner()).wait_recv()
+
+    def project(step):
+        begin = ((here.z + step) % 4) * group
+
+        def loop(kind, carry):
+            value = jnp.dot(
+                both[0, pl.ds(pl.multiple_of(begin, group), group), :], in_w[kind], preferred_element_type=f32
+            )
+            proj[kind, pl.ds(pl.multiple_of(8 + begin, 8), group), :] = value.astype(bf16).astype(f32)
+            return carry
+
+        lax.fori_loop(0, 3, loop, 0)
+
+    def grade(step):
+        rows = pl.ds(pl.multiple_of(((here.z + step) % 4) * group, group), group)
+        value = lax.dot_general(
+            both[1, rows, :], out_w[...], (((1,), (1,)), ((), ())), preferred_element_type=f32
+        )
+        grads[0, rows, :] = value * query[rows, :]
+        grads[1, rows, :] = value * gates[rows, :]
+
+    for which in range(2):
+        for slot in range(3):
+            gather(which, slot)
+    arrived(0, 0)
+    gather(0, 3)
+    gather(0, 4)
+    arrived(0, 1)
+    gather(0, 5)
+    arrived(0, 2)
+    gather(0, 6)
+    for copy in in_loads:
+        copy.wait()
+    project(0)
+    arrived(1, 0)
+    gather(1, 3)
+    gather(1, 4)
+    arrived(1, 1)
+    gather(1, 5)
+    arrived(1, 2)
+    gather(1, 6)
+    arrived(0, 5)
+    arrived(0, 6)
+    gather(0, 7)
+    arrived(0, 3)
+    project(-1)
+    arrived(0, 4)
+    project(1)
+    arrived(1, 5)
+    arrived(1, 6)
+    gather(1, 7)
+    arrived(0, 7)
+    norm_copy = pltpu.make_async_copy(both.at[0], norm_out, out_sem.at[0])
+    norm_copy.start()
+    project(2)
+
+    edge = remote(
+        proj.at[:, pl.ds(tokens, 8), :], proj.at[:, pl.ds(0, 8), :], edge_send.at[0], edge_recv.at[0],
+        here.along_ctx(1))
+    go(edge)
+    edge.wait_recv()
+
+    @pl.when(here.ctx == 0)
+    def _():
+        proj[:, pl.ds(0, 8), :] = jnp.zeros((3, 8, chans), f32)
+
+    steps = chans // 128
+
+    def tap(row, cols):
+        return taps[pl.ds(row, 1), cols]
+
+    def behind(value, count):
+        return value if count == 0 else pltpu.roll(value, count, 0)
+
+    def ahead(value, count):
+        return value if count == 0 else pltpu.roll(value, wide - count, 0)
+
+    def forward(index, carry):
+        begin = pl.multiple_of((index // steps) * span, span)
+        cols = tile(index % steps, 128)
+        feats = []
+        for kind in range(3):
+            held = proj[kind, pl.ds(begin, wide), cols]
+            total = tap(kind, cols) * held
+            for lag in (1, 2):
+                total = total + tap(lag * 3 + kind, cols) * behind(held, lag)
+            feats.append(total)
+        product = feats[1] * feats[2]
+        total = tap(9, cols) * product
+        for lag in range(1, 7):
+            total = total + tap(9 + lag, cols) * behind(product, lag)
+        rows = pl.ds(begin, span)
+        query[rows, cols] = feats[0][8:]
+        grads[3, rows, cols] = feats[1][8:]
+        grads[2, rows, cols] = feats[2][8:]
+        gates[rows, cols] = total[8:]
+        prods[pl.ds(pl.multiple_of(begin + 8, 8), span), cols] = product[8:]
+
+        @pl.when(index < steps)
+        def _():
+            prods[pl.ds(0, 8), cols] = product[:8]
+
+        acts[rows, tile(3 * steps + index % steps, 128)] = (feats[0][8:] * total[8:]).astype(bf16)
+        return carry
+
+    lax.fori_loop(0, (tokens // span) * steps, forward, 0)
+    head = remote(
+        grads.at[pl.ds(2, 2), pl.ds(0, 8), :], grads.at[pl.ds(2, 2), pl.ds(tokens, 8), :],
+        edge_send.at[1], edge_recv.at[1], here.along_ctx(-1))
+    go(head)
+    lags[...] = jnp.zeros_like(lags)
+
+    def turn(index, carry):
+        turned[tile(index, 128), :] = acts[:, tile(index, 128)].T
+        return carry
+
+    lax.fori_loop(3 * steps, 4 * steps, turn, 0)
+    out_load.wait()
+    grade(0)
+    arrived(1, 3)
+    grade(-1)
+    arrived(1, 4)
+    grade(1)
+    arrived(1, 7)
+    cot_copy = pltpu.make_async_copy(both.at[1], cot_out, out_sem.at[1])
+    cot_copy.start()
+    grade(2)
+    front = remote(
+        grads.at[pl.ds(0, 2), pl.ds(0, 8), :], grads.at[pl.ds(0, 2), pl.ds(tokens, 8), :],
+        edge_send.at[2], edge_recv.at[2], here.along_ctx(-1))
+    go(front)
+    head.wait_recv()
+    front.wait_recv()
+
+    @pl.when(here.ctx == 15)
+    def _():
+        grads[pl.ds(0, 2), pl.ds(tokens, 8), :] = jnp.zeros((2, 8, chans), f32)
+
+    def backward(index, carry):
+        begin = pl.multiple_of((index // steps) * span, span)
+        cols = tile(index % steps, 128)
+        rows = pl.ds(begin, wide)
+        inner = grads[0, rows, cols]
+        total = tap(9, cols) * inner
+        for lag in range(1, 7):
+            total = total + tap(9 + lag, cols) * ahead(inner, lag)
+        feats = (grads[1, rows, cols], total * grads[2, rows, cols], total * grads[3, rows, cols])
+
+        def add_lag(row, value):
+            lags[row, :, cols] += jnp.sum(value.reshape(span // 8, 8, 128), axis=0)
+
+        for kind in range(3):
+            feat = feats[kind]
+            summed = tap(kind, cols) * feat
+            for lag in (1, 2):
+                summed = summed + tap(lag * 3 + kind, cols) * ahead(feat, lag)
+            acts[pl.ds(begin, span), tile(kind * steps + index % steps, 128)] = summed[:span].astype(bf16)
+            held = proj[kind, rows, cols]
+            for lag in range(3):
+                add_lag(lag * 3 + kind, feat[:span] * behind(held, lag)[8:])
+        product = prods[rows, cols]
+        for lag in range(7):
+            add_lag(9 + lag, inner[:span] * behind(product, lag)[8:])
+        return carry
+
+    lax.fori_loop(0, (tokens // span) * steps, backward, 0)
+    lax.fori_loop(0, 3 * steps, turn, 0)
+    lag_out[...] = jnp.sum(lags[...], axis=1) * scale
+    norm_copy.wait()
+    cot_copy.wait()
+    for copy in sends:
+        copy.wait_send()
+
+
+def gathered(hidden, cot, gain, taps, in_weight, out_weight, tokens, scale):
+    block, width = hidden.shape
+    chans = out_weight.shape[0]
+    any_space = pl.BlockSpec(memory_space=pl.ANY)
+    vmem_space = pl.BlockSpec(memory_space=pltpu.VMEM)
+    bf16, f32 = jnp.bfloat16, jnp.float32
+    dma = pltpu.SemaphoreType.DMA
+    body = lambda *refs: gather_kernel(scale, tokens, *refs)
+    return pl.pallas_call(
+        body,
+        out_shape=(
+            jax.ShapeDtypeStruct((tokens, width), bf16),
+            jax.ShapeDtypeStruct((tokens, width), bf16),
+            jax.ShapeDtypeStruct((tokens, 4 * chans), bf16),
+            jax.ShapeDtypeStruct((4 * chans, tokens), bf16),
+            jax.ShapeDtypeStruct((16, chans), f32),
+        ),
+        in_specs=[vmem_space] * 4 + [any_space] * 2,
+        out_specs=(any_space, any_space, vmem_space, vmem_space, vmem_space),
+        scratch_shapes=[
+            pltpu.VMEM((2, tokens, width), bf16),
+            pltpu.VMEM(in_weight.shape, bf16),
+            pltpu.VMEM(out_weight.shape, bf16),
+            pltpu.VMEM((3, tokens + 8, chans), f32),
+            pltpu.VMEM((tokens, chans), f32),
+            pltpu.VMEM((tokens, chans), f32),
+            pltpu.VMEM((4, tokens + 8, chans), f32),
+            pltpu.VMEM((tokens + 8, chans), f32),
+            pltpu.VMEM((16, 8, chans), f32),
+            dma((4,)), dma((2, 8)), dma((2, 8)), dma((3,)), dma((3,)), dma((2,)),
+        ],
+        compiler_params=pltpu.CompilerParams(
+            collective_id=1, has_side_effects=True, vmem_limit_bytes=60 * 2**20
+        ),
+        name="gather_all",
+    )(hidden, cot, gain, taps, in_weight, out_weight)
+
+
 def reduce_kernel(
     scale,
-    acts_hbm, turned_hbm, in_w_hbm, out_w_hbm, norm_hbm, cot_hbm,
-    branch_ref, gnorm_ref, shard_ref,
+    hidden, cot, gain, lag_in, acts_hbm, turned_hbm, in_w_hbm, out_w_hbm, norm_hbm, cot_hbm,
+    layer_ref, input_ref, in_grad_ref, out_grad_ref, lag_ref,
     acts, turned, in_w, out_w, norms, cots,
-    sib_out, sums, y_in, x_pass, x_in, parts, tp_in,
-    load_sem, in_w_sem, col_sem, sib_send, sib_recv, y_send, y_recv, x_send, x_recv, tp_send, tp_recv,
+    sib_out, sums, y_in, x_pass, x_in, parts, tp_in, lag_sum, lag_got,
+    lag_send, lag_recv, load_sem, in_w_sem, col_sem, sib_send, sib_recv, y_send, y_recv, x_send, x_recv, tp_send, tp_recv,
 ):
     here = Place()
     tokens, width = norm_hbm.shape
@@ -146,7 +396,7 @@
 
     greet(
         [here.sibling(), here.along_y(1), here.along_y(-1), here.along_z(1), here.along_z(-1),
-         here.along_x(1), here.along_x(-1)]
+         here.along_x(1), here.along_x(-1), here.along_x(2), here.along_y(2)]
     )
     sends = []
 
@@ -282,17 +532,36 @@
         add_rows(parts.at[which], here.block(0, False) * block, block, [tp_in.at[which, 1], tp_in.at[which, 2]], 16)
         go(tp_copy(which, 7))
 
-    def tp_finish(which, result):
+    def tp_total(which, index):
+        at = tile(index, 16)
+        rows = pl.ds(pl.multiple_of(here.tp * block + index * 16, 16), 16)
+        total = parts[which, rows, :].astype(jnp.float32)
+        for slot in (4, 5, 6):
+            total = total + tp_in[which, slot, at, :].astype(jnp.float32)
+        return at, total
+
+    def layer_finish():
         for slot in (5, 6, 7):
-            tp_copy(which, slot).wait_recv()
+            tp_copy(0, slot).wait_recv()
 
         def loop(index, carry):
-            at = tile(index, 16)
-            rows = pl.ds(pl.multiple_of(here.tp * block + index * 16, 16), 16)
-            total = parts[which, rows, :].astype(jnp.float32)
-            for slot in (4, 5, 6):
-                total = total + tp_in[which, slot, at, :].astype(jnp.float32)
-            result[at, :] = total
+            at, total = tp_total(0, index)
+            layer_ref[at, :] = (hidden[at, :].astype(jnp.float32) + total).astype(jnp.bfloat16)
+            return carry
+
+        lax.fori_loop(0, block // 16, loop, 0)
+
+    def input_finish():
+        for slot in (5, 6, 7):
+            tp_copy(1, slot).wait_recv()
+
+        def loop(index, carry):
+            at, total = tp_total(1, index)
+            floats = hidden[at, :].astype(jnp.float32)
+            factor = lax.rsqrt(jnp.mean(floats * floats, axis=-1, keepdims=True) + 1e-05)
+            gained = total * gain[...]
+            inner = jnp.mean(floats * gained, axis=-1, keepdims=True) * factor * factor * factor
+            input_ref[at, :] = (cot[at, :].astype(jnp.float32) + gained * factor - floats * inner).astype(jnp.bfloat16)
             return carry
 
         lax.fori_loop(0, block // 16, loop, 0)
@@ -334,6 +603,26 @@
 
         lax.fori_loop(0, steps_in, loop, 0)
 
+    def lag_copy(step):
+        device = (
+            lambda: here.sibling(),
+            lambda: here.along_x(2),
+            lambda: here.along_y(1 - 2 * (here.y % 2)),
+            lambda: here.along_y(2),
+        )[step]()
+        return remote(lag_sum.at[step], lag_got.at[step], lag_send.at[step], lag_recv.at[step], device)
+
+    def lag_step(step):
+        lag_copy(step).wait_recv()
+        total = lag_sum[step] + lag_got[step]
+        if step < 3:
+            lag_sum[step + 1] = total
+            go(lag_copy(step + 1))
+        else:
+            lag_ref[...] = total
+
+    lag_sum[0] = lag_in[...]
+    go(lag_copy(0))
     turned_load.wait()
     for_sibling(0)
     for_sibling(1)
@@ -353,9 +642,11 @@
     for_sibling(4)
     for_self(3)
     tp_halves(0)
+    lag_step(0)
     gnorm_product()
     tp_begin(1)
     y_pass(0)
+    lag_step(1)
     for_sibling(5)
     for_self(4)
     go(y_copy(1, 0))
@@ -368,6 +659,7 @@
     go(y_copy(1, 3))
     for_self(7)
     tp_direct(0)
+    lag_step(2)
     tp_last(0)
     y_done(0)
     add_rows(sums.at[3], 0, half, [y_in.at[0, 3], y_in.at[0, 4]])
@@ -376,28 +668,34 @@
     go(x_copy(1))
     tp_halves(1)
     y_pass(1)
+    lag_step(3)
     tp_direct(1)
     tp_last(1)
     for side in range(2):
         x_copy(side).wait_recv()
         go(x_forward(side))
-    tp_finish(0, branch_ref)
-    tp_finish(1, gnorm_ref)
+    layer_finish()
+    input_finish()
     x_forward(0).wait_recv()
     x_forward(1).wait_recv()
     y_done(1)
 
+    def last_rows(row, pairs):
+        total = sums[7, row, :].astype(jnp.float32)
+        for other, at in pairs:
+            total = total + other[at, :].astype(jnp.float32)
+        return total
+
     def last(begin, others):
-        def loop(index, carry):
-            at = tile(index, 128)
-            rows = pl.ds(pl.multiple_of(begin + index * 128, 128), 128)
-            total = sums[7, rows, :].astype(jnp.float32)
-            for other in others:
-                total = total + other[at, :].astype(jnp.float32)
-            shard_ref[rows, :] = total.astype(jnp.bfloat16)
-            return carry
-
-        lax.fori_loop(0, half // 128, loop, 0)
+        for index in range(half // 128):
+            row = begin + index * 128
+            at = pl.ds(index * 128, 128)
+            total = last_rows(pl.ds(row, 128), [(other, at) for other in others])
+            kind, first = row // chans, row % chans
+            if kind < 3:
+                in_grad_ref[kind, :, pl.ds(first, 128)] = total.T.astype(jnp.bfloat16)
+            else:
+                out_grad_ref[pl.ds(first, 128), :] = total.astype(jnp.bfloat16)
 
     last(0, [y_in.at[1, 3], y_in.at[1, 4], x_in.at[0]])
     last(half, [y_in.at[1, 2], y_in.at[1, 5], x_in.at[1]])
@@ -407,7 +705,7 @@
         copy.wait_send()
 
 
-def reduced(acts, turned, in_weight, out_weight, norms, cots, scale):
+def reduced(hidden, cot, gain, lags, acts, turned, in_weight, out_weight, norms, cots, scale):
     tokens, width = norms.shape
     chans = out_weight.shape[0]
     rows_all = turned.shape[0]
@@ -422,12 +720,14 @@
     return pl.pallas_call(
         body,
         out_shape=(
-            jax.ShapeDtypeStruct((block, width), jnp.float32),
-            jax.ShapeDtypeStruct((block, width), jnp.float32),
-            jax.ShapeDtypeStruct((rows_all, cut), bf16),
+            jax.ShapeDtypeStruct((block, width), bf16),
+            jax.ShapeDtypeStruct((block, width), bf16),
+            jax.ShapeDtypeStruct((3, cut, chans), bf16),
+            jax.ShapeDtypeStruct((chans, cut), bf16),
+            jax.ShapeDtypeStruct((16, chans), jnp.float32),
         ),
-        in_specs=[any_space] * 6,
-        out_specs=(vmem_space, vmem_space, vmem_space),
+        in_specs=[vmem_space] * 4 + [any_space] * 6,
+        out_specs=(vmem_space,) * 5,
         scratch_shapes=[
             pltpu.VMEM(acts.shape, bf16),
             pltpu.VMEM(turned.shape, bf16),
@@ -442,83 +742,33 @@
             pltpu.VMEM((2, half, cut), bf16),
             pltpu.VMEM((2, tokens, width), bf16),
             pltpu.VMEM((2, 7, block, width), bf16),
-            dma((3,)), dma((2,)), dma((2, 16)),
+            pltpu.VMEM((4, 16, chans), jnp.float32),
+            pltpu.VMEM((4, 16, chans), jnp.float32),
+            dma((4,)), dma((4,)), dma((3,)), dma((2,)), dma((2, 16)),
             dma((8,)), dma((8,)), dma((2, 6)), dma((2, 6)), dma((4,)), dma((4,)), dma((2, 8)), dma((2, 8)),
         ],
         compiler_params=pltpu.CompilerParams(
             collective_id=0, has_side_effects=True, vmem_limit_bytes=63 * 2**20
         ),
         name="reduce_all",
-    )(acts, turned, in_weight, out_weight, norms, cots)
+    )(hidden, cot, gain, lags, acts, turned, in_weight, out_weight, norms, cots)
 
 
 def local(hidden_in, cotangent, norm_gain, in_weight, filter_taps, inner_taps, out_weight):
-    rows_local = hidden_in.shape[0]
-    model_width = hidden_in.shape[1]
     channels = in_weight.shape[2]
-    block_rows = rows_local * lax.axis_size("tp")
-    loss_scale = (block_rows * lax.axis_size("ctx")) ** (-0.5)
-    short_edge = filter_taps.shape[0] - 1
-    inner_edge = inner_taps.shape[0] - 1
-    reach = short_edge + inner_edge
-    normal_rows = normed(hidden_in, norm_gain).astype(jnp.bfloat16)
-    flat_in = in_weight.reshape(model_width, 3 * channels)
-    gathered = lax.all_gather(normal_rows, "tp", axis=0, tiled=True)
-    projected = jnp.dot(gathered, flat_in, preferred_element_type=jnp.float32).astype(jnp.bfloat16)
-    projected = projected.reshape(block_rows, 3, channels)
-    earlier = passed_along(projected[block_rows - reach :], "ctx", 1)
-    blended = taps_causal(
-        jnp.concatenate([earlier, projected]), filter_taps, block_rows + inner_edge
+    tokens = hidden_in.shape[0] * lax.axis_size("tp")
+    scale = (tokens * lax.axis_size("ctx")) ** (-0.5)
+    gain = norm_gain.reshape(1, -1)
+    taps = jnp.concatenate([filter_taps.reshape(9, channels), inner_taps])
+    kinds = jnp.transpose(in_weight, (1, 0, 2))
+    norms, cots, acts, turned, lags = gathered(
+        hidden_in, cotangent, gain, taps, kinds, out_weight, tokens, scale
     )
-    features = blended[inner_edge:]
-    before = blended[:inner_edge, 1] * blended[:inner_edge, 2]
-    shifted_in = jnp.concatenate([earlier[inner_edge:], projected])
-    query_vals = features[:, 0]
-    key_vals = features[:, 1]
-    value_vals = features[:, 2]
-    wide_prods = jnp.concatenate([before, key_vals * value_vals])
-    gate_vals = taps_causal(wide_prods, inner_taps, block_rows)
-    mixed = (query_vals * gate_vals).astype(jnp.bfloat16)
-    grad_all = lax.all_gather(cotangent, "tp", axis=0, tiled=True)
-    grad_mixed = lax.dot_general(
-        grad_all, out_weight, (((1,), (1,)), ((), ())), preferred_element_type=jnp.float32
+    layer_out, grad_input, grad_kinds, grad_out_weight, lags = reduced(
+        hidden_in, cotangent, gain, lags, acts, turned, kinds, out_weight, norms, cots, scale
     )
-    grad_query = grad_mixed * gate_vals
-    grad_gates = grad_mixed * query_vals
-    head_prod = taps_ahead(grad_gates[:reach], inner_taps, short_edge)
-    head_feat = jnp.stack(
-        [
-            grad_query[:short_edge],
-            head_prod * value_vals[:short_edge],
-            head_prod * key_vals[:short_edge],
-        ],
-        axis=1,
-    )
-    next_gates, next_feat = passed_along((grad_gates[:inner_edge], head_feat), "ctx", -1)
-    grad_products = taps_ahead(jnp.concatenate([grad_gates, next_gates]), inner_taps, block_rows)
-    grad_features = jnp.stack(
-        [grad_query, grad_products * value_vals, grad_products * key_vals], axis=1
-    )
-    filter_part = lagged_sums(grad_features, shifted_in, block_rows, short_edge + 1) * loss_scale
-    inner_part = lagged_sums(grad_gates, wide_prods, block_rows, inner_edge + 1) * loss_scale
-    grad_filter, grad_inner = (
-        lax.psum(filter_part.astype(jnp.bfloat16), "ctx").astype(jnp.float32),
-        lax.psum(inner_part.astype(jnp.bfloat16), "ctx").astype(jnp.float32),
-    )
-    grad_proj = taps_ahead(
-        jnp.concatenate([grad_features, next_feat]), filter_taps, block_rows
-    ).astype(jnp.bfloat16)
-    acts = jnp.concatenate([grad_proj.reshape(block_rows, 3 * channels), mixed], axis=1)
-    branch, grad_normed, shard = reduced(
-        acts, acts.T, jnp.transpose(in_weight, (1, 0, 2)), out_weight, gathered, grad_all, loss_scale
-    )
-    layer_out = (hidden_in.astype(jnp.float32) + branch).astype(jnp.bfloat16)
-    _, pullback = jax.vjp(lambda values: normed(values, norm_gain), hidden_in.astype(jnp.float32))
-    grad_input = (cotangent.astype(jnp.float32) + pullback(grad_normed)[0]).astype(jnp.bfloat16)
-    cut = shard.shape[1]
-    grad_in_weight = jnp.transpose(shard[: 3 * channels].reshape(3, channels, cut), (2, 0, 1))
-    grad_out_weight = shard[3 * channels :]
-    return (layer_out, grad_input, grad_in_weight, grad_out_weight, grad_filter, grad_inner)
+    grad_in_weight = jnp.transpose(grad_kinds, (1, 0, 2))
+    return (layer_out, grad_input, grad_in_weight, grad_out_weight, lags[:9].reshape(3, 3, channels), lags[9:])
 
 
 def solution(mesh):

time: 442 us -> 214 us (0.48)
  waiting for transfers between devices: 151 us -> 0 us
  Pallas kernels: 100 us -> 200 us
  blocking collectives: 69 us -> 0 us
  other arithmetic: 45 us -> 1.34 us
  local copies, waits for them, and re-layouts: 36.9 us -> 10.9 us
  matrix products: 19.6 us -> 0 us
  between operations: 14.5 us -> 0.65 us
    all_gather x2 -> x0, waiting for transfers between devices: 150 us -> none  [the longest x1 75.2 us: local(): gathered = lax.all_gather(normal_rows, 'tp', axis=0, tiled=True)]
    pallas_call x1 -> x2, Pallas kernels: 100 us -> 200 us  [the longest x1 104 us: reduced(): pl.pallas_call(body, out_shape=(jax.ShapeDtypeStruct((block, width), bf16...]
    psum x1 -> x0, blocking collectives: 69 us -> none  [local(): lax.psum(filter_part.astype(jnp.bfloat16), 'ctx').astype(jnp.float32)]
    another operation x6 -> x0, other arithmetic: 26.3 us -> none  [the longest x3 23.2 us: local(): jnp.stack([grad_query, grad_products * value_vals, grad_products * key_va...]
    dot_general x2 -> x0, matrix products: 19.6 us -> none  [the longest x1 11 us: local(): jnp.dot(gathered, flat_in, preferred_element_type=jnp.float32)]
    unnamed x63 -> x4, local copies, waits for them, and re-layouts: 19.4 us -> 7.47 us
    convert_element_type x6 -> x0, other arithmetic: 5.21 us -> none  [the longest x1 2.02 us: local(): normal_rows = normed(hidden_in, norm_gain).astype(jnp.bfloat16)]
    slice x7 -> x1, local copies, waits for them, and re-layouts: 6.44 us -> 1.33 us  [local(): lags[9:]]
  transfers between devices with their start and end apart: 5 -> 0, of which waited for: 3 -> 0; matrix products, arithmetic and copies ran while one was open for 11% -> 0% of each run, Pallas kernels for 0% -> 0%
where the time goes in v2:
time: 214 us; the launch traced here: 213 us
  Pallas kernels  200 us (93%)
  local copies, waits for them, and re-layouts  10.9 us (5%)
    pallas_call x1, Pallas kernels, reduced(): pl.pallas_call(body, out_shape=(jax.ShapeDtypeStruct((block, width), bf16...  104 us
    pallas_call x1, Pallas kernels, gathered(): pl.pallas_call(body, out_shape=(jax.ShapeDtypeStruct((tokens, width), bf1...  96.2 us
    unnamed x4, local copies, waits for them, and re-layouts  7.47 us

profile of v2, /device:TPU:0, one launch (start us, length us, event | category | flops | bytes accessed | tf_op | source)
XLA Modules:
  0.0 212.8 jit_solution(11950104120923882298)
XLA Ops:
  0.6 0.8 reshape.22
  1.4 1.3 pad_maximum_fusion.refs_3_
  2.7 96.2 %gather_all.1 = (bf16[512,4096]{1,0:T(8,128)(2,1)}, bf16[512,4096]{1,0:T(8,128)(2,1)}, bf16[512,2048]{1,0:T(8,128)(2,1)}, bf16[2048,512]{1,0:T(8,128)(2,1)}, f32[16,512]{1,0:T(8,128)}) custom-call(bf16[64,4096]{1,0:T(8,128)(2,1)} %refs_0_.3, bf16[64,4096]{1,0:T(8,128)(2,1)} %refs_1_.3, f32[1,4096]{1,0:T(1,128)} %bitcast.8, ...), custom_call_target="tpu_custom_call" | custom-call | tf_op jit(solution)/shard_map/gather_all/pallas_call | solution.py:314
  99.0 103.7 %reduce_all.1 = (bf16[64,4096]{1,0:T(8,128)(2,1)}, bf16[64,4096]{1,0:T(8,128)(2,1)}, bf16[3,256,512]{2,1,0:T(8,128)(2,1)}, bf16[512,256]{1,0:T(8,128)(2,1)}, f32[16,512]{1,0:T(8,128)}) custom-call(bf16[64,4096]{1,0:T(8,128)(2,1)} %refs_0_.3, bf16[64,4096]{1,0:T(8,128)(2,1)} %refs_1_.3, f32[1,4096]{1,0:T(1,128)} %bitcast.9, ...), custom_call_target="tpu_custom_call" | custom-call | tf_op jit(solution)/shard_map/reduce_all/pallas_call | solution.py:720
  202.6 1.3 slice.7
  204.0 1.4 reshape.23
  205.3 1.9 copy.17
  207.2 1.9 copy.18
  209.1 2.1 copy.19
  211.1 1.7 copy.20

commit v3 on v2

--- a/solution.py
+++ b/solution.py
@@ -59,9 +59,9 @@
 
 def gather_kernel(
     scale, tokens,
-    hidden, cot, gain, taps, in_w_hbm, out_w_hbm,
-    norm_out, cot_out, acts, turned, lag_out,
-    both, in_w, out_w, proj, query, gates, grads, prods, lags,
+    hidden, cot, gain, short_taps, inner_taps, in_w_hbm, out_w_hbm,
+    norm_out, cot_out, acts_out, turned_out, lag_out,
+    both, in_w, out_w, proj, query, gates, grads, prods, lags, acts, turned,
     load_sem, send_sem, recv_sem, edge_send, edge_recv, out_sem,
 ):
     here = Place()
@@ -150,26 +150,20 @@
         grads[0, rows, :] = value * query[rows, :]
         grads[1, rows, :] = value * gates[rows, :]
 
-    for which in range(2):
-        for slot in range(3):
-            gather(which, slot)
-    arrived(0, 0)
-    gather(0, 3)
-    gather(0, 4)
+    for slot in range(3):
+        gather(0, slot)
     arrived(0, 1)
     gather(0, 5)
     arrived(0, 2)
     gather(0, 6)
+    arrived(0, 0)
+    gather(0, 3)
+    gather(0, 4)
+    for slot in range(3):
+        gather(1, slot)
     for copy in in_loads:
         copy.wait()
     project(0)
-    arrived(1, 0)
-    gather(1, 3)
-    gather(1, 4)
-    arrived(1, 1)
-    gather(1, 5)
-    arrived(1, 2)
-    gather(1, 6)
     arrived(0, 5)
     arrived(0, 6)
     gather(0, 7)
@@ -177,28 +171,33 @@
     project(-1)
     arrived(0, 4)
     project(1)
-    arrived(1, 5)
-    arrived(1, 6)
-    gather(1, 7)
+    arrived(1, 1)
+    gather(1, 5)
+    arrived(1, 2)
+    gather(1, 6)
     arrived(0, 7)
-    norm_copy = pltpu.make_async_copy(both.at[0], norm_out, out_sem.at[0])
-    norm_copy.start()
     project(2)
-
     edge = remote(
         proj.at[:, pl.ds(tokens, 8), :], proj.at[:, pl.ds(0, 8), :], edge_send.at[0], edge_recv.at[0],
         here.along_ctx(1))
     go(edge)
-    edge.wait_recv()
-
-    @pl.when(here.ctx == 0)
-    def _():
-        proj[:, pl.ds(0, 8), :] = jnp.zeros((3, 8, chans), f32)
+    arrived(1, 0)
+    gather(1, 3)
+    gather(1, 4)
+    arrived(1, 5)
+    arrived(1, 6)
+    gather(1, 7)
+    norm_copy = pltpu.make_async_copy(both.at[0], norm_out, out_sem.at[0])
+    norm_copy.start()
 
     steps = chans // 128
-
-    def tap(row, cols):
-        return taps[pl.ds(row, 1), cols]
+    bands = tokens // span
+
+    def short(lag, kind, cols):
+        return short_taps[lag, pl.ds(kind, 1), cols]
+
+    def inner(lag, cols):
+        return inner_taps[pl.ds(lag, 1), cols]
 
     def behind(value, count):
         return value if count == 0 else pltpu.roll(value, count, 0)
@@ -212,29 +211,31 @@
         feats = []
         for kind in range(3):
             held = proj[kind, pl.ds(begin, wide), cols]
-            total = tap(kind, cols) * held
+            total = short(0, kind, cols) * held
             for lag in (1, 2):
-                total = total + tap(lag * 3 + kind, cols) * behind(held, lag)
+                total = total + short(lag, kind, cols) * behind(held, lag)
             feats.append(total)
         product = feats[1] * feats[2]
-        total = tap(9, cols) * product
+        total = inner(0, cols) * product
         for lag in range(1, 7):
-            total = total + tap(9 + lag, cols) * behind(product, lag)
+            total = total + inner(lag, cols) * behind(product, lag)
         rows = pl.ds(begin, span)
         query[rows, cols] = feats[0][8:]
         grads[3, rows, cols] = feats[1][8:]
         grads[2, rows, cols] = feats[2][8:]
         gates[rows, cols] = total[8:]
-        prods[pl.ds(pl.multiple_of(begin + 8, 8), span), cols] = product[8:]
-
-        @pl.when(index < steps)
-        def _():
-            prods[pl.ds(0, 8), cols] = product[:8]
-
+        prods[rows, cols] = product[8:]
         acts[rows, tile(3 * steps + index % steps, 128)] = (feats[0][8:] * total[8:]).astype(bf16)
         return carry
 
-    lax.fori_loop(0, (tokens // span) * steps, forward, 0)
+    lax.fori_loop(steps, bands * steps, forward, 0)
+    edge.wait_recv()
+
+    @pl.when(here.ctx == 0)
+    def _():
+        proj[:, pl.ds(0, 8), :] = jnp.zeros((3, 8, chans), f32)
+
+    lax.fori_loop(0, steps, forward, 0)
     head = remote(
         grads.at[pl.ds(2, 2), pl.ds(0, 8), :], grads.at[pl.ds(2, 2), pl.ds(tokens, 8), :],
         edge_send.at[1], edge_recv.at[1], here.along_ctx(-1))
@@ -260,50 +261,59 @@
         grads.at[pl.ds(0, 2), pl.ds(0, 8), :], grads.at[pl.ds(0, 2), pl.ds(tokens, 8), :],
         edge_send.at[2], edge_recv.at[2], here.along_ctx(-1))
     go(front)
-    head.wait_recv()
-    front.wait_recv()
-
-    @pl.when(here.ctx == 15)
-    def _():
-        grads[pl.ds(0, 2), pl.ds(tokens, 8), :] = jnp.zeros((2, 8, chans), f32)
 
     def backward(index, carry):
         begin = pl.multiple_of((index // steps) * span, span)
         cols = tile(index % steps, 128)
         rows = pl.ds(begin, wide)
-        inner = grads[0, rows, cols]
-        total = tap(9, cols) * inner
-        for lag in range(1, 7):
-            total = total + tap(9 + lag, cols) * ahead(inner, lag)
-        feats = (grads[1, rows, cols], total * grads[2, rows, cols], total * grads[3, rows, cols])
+        here_rows = pl.ds(begin, span)
 
         def add_lag(row, value):
             lags[row, :, cols] += jnp.sum(value.reshape(span // 8, 8, 128), axis=0)
 
+        gated = grads[0, rows, cols]
+        product = prods[here_rows, cols]
+        total = inner(0, cols) * gated
+        add_lag(9, gated[:span] * product)
+        for lag in range(1, 7):
+            moved = ahead(gated, lag)
+            total = total + inner(lag, cols) * moved
+            add_lag(9 + lag, moved[:span] * product)
+        feats = (grads[1, rows, cols], total * grads[2, rows, cols], total * grads[3, rows, cols])
         for kind in range(3):
             feat = feats[kind]
-            summed = tap(kind, cols) * feat
+            held = proj[kind, pl.ds(pl.multiple_of(begin + 8, 8), span), cols]
+            summed = short(0, kind, cols) * feat[:span]
+            add_lag(kind, feat[:span] * held)
             for lag in (1, 2):
-                summed = summed + tap(lag * 3 + kind, cols) * ahead(feat, lag)
-            acts[pl.ds(begin, span), tile(kind * steps + index % steps, 128)] = summed[:span].astype(bf16)
-            held = proj[kind, rows, cols]
-            for lag in range(3):
-                add_lag(lag * 3 + kind, feat[:span] * behind(held, lag)[8:])
-        product = prods[rows, cols]
-        for lag in range(7):
-            add_lag(9 + lag, inner[:span] * behind(product, lag)[8:])
+                moved = ahead(feat, lag)[:span]
+                summed = summed + short(lag, kind, cols) * moved
+                add_lag(lag * 3 + kind, moved * held)
+            acts[here_rows, tile(kind * steps + index % steps, 128)] = summed.astype(bf16)
         return carry
 
-    lax.fori_loop(0, (tokens // span) * steps, backward, 0)
+    lax.fori_loop(0, (bands - 1) * steps, backward, 0)
+    head.wait_recv()
+    front.wait_recv()
+
+    @pl.when(here.ctx == 15)
+    def _():
+        grads[pl.ds(0, 2), pl.ds(tokens, 8), :] = jnp.zeros((2, 8, chans), f32)
+
+    lax.fori_loop((bands - 1) * steps, bands * steps, backward, 0)
+    acts_copy = pltpu.make_async_copy(acts, acts_out, out_sem.at[2])
+    acts_copy.start()
     lax.fori_loop(0, 3 * steps, turn, 0)
+    turned_copy = pltpu.make_async_copy(turned, turned_out, out_sem.at[3])
+    turned_copy.start()
     lag_out[...] = jnp.sum(lags[...], axis=1) * scale
-    norm_copy.wait()
-    cot_copy.wait()
+    for copy in (norm_copy, cot_copy, acts_copy, turned_copy):
+        copy.wait()
     for copy in sends:
         copy.wait_send()
 
 
-def gathered(hidden, cot, gain, taps, in_weight, out_weight, tokens, scale):
+def gathered(hidden, cot, gain, short_taps, inner_taps, in_weight, out_weight, tokens, scale):
     block, width = hidden.shape
     chans = out_weight.shape[0]
     any_space = pl.BlockSpec(memory_space=pl.ANY)
@@ -320,8 +330,8 @@
             jax.ShapeDtypeStruct((4 * chans, tokens), bf16),
             jax.ShapeDtypeStruct((16, chans), f32),
         ),
-        in_specs=[vmem_space] * 4 + [any_space] * 2,
-        out_specs=(any_space, any_space, vmem_space, vmem_space, vmem_space),
+        in_specs=[vmem_space] * 5 + [any_space] * 2,
+        out_specs=(any_space, any_space, any_space, any_space, vmem_space),
         scratch_shapes=[
             pltpu.VMEM((2, tokens, width), bf16),
             pltpu.VMEM(in_weight.shape, bf16),
@@ -330,15 +340,17 @@
             pltpu.VMEM((tokens, chans), f32),
             pltpu.VMEM((tokens, chans), f32),
             pltpu.VMEM((4, tokens + 8, chans), f32),
-            pltpu.VMEM((tokens + 8, chans), f32),
+            pltpu.VMEM((tokens, chans), f32),
             pltpu.VMEM((16, 8, chans), f32),
-            dma((4,)), dma((2, 8)), dma((2, 8)), dma((3,)), dma((3,)), dma((2,)),
+            pltpu.VMEM((tokens, 4 * chans), bf16),
+            pltpu.VMEM((4 * chans, tokens), bf16),
+            dma((4,)), dma((2, 8)), dma((2, 8)), dma((3,)), dma((3,)), dma((4,)),
         ],
         compiler_params=pltpu.CompilerParams(
             collective_id=1, has_side_effects=True, vmem_limit_bytes=60 * 2**20
         ),
         name="gather_all",
-    )(hidden, cot, gain, taps, in_weight, out_weight)
+    )(hidden, cot, gain, short_taps, inner_taps, in_weight, out_weight)
 
 
 def reduce_kernel(
@@ -398,11 +410,14 @@
         [here.sibling(), here.along_y(1), here.along_y(-1), here.along_z(1), here.along_z(-1),
          here.along_x(1), here.along_x(-1), here.along_x(2), here.along_y(2)]
     )
-    sends = []
-
-    def go(copy):
+    sends = {}
+
+    def go(name, copy):
         copy.start()
-        sends.append(copy)
+        sends[name] = copy
+
+    def drained(name):
+        sends.pop(name).wait_send()
 
     def product(position, write):
         for copy in loads(position):
@@ -468,10 +483,10 @@
     def y_pass(group):
         y_copy(group, 0).wait_recv()
         add_rows(sums.at[group * 4 + 1], 0, half, [y_in.at[group, 0]])
-        go(y_copy(group, 4))
+        go(("y", group, 4), y_copy(group, 4))
         y_copy(group, 1).wait_recv()
         add_rows(sums.at[group * 4 + 2], half, half, [y_in.at[group, 1]])
-        go(y_copy(group, 5))
+        go(("y", group, 5), y_copy(group, 5))
 
     def y_done(group):
         for slot in (3, 4, 2, 5):
@@ -508,29 +523,29 @@
 
     def tp_begin(which):
         for slot in range(3):
-            go(tp_copy(which, slot))
+            go(("tp", which, slot), tp_copy(which, slot))
 
     def tp_halves(which):
         tp_copy(which, 0).wait_recv()
         add_rows(parts.at[which], here.block(2, True) * block, block, [tp_in.at[which, 0]], 16)
-        go(tp_copy(which, 3))
-        go(tp_copy(which, 4))
+        go(("tp", which, 3), tp_copy(which, 3))
+        go(("tp", which, 4), tp_copy(which, 4))
 
     def tp_direct(which):
         tp_copy(which, 3).wait_recv()
         add_rows(parts.at[which], here.block(1, True) * block, quarter, [tp_in.at[which, 3, pl.ds(0, quarter)]], 16)
-        go(tp_copy(which, 5))
+        go(("tp", which, 5), tp_copy(which, 5))
         tp_copy(which, 4).wait_recv()
         add_rows(
             parts.at[which], here.block(-1, True) * block + quarter, quarter,
             [tp_in.at[which, 3, pl.ds(quarter, quarter)]], 16)
-        go(tp_copy(which, 6))
+        go(("tp", which, 6), tp_copy(which, 6))
 
     def tp_last(which):
         tp_copy(which, 1).wait_recv()
         tp_copy(which, 2).wait_recv()
         add_rows(parts.at[which], here.block(0, False) * block, block, [tp_in.at[which, 1], tp_in.at[which, 2]], 16)
-        go(tp_copy(which, 7))
+        go(("tp", which, 7), tp_copy(which, 7))
 
     def tp_total(which, index):
         at = tile(index, 16)
@@ -582,18 +597,13 @@
             slot = step % 2
             in_load(step, slot).wait()
 
-            def inner(index, carry):
-                rows = tile(index, tokens // 2)
-                value = jnp.zeros((tokens // 2, step_in), jnp.float32)
-                for kind in range(3):
-                    value = value + lax.dot_general(
-                        acts[rows, pl.ds(kind * chans, chans)], in_w[slot, kind],
-                        (((1,), (1,)), ((), ())), preferred_element_type=jnp.float32,
-                    )
-                parts[1, rows, tile(step, step_in)] = value.astype(jnp.bfloat16)
-                return carry
-
-            lax.fori_loop(0, 2, inner, 0)
+            value = jnp.zeros((tokens, step_in), jnp.float32)
+            for kind in range(3):
+                value = value + lax.dot_general(
+                    acts[:, pl.ds(kind * chans, chans)], in_w[slot, kind],
+                    (((1,), (1,)), ((), ())), preferred_element_type=jnp.float32,
+                )
+            parts[1, :, tile(step, step_in)] = value.astype(jnp.bfloat16)
 
             @pl.when(step + 2 < steps_in)
             def _():
@@ -617,63 +627,70 @@
         total = lag_sum[step] + lag_got[step]
         if step < 3:
             lag_sum[step + 1] = total
-            go(lag_copy(step + 1))
+            go(("lag", step + 1), lag_copy(step + 1))
         else:
             lag_ref[...] = total
 
+    def y_go(group, slot):
+        go(("y", group, slot), y_copy(group, slot))
+
     lag_sum[0] = lag_in[...]
-    go(lag_copy(0))
+    go(("lag", 0), lag_copy(0))
     turned_load.wait()
     for_sibling(0)
     for_sibling(1)
     for_self(0)
-    go(y_copy(0, 0))
-    go(y_copy(0, 1))
+    y_go(0, 0)
+    y_go(0, 1)
     acts_load.wait()
     out_load.wait()
     branch_product()
     tp_begin(0)
     for_sibling(2)
     for_self(1)
-    go(y_copy(0, 2))
+    y_go(0, 2)
     for_sibling(3)
     for_self(2)
-    go(y_copy(0, 3))
+    y_go(0, 3)
+    lag_step(0)
+    gnorm_product()
+    tp_halves(0)
+    tp_last(0)
+    tp_begin(1)
+    y_pass(0)
     for_sibling(4)
     for_self(3)
-    tp_halves(0)
-    lag_step(0)
-    gnorm_product()
-    tp_begin(1)
-    y_pass(0)
-    lag_step(1)
     for_sibling(5)
     for_self(4)
-    go(y_copy(1, 0))
-    go(y_copy(1, 1))
+    tp_direct(0)
     for_sibling(6)
     for_self(5)
-    go(y_copy(1, 2))
     for_sibling(7)
     for_self(6)
-    go(y_copy(1, 3))
     for_self(7)
-    tp_direct(0)
-    lag_step(2)
-    tp_last(0)
+    lag_step(1)
+    for slot in range(4):
+        drained(("y", 0, slot))
+    y_go(1, 0)
+    y_go(1, 1)
     y_done(0)
     add_rows(sums.at[3], 0, half, [y_in.at[0, 3], y_in.at[0, 4]])
-    go(x_copy(0))
+    go(("x", 0), x_copy(0))
     add_rows(sums.at[3], half, half, [y_in.at[0, 2], y_in.at[0, 5]])
-    go(x_copy(1))
+    go(("x", 1), x_copy(1))
+    drained(("y", 0, 4))
+    drained(("y", 0, 5))
+    y_go(1, 2)
+    y_go(1, 3)
+    lag_step(2)
     tp_halves(1)
     y_pass(1)
-    lag_step(3)
-    tp_direct(1)
-    tp_last(1)
     for side in range(2):
         x_copy(side).wait_recv()
-        go(x_forward(side))
+        go(("x", 2 + side), x_forward(side))
+    tp_last(1)
+    tp_direct(1)
+    lag_step(3)
     layer_finish()
     input_finish()
     x_forward(0).wait_recv()
@@ -701,7 +718,7 @@
     last(half, [y_in.at[1, 2], y_in.at[1, 5], x_in.at[1]])
     for index in range(4, 8):
         sib_copy(index).wait_send()
-    for copy in sends:
+    for copy in sends.values():
         copy.wait_send()
 
 
@@ -754,21 +771,54 @@
     )(hidden, cot, gain, lags, acts, turned, in_weight, out_weight, norms, cots)
 
 
+def place_kernel(
+    layer, grad, kinds, outer, lags, layer_to, grad_to, kinds_to, outer_to, short_to, inner_to,
+    layer_at, grad_at, kinds_at, outer_at, sems,
+):
+    pairs = ((kinds, kinds_at, kinds_to), (layer, layer_at, layer_to), (grad, grad_at, grad_to), (outer, outer_at, outer_to))
+    reads = [pltpu.make_async_copy(pair[0], pair[1], sems.at[0, index]) for index, pair in enumerate(pairs)]
+    writes = [pltpu.make_async_copy(pair[1], pair[2], sems.at[1, index]) for index, pair in enumerate(pairs)]
+    for copy in reads:
+        copy.start()
+    for lag in range(3):
+        short_to[lag] = lags[pl.ds(3 * lag, 3), :]
+    inner_to[...] = lags[pl.ds(9, 7), :]
+    for read, write in zip(reads, writes):
+        read.wait()
+        write.start()
+    for copy in writes:
+        copy.wait()
+
+
+def placed_results(layer, grad, kinds, outer, lags):
+    chans = lags.shape[1]
+    any_space = pl.BlockSpec(memory_space=pl.ANY)
+    vmem_space = pl.BlockSpec(memory_space=pltpu.VMEM)
+    arrays = (layer, grad, kinds, outer)
+    return pl.pallas_call(
+        place_kernel,
+        out_shape=tuple(jax.ShapeDtypeStruct(array.shape, array.dtype) for array in arrays)
+        + (jax.ShapeDtypeStruct((3, 3, chans), jnp.float32), jax.ShapeDtypeStruct((7, chans), jnp.float32)),
+        in_specs=[any_space] * 4 + [vmem_space],
+        out_specs=(any_space,) * 4 + (vmem_space,) * 2,
+        scratch_shapes=[pltpu.VMEM(array.shape, array.dtype) for array in arrays] + [pltpu.SemaphoreType.DMA((2, 4))],
+        compiler_params=pltpu.CompilerParams(vmem_limit_bytes=60 * 2**20),
+        name="place_results",
+    )(layer, grad, kinds, outer, lags)
+
+
 def local(hidden_in, cotangent, norm_gain, in_weight, filter_taps, inner_taps, out_weight):
-    channels = in_weight.shape[2]
     tokens = hidden_in.shape[0] * lax.axis_size("tp")
     scale = (tokens * lax.axis_size("ctx")) ** (-0.5)
     gain = norm_gain.reshape(1, -1)
-    taps = jnp.concatenate([filter_taps.reshape(9, channels), inner_taps])
     kinds = jnp.transpose(in_weight, (1, 0, 2))
     norms, cots, acts, turned, lags = gathered(
-        hidden_in, cotangent, gain, taps, kinds, out_weight, tokens, scale
+        hidden_in, cotangent, gain, filter_taps, inner_taps, kinds, out_weight, tokens, scale
     )
-    layer_out, grad_input, grad_kinds, grad_out_weight, lags = reduced(
-        hidden_in, cotangent, gain, lags, acts, turned, kinds, out_weight, norms, cots, scale
+    layer_out, grad_input, grad_kinds, grad_out_weight, grad_filter, grad_inner = placed_results(
+        *reduced(hidden_in, cotangent, gain, lags, acts, turned, kinds, out_weight, norms, cots, scale)
     )
-    grad_in_weight = jnp.transpose(grad_kinds, (1, 0, 2))
-    return (layer_out, grad_input, grad_in_weight, grad_out_weight, lags[:9].reshape(3, 3, channels), lags[9:])
+    return (layer_out, grad_input, jnp.transpose(grad_kinds, (1, 0, 2)), grad_out_weight, grad_filter, grad_inner)
 
 
 def solution(mesh):

time: 214 us -> 176 us (0.82)
  Pallas kernels: 200 us -> 174 us
  local copies, waits for them, and re-layouts: 10.9 us -> 0 us
    pallas_call x1, Pallas kernels: 96.2 us -> 77.7 us  [gathered(): pl.pallas_call(body, out_shape=(jax.ShapeDtypeStruct((tokens, width), bf1...]
    pallas_call x1, Pallas kernels: 104 us -> 92.7 us  [reduced(): pl.pallas_call(body, out_shape=(jax.ShapeDtypeStruct((block, width), bf16...]
    unnamed x4 -> x0, local copies, waits for them, and re-layouts: 7.47 us -> none
    pallas_call x0 -> x1, Pallas kernels: none -> 3.88 us  [placed_results(): pl.pallas_call(place_kernel, out_shape=tuple((jax.ShapeDtypeStruct(array....]
where the time goes in v3:
time: 176 us; the launch traced here: 175 us
  Pallas kernels  174 us (99%)
    pallas_call x1, Pallas kernels, reduced(): pl.pallas_call(body, out_shape=(jax.ShapeDtypeStruct((block, width), bf16...  92.7 us
    pallas_call x1, Pallas kernels, gathered(): pl.pallas_call(body, out_shape=(jax.ShapeDtypeStruct((tokens, width), bf1...  77.7 us
    pallas_call x1, Pallas kernels, placed_results(): pl.pallas_call(place_kernel, out_shape=tuple((jax.ShapeDtypeStruct(array....  3.88 us

profile of v3, /device:TPU:0, one launch (start us, length us, event | category | flops | bytes accessed | tf_op | source)
XLA Modules:
  0.0 175.1 jit_solution(1809955491824987982)
XLA Ops:
  0.6 77.7 %gather_all.1 = (bf16[512,4096]{1,0:T(8,128)(2,1)}, bf16[512,4096]{1,0:T(8,128)(2,1)}, bf16[512,2048]{1,0:T(8,128)(2,1)}, bf16[2048,512]{1,0:T(8,128)(2,1)}, f32[16,512]{1,0:T(8,128)}) custom-call(bf16[64,4096]{1,0:T(8,128)(2,1)} %refs_0_.3, bf16[64,4096]{1,0:T(8,128)(2,1)} %refs_1_.3, f32[1,4096]{1,0:T(1,128)} %bitcast.5, f32[3,3,512]{2,1,0:T(4,128)} %refs_3_.1, ...), custom_call_target="tpu_custom_call" | custom-call | tf_op jit(solution)/shard_map/gather_all/pallas_call | solution.py:324
  78.3 92.7 %reduce_all.1 = (bf16[64,4096]{1,0:T(8,128)(2,1)}, bf16[64,4096]{1,0:T(8,128)(2,1)}, bf16[3,256,512]{2,1,0:T(8,128)(2,1)}, bf16[512,256]{1,0:T(8,128)(2,1)}, f32[16,512]{1,0:T(8,128)}) custom-call(bf16[64,4096]{1,0:T(8,128)(2,1)} %refs_0_.3, bf16[64,4096]{1,0:T(8,128)(2,1)} %refs_1_.3, f32[1,4096]{1,0:T(1,128)} %bitcast.6, ...), custom_call_target="tpu_custom_call" | custom-call | tf_op jit(solution)/shard_map/reduce_all/pallas_call | solution.py:737
  171.1 3.9 %place_results.1 = (bf16[64,4096]{1,0:T(8,128)(2,1)}, bf16[64,4096]{1,0:T(8,128)(2,1)}, bf16[3,256,512]{2,1,0:T(8,128)(2,1)}, bf16[512,256]{1,0:T(8,128)(2,1)}, f32[3,3,512]{2,1,0:T(4,128)}, /*index=5*/f32[7,512]{1,0:T(8,128)}) custom-call(bf16[64,4096]{1,0:T(8,128)(2,1)} %get-tuple-element.27.layer, bf16[64,4096]{1,0:T(8,128)(2,1)} %get-tuple-element.28.grad, ...), custom_call_target="tpu_custom_call" | custom-call | tf_op jit(solution)/shard_map/place_results/pallas_call | solution.py:798

commit v4 on v0

v4 whole, which is shorter than its diff:
```python
import jax
import jax.numpy as jnp
from jax import lax
from jax.experimental import pallas as pl
from jax.experimental.pallas import tpu as pltpu
from jax.sharding import PartitionSpec as P

MESH = pl.DeviceIdType.MESH
DELTAS = (2, 1, 3, 0)


class Place:
    def __init__(self):
        ctx, tp = lax.axis_index("ctx"), lax.axis_index("tp")
        self.y, self.x_hi, self.core = ctx // 4, (ctx // 2) % 2, ctx % 2
        self.z, self.x_lo = tp // 2, tp % 2
        self.ctx, self.tp = ctx, tp

    def sibling(self):
        return (self.y * 4 + self.x_hi * 2 + 1 - self.core, self.tp)

    def along_y(self, step):
        return (((self.y + step) % 4) * 4 + self.x_hi * 2 + self.core, self.tp)

    def along_z(self, step):
        return (self.ctx, ((self.z + step) % 4) * 2 + self.x_lo)

    def along_x(self, step):
        x = (self.x_hi * 2 + self.x_lo + step) % 4
        return (self.y * 4 + (x // 2) * 2 + self.core, self.z * 2 + x % 2)

    def along_ctx(self, step):
        return ((self.ctx + step) % 16, self.tp)

    def partner(self):
        return (self.ctx, self.z * 2 + 1 - self.x_lo)

    def block(self, step, same):
        x_lo = self.x_lo if same else 1 - self.x_lo
        return ((self.z + step) % 4) * 2 + x_lo


def remote(source, target, send, recv, device):
    return pltpu.make_async_remote_copy(
        src_ref=source, dst_ref=target, send_sem=send, recv_sem=recv, device_id=device, device_id_type=MESH
    )


def tile(index, size):
    return pl.ds(pl.multiple_of(index * size, size), size)


def layer_kernel(
    scale, tokens,
    hidden, cot, gain, short_taps, inner_taps, in_w_hbm, out_w_hbm,
    layer_ref, input_ref, in_grad_ref, out_grad_ref, lag_ref,
    both, out_w, proj, edges, lags, acts, turned, part,
    sums_out, sums_in, y_out, y_in, pass_out, pass_in, x_out, x_in, tp_in, lag_sum, lag_got,
    load_sem, in_w_sem, send_sem, recv_sem, edge_send, edge_recv,
    sib_send, sib_recv, y_send, y_recv, x_send, x_recv, tp_send, tp_recv, lag_send, lag_recv,
):
    here = Place()
    block, width = hidden.shape
    chans = out_w_hbm.shape[0]
    cut = width // 16
    half = block // 2
    group = 2 * block
    wide, span = 72, 64
    steps = chans // 128
    bands = tokens // span
    step_in = 512
    bf16, f32 = jnp.bfloat16, jnp.float32

    out_load = pltpu.make_async_copy(out_w_hbm, out_w, load_sem.at[3])
    barrier = pltpu.get_barrier_semaphore()
    devices = [
        here.sibling(), here.along_y(1), here.along_y(-1), here.along_y(2), here.along_z(1), here.along_z(-1),
        here.along_x(1), here.along_x(-1), here.along_x(2), here.along_ctx(1), here.along_ctx(-1),
    ]
    for device in devices:
        pl.semaphore_signal(barrier, inc=1, device_id=device, device_id_type=MESH)

    sends = {}

    def go(name, build):
        build().start()
        sends[name] = build

    def drained(name):
        sends.pop(name)().wait_send()


    def rows_of(step, same, begin=0, size=block):
        return pl.ds(pl.multiple_of(here.block(step, same) * block + begin, size), size)

    def gather_copy(which, slot):
        rows, device = (
            lambda: (rows_of(0, True), here.partner()),
            lambda: (rows_of(0, True), here.along_z(1)),
            lambda: (rows_of(0, True), here.along_z(-1)),
            lambda: (rows_of(0, False), here.along_z(1)),
            lambda: (rows_of(0, False), here.along_z(-1)),
            lambda: (rows_of(-1, True, 0, half), here.along_z(1)),
            lambda: (rows_of(1, True, half, half), here.along_z(-1)),
            lambda: (rows_of(2, True), here.partner()),
        )[slot]()
        held = both.at[which, rows]
        return remote(held, held, send_sem.at[which, slot], recv_sem.at[which, slot], device)

    def gather(which, slot):
        go(("gather", which, slot), lambda: gather_copy(which, slot))

    def arrived(which, slot):
        rows = (
            lambda: rows_of(0, False),
            lambda: rows_of(-1, True),
            lambda: rows_of(1, True),
            lambda: rows_of(-1, False),
            lambda: rows_of(1, False),
            lambda: rows_of(2, True, 0, half),
            lambda: rows_of(2, True, half, half),
            lambda: rows_of(2, False),
        )[slot]()
        held = both.at[which, rows]
        remote(held, held, send_sem.at[which, slot], recv_sem.at[which, slot], here.partner()).wait_recv()


    parts = (part, out_w)

    def tp_copy(which, slot):
        source, held = parts[which], tp_in.at[which]
        first = pl.ds(0, half)
        second = pl.ds(half, half)
        rows, place, device = (
            lambda: (rows_of(2, False), held.at[0], here.partner()),
            lambda: (rows_of(1, False), held.at[1], here.along_z(1)),
            lambda: (rows_of(-1, False), held.at[2], here.along_z(-1)),
            lambda: (rows_of(2, True, 0, half), held.at[3, first], here.along_z(1)),
            lambda: (rows_of(2, True, half, half), held.at[3, second], here.along_z(-1)),
            lambda: (rows_of(1, True), held.at[4], here.along_z(1)),
            lambda: (rows_of(-1, True), held.at[5], here.along_z(-1)),
            lambda: (rows_of(0, False), held.at[6], here.partner()),
        )[slot]()
        return remote(source.at[rows], place, tp_send.at[which, slot], tp_recv.at[which, slot], device)

    def tp_go(which, slot):
        go(("tp", which, slot), lambda: tp_copy(which, slot))

    def add_rows(ref, base, length, others, size=128):
        def loop(index, carry):
            at = tile(index, size)
            rows = pl.ds(pl.multiple_of(base + index * size, size), size)
            total = ref[rows, :].astype(f32)
            for other in others:
                total = total + other[at, :].astype(f32)
            ref[rows, :] = total.astype(bf16)
            return carry

        lax.fori_loop(0, length // size, loop, 0)

    def tp_begin(which):
        for slot in range(3):
            tp_go(which, slot)

    def tp_halves(which):
        tp_copy(which, 0).wait_recv()
        add_rows(parts[which], here.block(2, True) * block, block, [tp_in.at[which, 0]], 16)
        tp_go(which, 3)
        tp_go(which, 4)

    def tp_direct(which):
        tp_copy(which, 3).wait_recv()
        add_rows(parts[which], here.block(1, True) * block, half, [tp_in.at[which, 3, pl.ds(0, half)]], 16)
        tp_go(which, 5)
        tp_copy(which, 4).wait_recv()
        add_rows(
            parts[which], here.block(-1, True) * block + half, half, [tp_in.at[which, 3, pl.ds(half, half)]], 16)
        tp_go(which, 6)

    def tp_last(which):
        tp_copy(which, 1).wait_recv()
        tp_copy(which, 2).wait_recv()
        add_rows(parts[which], here.block(0, False) * block, block, [tp_in.at[which, 1], tp_in.at[which, 2]], 16)
        tp_go(which, 7)

    def tp_total(which, index):
        at = tile(index, 16)
        rows = pl.ds(pl.multiple_of(here.tp * block + index * 16, 16), 16)
        total = parts[which][rows, :].astype(f32)
        for slot in (4, 5, 6):
            total = total + tp_in[which, slot, at, :].astype(f32)
        return at, total


    sums = (sums_out, sums_in)
    arriving = (y_out, y_in)
    passing = (pass_out, pass_in)
    crossing = (x_out, x_in)

    def halves(kind):
        size = sums[kind].shape[1] // 2
        return pl.ds(0, size), pl.ds(size, size), size

    def target(index, core):
        y = (here.y + DELTAS[index % 4]) % 4
        x_hi = 1 - here.x_hi if index < 4 else here.x_hi
        return y * 4 + x_hi * 2 + core

    def product(kind, index, core, write):
        cols = tile(target(index, core), cut)

        def one(step, carry):
            rows = tile(step, chans)
            first = 3 * chans if kind == 0 else 0
            left = turned[pl.ds(pl.multiple_of(first + step * chans, chans), chans), :]
            value = jnp.dot(left, both[1 - kind, :, cols], preferred_element_type=f32)
            write(rows, value * scale)
            return carry

        lax.fori_loop(0, (1, 3)[kind], one, 0)

    def sib_copy(kind, sib, index):
        return remote(
            sib.at[index % 4], sums[kind].at[index], sib_send.at[kind, index], sib_recv.at[kind, index],
            here.sibling())

    def for_sibling(kind, sib, index):
        if index >= 4:
            drained(("sib", kind, index - 4))

        def write(rows, value):
            sib[index % 4, rows, :] = value.astype(bf16)

        product(kind, index, 1 - here.core, write)
        go(("sib", kind, index), lambda: sib_copy(kind, sib, index))

    def for_self(kind, sib, index):
        sib_copy(kind, sib, index).wait_recv()

        def write(rows, value):
            held = sums[kind][index, rows, :].astype(f32)
            sums[kind][index, rows, :] = (held + value).astype(bf16)

        product(kind, index, here.core, write)

    def y_copy(kind, far, slot):
        upper, lower, _ = halves(kind)
        index, rows, step = (
            (0, upper, 1), (0, lower, -1), (1, lower, 1), (2, upper, -1), (1, upper, 1), (2, lower, -1)
        )[slot]
        return remote(
            sums[kind].at[far * 4 + index, rows], arriving[kind].at[far, slot],
            y_send.at[kind, far, slot], y_recv.at[kind, far, slot], here.along_y(step),
        )

    def y_go(kind, far, slot):
        go(("y", kind, far, slot), lambda: y_copy(kind, far, slot))

    def y_pass(kind, far):
        size = halves(kind)[2]
        y_copy(kind, far, 0).wait_recv()
        add_rows(sums[kind].at[far * 4 + 1], 0, size, [arriving[kind].at[far, 0]])
        y_go(kind, far, 4)
        y_copy(kind, far, 1).wait_recv()
        add_rows(sums[kind].at[far * 4 + 2], size, size, [arriving[kind].at[far, 1]])
        y_go(kind, far, 5)

    def y_done(kind, far):
        for slot in (3, 4, 2, 5):
            y_copy(kind, far, slot).wait_recv()

    def x_copy(kind, side):
        rows = halves(kind)[side]
        return remote(
            sums[kind].at[3, rows], passing[kind].at[side], x_send.at[kind, side], x_recv.at[kind, side],
            here.along_x((1, -1)[side]))

    def x_forward(kind, side):
        return remote(
            passing[kind].at[side], crossing[kind].at[side], x_send.at[kind, 2 + side], x_recv.at[kind, 2 + side],
            here.along_x((1, -1)[side]))

    def x_begin(kind):
        size = halves(kind)[2]
        y_done(kind, 0)
        add_rows(sums[kind].at[3], 0, size, [arriving[kind].at[0, 3], arriving[kind].at[0, 4]])
        go(("x", kind, 0), lambda: x_copy(kind, 0))
        add_rows(sums[kind].at[3], size, size, [arriving[kind].at[0, 2], arriving[kind].at[0, 5]])
        go(("x", kind, 1), lambda: x_copy(kind, 1))

    def x_go(kind, side):
        go(("x", kind, 2 + side), lambda: x_forward(kind, side))

    def x_on(kind):
        for side in range(2):
            x_copy(kind, side).wait_recv()
            x_go(kind, side)

    def last(kind, side):
        size = halves(kind)[2]
        begin = side * size
        others = [arriving[kind].at[1, slot] for slot in ((3, 4), (2, 5))[side]] + [crossing[kind].at[side]]
        for index in range(size // 128):
            row = begin + index * 128
            total = sums[kind][7, pl.ds(row, 128), :].astype(f32)
            for other in others:
                total = total + other[pl.ds(index * 128, 128), :].astype(f32)
            if kind == 1:
                in_grad_ref[row // chans, :, pl.ds(row % chans, 128)] = total.T.astype(bf16)
            else:
                out_grad_ref[pl.ds(row, 128), :] = total.astype(bf16)

    def lag_copy(step):
        device = (
            lambda: here.sibling(),
            lambda: here.along_x(2),
            lambda: here.along_y(1 - 2 * (here.y % 2)),
            lambda: here.along_y(2),
        )[step]()
        return remote(lag_sum.at[step], lag_got.at[step], lag_send.at[step], lag_recv.at[step], device)

    def lag_step(step):
        lag_copy(step).wait_recv()
        total = lag_sum[step] + lag_got[step]
        if step < 3:
            lag_sum[step + 1] = total
            go(("lag", step + 1), lambda: lag_copy(step + 1))
        else:
            lag_ref[...] = total

    def gather_phase(in_w):
        loads = [pltpu.make_async_copy(in_w_hbm.at[kind], in_w.at[kind], load_sem.at[kind]) for kind in range(3)]
        for copy in loads:
            copy.start()
        out_load.start()

        def normalise(index, carry):
            at = tile(index, 16)
            rows = pl.ds(pl.multiple_of(here.tp * block + index * 16, 16), 16)
            floats = hidden[at, :].astype(f32)
            factor = lax.rsqrt(jnp.mean(floats * floats, axis=-1, keepdims=True) + 1e-05)
            both[0, rows, :] = (floats * factor * gain[...]).astype(bf16)
            both[1, rows, :] = cot[at, :]
            return carry

        lax.fori_loop(0, block // 16, normalise, 0)
        pl.semaphore_wait(barrier, len(devices))

        def project(step):
            begin = ((here.z + step) % 4) * group

            def loop(kind, carry):
                value = jnp.dot(
                    both[0, pl.ds(pl.multiple_of(begin, group), group), :], in_w[kind], preferred_element_type=f32
                )
                proj[kind, pl.ds(pl.multiple_of(8 + begin, 8), group), :] = value.astype(bf16).astype(f32)
                return carry

            lax.fori_loop(0, 3, loop, 0)

        for slot in range(3):
            gather(0, slot)
        arrived(0, 1)
        gather(0, 5)
        arrived(0, 2)
        gather(0, 6)
        arrived(0, 0)
        gather(0, 3)
        gather(0, 4)
        for slot in range(3):
            gather(1, slot)
        for copy in loads:
            copy.wait()
        project(0)
        arrived(0, 5)
        arrived(0, 6)
        gather(0, 7)
        arrived(0, 3)
        project(-1)
        arrived(0, 4)
        project(1)
        arrived(1, 1)
        gather(1, 5)
        arrived(1, 2)
        gather(1, 6)
        arrived(0, 7)
        project(2)

    def filter_phase(query, gates, prods, grads, sib):
        def edge_copy():
            return remote(
                proj.at[:, pl.ds(tokens, 8), :], proj.at[:, pl.ds(0, 8), :], edge_send.at[0], edge_recv.at[0],
                here.along_ctx(1))

        def front_copy(which):
            first = pl.ds((0, 2)[which], 2)
            return remote(
                grads.at[first, pl.ds(0, 8), :], edges.at[first], edge_send.at[1 + which], edge_recv.at[1 + which],
                here.along_ctx(-1))

        go(("edge", 0), edge_copy)
        arrived(1, 0)
        gather(1, 3)
        gather(1, 4)
        arrived(1, 5)
        arrived(1, 6)
        gather(1, 7)

        def short(lag, kind, cols):
            return short_taps[lag, pl.ds(kind, 1), cols]

        def inner(lag, cols):
            return inner_taps[pl.ds(lag, 1), cols]

        def behind(value, count):
            return pltpu.roll(value, count, 0)

        def ahead(value, count):
            return pltpu.roll(value, wide - count, 0)

        def forward(index, carry):
            begin = pl.multiple_of((index // steps) * span, span)
            cols = tile(index % steps, 128)
            feats = []
            for kind in range(3):
                held = proj[kind, pl.ds(begin, wide), cols]
                total = short(0, kind, cols) * held
                for lag in (1, 2):
                    total = total + short(lag, kind, cols) * behind(held, lag)
                feats.append(total)
            product = feats[1] * feats[2]
            total = inner(0, cols) * product
            for lag in range(1, 7):
                total = total + inner(lag, cols) * behind(product, lag)
            rows = pl.ds(begin, span)
            query[rows, cols] = feats[0][8:]
            grads[3, rows, cols] = feats[1][8:]
            grads[2, rows, cols] = feats[2][8:]
            gates[rows, cols] = total[8:]
            prods[rows, cols] = product[8:]
            acts[rows, tile(3 * steps + index % steps, 128)] = (feats[0][8:] * total[8:]).astype(bf16)
            return carry

        lax.fori_loop(steps, bands * steps, forward, 0)
        edge_copy().wait_recv()

        @pl.when(here.ctx == 0)
        def _():
            proj[:, pl.ds(0, 8), :] = jnp.zeros((3, 8, chans), f32)

        lax.fori_loop(0, steps, forward, 0)
        go(("edge", 1), lambda: front_copy(1))
        lags[...] = jnp.zeros_like(lags)

        def turn(index, carry):
            turned[tile(index, 128), :] = acts[:, tile(index, 128)].T
            return carry

        lax.fori_loop(3 * steps, 4 * steps, turn, 0)
        out_load.wait()

        def branch_product(index, carry):
            cols = tile(index, chans)
            value = jnp.dot(acts[:, pl.ds(3 * chans, chans)], out_w[:, cols], preferred_element_type=f32)
            part[:, cols] = value.astype(bf16)
            return carry

        lax.fori_loop(0, width // chans, branch_product, 0)

        def grade(step):
            rows = pl.ds(pl.multiple_of(((here.z + step) % 4) * group, group), group)
            value = lax.dot_general(
                both[1, rows, :], out_w[...], (((1,), (1,)), ((), ())), preferred_element_type=f32
            )
            grads[0, rows, :] = value * query[rows, :]
            grads[1, rows, :] = value * gates[rows, :]

        grade(0)
        arrived(1, 3)
        arrived(1, 4)
        arrived(1, 7)
        tp_begin(0)
        for_sibling(0, sib, 0)
        for_sibling(0, sib, 1)
        for_sibling(0, sib, 2)
        for_self(0, sib, 0)
        y_go(0, 0, 0)
        y_go(0, 0, 1)
        for_sibling(0, sib, 3)
        for_self(0, sib, 1)
        y_go(0, 0, 2)
        for_self(0, sib, 2)
        y_go(0, 0, 3)
        grade(-1)
        grade(1)
        grade(2)
        go(("edge", 2), lambda: front_copy(0))
        y_pass(0, 0)
        for index in range(4, 8):
            for_sibling(0, sib, index)
            for_self(0, sib, index - 1)
            if index == 5:
                y_go(0, 1, 0)
                y_go(0, 1, 1)
            if index == 6:
                y_go(0, 1, 2)
            if index == 7:
                y_go(0, 1, 3)
        for_self(0, sib, 7)

        def backward(index, carry):
            begin = pl.multiple_of((index // steps) * span, span)
            cols = tile(index % steps, 128)
            rows = pl.ds(begin, wide)
            here_rows = pl.ds(begin, span)

            def add_lag(row, value):
                lags[row, :, cols] += jnp.sum(value.reshape(span // 8, 8, 128), axis=0)

            gated = grads[0, rows, cols]
            product = prods[here_rows, cols]
            total = inner(0, cols) * gated
            add_lag(9, gated[:span] * product)
            for lag in range(1, 7):
                moved = ahead(gated, lag)
                total = total + inner(lag, cols) * moved
                add_lag(9 + lag, moved[:span] * product)
            feats = (grads[1, rows, cols], total * grads[2, rows, cols], total * grads[3, rows, cols])
            for kind in range(3):
                feat = feats[kind]
                held = proj[kind, pl.ds(pl.multiple_of(begin + 8, 8), span), cols]
                summed = short(0, kind, cols) * feat[:span]
                add_lag(kind, feat[:span] * held)
                for lag in (1, 2):
                    moved = ahead(feat, lag)[:span]
                    summed = summed + short(lag, kind, cols) * moved
                    add_lag(lag * 3 + kind, moved * held)
                acts[here_rows, tile(kind * steps + index % steps, 128)] = summed.astype(bf16)
            return carry

        lax.fori_loop(0, (bands - 1) * steps, backward, 0)
        front_copy(1).wait_recv()
        front_copy(0).wait_recv()
        grads[:, pl.ds(tokens, 8), :] = edges[...]

        @pl.when(here.ctx == 15)
        def _():
            grads[pl.ds(0, 2), pl.ds(tokens, 8), :] = jnp.zeros((2, 8, chans), f32)

        lax.fori_loop((bands - 1) * steps, bands * steps, backward, 0)
        lax.fori_loop(0, 3 * steps, turn, 0)
        lag_sum[0] = jnp.sum(lags[...], axis=1) * scale
        go(("lag", 0), lambda: lag_copy(0))
        y_pass(0, 1)
        x_begin(0)
        for index in range(3):
            drained(("edge", index))
        for index in range(4, 8):
            drained(("sib", 0, index))

    def reduce_phase(in_w, sib):
        def in_load(step, slot):
            return pltpu.make_async_copy(in_w_hbm.at[:, tile(step, step_in), :], in_w.at[slot], in_w_sem.at[slot])

        in_load(0, 0).start()
        in_load(1, 1).start()

        def gnorm_product():
            def loop(step, carry):
                slot = step % 2
                in_load(step, slot).wait()
                value = jnp.zeros((tokens, step_in), f32)
                for kind in range(3):
                    value = value + lax.dot_general(
                        acts[:, pl.ds(kind * chans, chans)], in_w[slot, kind],
                        (((1,), (1,)), ((), ())), preferred_element_type=f32,
                    )
                out_w[:, tile(step, step_in)] = value.astype(bf16)

                @pl.when(step + 2 < width // step_in)
                def _():
                    in_load(step + 2, slot).start()

                return carry

            lax.fori_loop(0, width // step_in, loop, 0)

        for_sibling(1, sib, 0)
        for_sibling(1, sib, 1)
        for_self(1, sib, 0)
        y_go(1, 0, 0)
        y_go(1, 0, 1)
        tp_halves(0)
        tp_last(0)
        for_sibling(1, sib, 2)
        for_self(1, sib, 1)
        y_go(1, 0, 2)
        for_sibling(1, sib, 3)
        for_self(1, sib, 2)
        y_go(1, 0, 3)
        lag_step(0)
        x_on(0)
        tp_direct(0)
        gnorm_product()
        tp_begin(1)
        y_pass(1, 0)
        lag_step(1)
        for index in range(4, 8):
            for_sibling(1, sib, index)
            for_self(1, sib, index - 1)
        for_self(1, sib, 7)
        for slot in range(4):
            drained(("y", 1, 0, slot))
        y_go(1, 1, 0)
        y_go(1, 1, 1)
        tp_halves(1)
        lag_step(2)
        x_begin(1)
        drained(("y", 1, 0, 4))
        drained(("y", 1, 0, 5))
        y_go(1, 1, 2)
        y_go(1, 1, 3)
        for slot in (5, 6, 7):
            tp_copy(0, slot).wait_recv()

        def layer_finish(index, carry):
            at, total = tp_total(0, index)
            layer_ref[at, :] = (hidden[at, :].astype(f32) + total).astype(bf16)
            return carry

        lax.fori_loop(0, block // 16, layer_finish, 0)
        for side in range(2):
            x_forward(0, side).wait_recv()
        y_done(0, 1)
        last(0, 0)
        last(0, 1)
        lag_step(3)
        y_pass(1, 1)
        x_on(1)
        tp_last(1)
        tp_direct(1)
        for slot in (5, 6, 7):
            tp_copy(1, slot).wait_recv()

        def input_finish(index, carry):
            at, total = tp_total(1, index)
            floats = hidden[at, :].astype(f32)
            factor = lax.rsqrt(jnp.mean(floats * floats, axis=-1, keepdims=True) + 1e-05)
            gained = total * gain[...]
            inner = jnp.mean(floats * gained, axis=-1, keepdims=True) * factor * factor * factor
            input_ref[at, :] = (cot[at, :].astype(f32) + gained * factor - floats * inner).astype(bf16)
            return carry

        lax.fori_loop(0, block // 16, input_finish, 0)
        for side in range(2):
            x_forward(1, side).wait_recv()
        y_done(1, 1)
        last(1, 0)
        last(1, 1)
        for name in list(sends):
            drained(name)

    pl.run_scoped(gather_phase, pltpu.VMEM((3, width, chans), bf16))
    pl.run_scoped(
        filter_phase,
        pltpu.VMEM((tokens, chans), f32),
        pltpu.VMEM((tokens, chans), f32),
        pltpu.VMEM((tokens, chans), f32),
        pltpu.VMEM((4, tokens + 8, chans), f32),
        pltpu.VMEM((4, chans, cut), bf16),
    )
    pl.run_scoped(
        reduce_phase, pltpu.VMEM((2, 3, step_in, chans), bf16), pltpu.VMEM((4, 3 * chans, cut), bf16)
    )


def layer_results(hidden, cot, gain, short_taps, inner_taps, in_weight, out_weight, tokens, scale):
    block, width = hidden.shape
    chans = out_weight.shape[0]
    cut = width // 16
    any_space = pl.BlockSpec(memory_space=pl.ANY)
    vmem_space = pl.BlockSpec(memory_space=pltpu.VMEM)
    bf16, f32 = jnp.bfloat16, jnp.float32
    dma = pltpu.SemaphoreType.DMA
    body = lambda *refs: layer_kernel(scale, tokens, *refs)
    return pl.pallas_call(
        body,
        out_shape=(
            jax.ShapeDtypeStruct((block, width), bf16),
            jax.ShapeDtypeStruct((block, width), bf16),
            jax.ShapeDtypeStruct((3, cut, chans), bf16),
            jax.ShapeDtypeStruct((chans, cut), bf16),
            jax.ShapeDtypeStruct((16, chans), f32),
        ),
        in_specs=[vmem_space] * 5 + [any_space] * 2,
        out_specs=(vmem_space,) * 5,
        scratch_shapes=[
            pltpu.VMEM((2, tokens, width), bf16),
            pltpu.VMEM(out_weight.shape, bf16),
            pltpu.VMEM((3, tokens + 8, chans), f32),
            pltpu.VMEM((4, 8, chans), f32),
            pltpu.VMEM((16, 8, chans), f32),
            pltpu.VMEM((tokens, 4 * chans), bf16),
            pltpu.VMEM((4 * chans, tokens), bf16),
            pltpu.VMEM((tokens, width), bf16),
            pltpu.VMEM((8, chans, cut), bf16),
            pltpu.VMEM((8, 3 * chans, cut), bf16),
            pltpu.VMEM((2, 6, chans // 2, cut), bf16),
            pltpu.VMEM((2, 6, 3 * chans // 2, cut), bf16),
            pltpu.VMEM((2, chans // 2, cut), bf16),
            pltpu.VMEM((2, 3 * chans // 2, cut), bf16),
            pltpu.VMEM((2, chans // 2, cut), bf16),
            pltpu.VMEM((2, 3 * chans // 2, cut), bf16),
            pltpu.VMEM((2, 7, block, width), bf16),
            pltpu.VMEM((4, 16, chans), f32),
            pltpu.VMEM((4, 16, chans), f32),
            dma((4,)), dma((2,)), dma((2, 8)), dma((2, 8)), dma((3,)), dma((3,)),
            dma((2, 8)), dma((2, 8)), dma((2, 2, 6)), dma((2, 2, 6)), dma((2, 4)), dma((2, 4)),
            dma((2, 8)), dma((2, 8)), dma((4,)), dma((4,)),
        ],
        compiler_params=pltpu.CompilerParams(
            collective_id=0, has_side_effects=True, vmem_limit_bytes=63 * 2**20
        ),
        name="whole_layer",
    )(hidden, cot, gain, short_taps, inner_taps, in_weight, out_weight)


def place_kernel(
    layer, grad, kinds, outer, lags, layer_to, grad_to, kinds_to, outer_to, short_to, inner_to,
    layer_at, grad_at, kinds_at, outer_at, sems,
):
    pairs = ((kinds, kinds_at, kinds_to), (layer, layer_at, layer_to), (grad, grad_at, grad_to), (outer, outer_at, outer_to))
    reads = [pltpu.make_async_copy(pair[0], pair[1], sems.at[0, index]) for index, pair in enumerate(pairs)]
    writes = [pltpu.make_async_copy(pair[1], pair[2], sems.at[1, index]) for index, pair in enumerate(pairs)]
    for copy in reads:
        copy.start()
    for lag in range(3):
        short_to[lag] = lags[pl.ds(3 * lag, 3), :]
    inner_to[...] = lags[pl.ds(9, 7), :]
    for read, write in zip(reads, writes):
        read.wait()
        write.start()
    for copy in writes:
        copy.wait()


def placed_results(layer, grad, kinds, outer, lags):
    chans = lags.shape[1]
    any_space = pl.BlockSpec(memory_space=pl.ANY)
    vmem_space = pl.BlockSpec(memory_space=pltpu.VMEM)
    arrays = (layer, grad, kinds, outer)
    return pl.pallas_call(
        place_kernel,
        out_shape=tuple(jax.ShapeDtypeStruct(array.shape, array.dtype) for array in arrays)
        + (jax.ShapeDtypeStruct((3, 3, chans), jnp.float32), jax.ShapeDtypeStruct((7, chans), jnp.float32)),
        in_specs=[any_space] * 4 + [vmem_space],
        out_specs=(any_space,) * 4 + (vmem_space,) * 2,
        scratch_shapes=[pltpu.VMEM(array.shape, array.dtype) for array in arrays] + [pltpu.SemaphoreType.DMA((2, 4))],
        compiler_params=pltpu.CompilerParams(vmem_limit_bytes=60 * 2**20),
        name="place_results",
    )(layer, grad, kinds, outer, lags)


def local(hidden_in, cotangent, norm_gain, in_weight, filter_taps, inner_taps, out_weight):
    tokens = hidden_in.shape[0] * lax.axis_size("tp")
    scale = (tokens * lax.axis_size("ctx")) ** (-0.5)
    gain = norm_gain.reshape(1, -1)
    kinds = jnp.transpose(in_weight, (1, 0, 2))
    layer_out, grad_input, grad_kinds, grad_out_weight, grad_filter, grad_inner = placed_results(
        *layer_results(hidden_in, cotangent, gain, filter_taps, inner_taps, kinds, out_weight, tokens, scale)
    )
    return (layer_out, grad_input, jnp.transpose(grad_kinds, (1, 0, 2)), grad_out_weight, grad_filter, grad_inner)


def solution(mesh):
    placed = (
        P(("ctx", "tp"), None),
        P(("ctx", "tp"), None),
        P(),
        P(None, None, "tp"),
        P(None, None, "tp"),
        P(None, "tp"),
        P("tp", None),
    )
    return jax.shard_map(
        local,
        mesh=mesh,
        in_specs=placed,
        out_specs=(
            P(("ctx", "tp"), None),
            P(("ctx", "tp"), None),
            P("ctx", None, "tp"),
            P("tp", "ctx"),
            P(None, None, "tp"),
            P(None, "tp"),
        ),
        check_vma=False,
    )
```

time: 640 us -> 163 us (0.25)
  waiting for transfers between devices: 428 us -> 0 us
  Pallas kernels: 0 us -> 162 us
  blocking collectives: 71.5 us -> 0 us
  matrix products: 53.6 us -> 0 us
  local copies, waits for them, and re-layouts: 44.7 us -> 0 us
  other arithmetic: 21.1 us -> 0 us
  between operations: 14.4 us -> 0.8 us
    reduce_scatter x4 -> x0, waiting for transfers between devices: 274 us -> none  [the longest x1 126 us: local(): lax.psum_scatter(scaled_in.astype(jnp.bfloat16), 'ctx', scatter_dimension...]
    pallas_call x0 -> x2, Pallas kernels: none -> 162 us  [the longest x1 158 us: layer_results(): pl.pallas_call(body, out_shape=(jax.ShapeDtypeStruct((block, width), bf16...]
    all_gather x2 -> x0, waiting for transfers between devices: 149 us -> none  [the longest x1 75.8 us: local(): gathered = lax.all_gather(normal_rows, 'tp', axis=0, tiled=True)]
    psum x1 -> x0, blocking collectives: 71.5 us -> none  [local(): lax.psum(filter_part.astype(jnp.bfloat16), 'ctx').astype(jnp.float32)]
    dot_general x6 -> x0, matrix products: 53.6 us -> none  [the longest x1 11.5 us: local(): lax.dot_general(gathered, flat_grad, (((0,), (0,)), ((), ())), preferred_...]
    convert_element_type x3 -> x0, local copies, waits for them, and re-layouts: 20.2 us -> none  [the longest x1 16.7 us: local(): scaled_in.astype(jnp.bfloat16)]
    unnamed x21 -> x0, local copies, waits for them, and re-layouts: 18.1 us -> none
  transfers between devices with their start and end apart: 9 -> 0, of which waited for: 7 -> 0; matrix products, arithmetic and copies ran while one was open for 15% -> 0% of each run, Pallas kernels for 0% -> 0%
where the time goes in v4:
time: 163 us
  Pallas kernels  162 us (99%)
    pallas_call x1, Pallas kernels, layer_results(): pl.pallas_call(body, out_shape=(jax.ShapeDtypeStruct((block, width), bf16...  158 us
    pallas_call x1, Pallas kernels, placed_results(): pl.pallas_call(place_kernel, out_shape=tuple((jax.ShapeDtypeStruct(array....  3.88 us

profile of v4, /device:TPU:0, one launch (start us, length us, event | category | flops | bytes accessed | tf_op | source)
XLA Modules:
  0.0 162.5 jit_solution(4059416703972516944)
XLA Ops:
  0.6 157.9 %whole_layer.1 = (bf16[64,4096]{1,0:T(8,128)(2,1)}, bf16[64,4096]{1,0:T(8,128)(2,1)}, bf16[3,256,512]{2,1,0:T(8,128)(2,1)}, bf16[512,256]{1,0:T(8,128)(2,1)}, f32[16,512]{1,0:T(8,128)}) custom-call(bf16[64,4096]{1,0:T(8,128)(2,1)} %refs_0_.1, bf16[64,4096]{1,0:T(8,128)(2,1)} %refs_1_.1, f32[1,4096]{1,0:T(1,128)} %bitcast.4, f32[3,3,512]{2,1,0:T(4,128)} %refs_3_.1, ...), custom_call_target="tpu_custom_call" | custom-call | tf_op jit(solution)/shard_map/whole_layer/pallas_call | solution.py:686
  158.5 3.9 %place_results.1 = (bf16[64,4096]{1,0:T(8,128)(2,1)}, bf16[64,4096]{1,0:T(8,128)(2,1)}, bf16[3,256,512]{2,1,0:T(8,128)(2,1)}, bf16[512,256]{1,0:T(8,128)(2,1)}, f32[3,3,512]{2,1,0:T(4,128)}, /*index=5*/f32[7,512]{1,0:T(8,128)}) custom-call(bf16[64,4096]{1,0:T(8,128)(2,1)} %get-tuple-element.17.layer, bf16[64,4096]{1,0:T(8,128)(2,1)} %get-tuple-element.18.grad, ...), custom_call_target="tpu_custom_call" | custom-call | tf_op jit(solution)/shard_map/place_results/pallas_call | solution.py:752

commit v5 on v4

--- a/solution.py
+++ b/solution.py
@@ -69,6 +69,7 @@
     steps = chans // 128
     bands = tokens // span
     step_in = 512
+    x_cols = (width // 128 * 5 // 32) * 128
     bf16, f32 = jnp.bfloat16, jnp.float32
 
     out_load = pltpu.make_async_copy(out_w_hbm, out_w, load_sem.at[3])
@@ -92,6 +93,11 @@
 
     def rows_of(step, same, begin=0, size=block):
         return pl.ds(pl.multiple_of(here.block(step, same) * block + begin, size), size)
+
+    every = pl.ds(0, width)
+    by_x = pl.ds(0, x_cols)
+    by_z = pl.ds(x_cols, width - x_cols)
+    slot_cols = (every, every, every, by_z, by_z, every, every, every, by_x, by_x)
 
     def gather_copy(which, slot):
         rows, device = (
@@ -103,8 +109,10 @@
             lambda: (rows_of(-1, True, 0, half), here.along_z(1)),
             lambda: (rows_of(1, True, half, half), here.along_z(-1)),
             lambda: (rows_of(2, True), here.partner()),
+            lambda: (rows_of(-1, True), here.partner()),
+            lambda: (rows_of(1, True), here.partner()),
         )[slot]()
-        held = both.at[which, rows]
+        held = both.at[which, rows, slot_cols[slot]]
         return remote(held, held, send_sem.at[which, slot], recv_sem.at[which, slot], device)
 
     def gather(which, slot):
@@ -120,8 +128,10 @@
             lambda: rows_of(2, True, 0, half),
             lambda: rows_of(2, True, half, half),
             lambda: rows_of(2, False),
+            lambda: rows_of(-1, False),
+            lambda: rows_of(1, False),
         )[slot]()
-        held = both.at[which, rows]
+        held = both.at[which, rows, slot_cols[slot]]
         remote(held, held, send_sem.at[which, slot], recv_sem.at[which, slot], here.partner()).wait_recv()
 
 
@@ -362,8 +372,10 @@
             gather(0, slot)
         arrived(0, 1)
         gather(0, 5)
+        gather(0, 8)
         arrived(0, 2)
         gather(0, 6)
+        gather(0, 9)
         arrived(0, 0)
         gather(0, 3)
         gather(0, 4)
@@ -376,13 +388,17 @@
         arrived(0, 6)
         gather(0, 7)
         arrived(0, 3)
+        arrived(0, 8)
         project(-1)
         arrived(0, 4)
+        arrived(0, 9)
         project(1)
         arrived(1, 1)
         gather(1, 5)
+        gather(1, 8)
         arrived(1, 2)
         gather(1, 6)
+        gather(1, 9)
         arrived(0, 7)
         project(2)
 
@@ -467,18 +483,8 @@
 
         lax.fori_loop(0, width // chans, branch_product, 0)
 
-        def grade(step):
-            rows = pl.ds(pl.multiple_of(((here.z + step) % 4) * group, group), group)
-            value = lax.dot_general(
-                both[1, rows, :], out_w[...], (((1,), (1,)), ((), ())), preferred_element_type=f32
-            )
-            grads[0, rows, :] = value * query[rows, :]
-            grads[1, rows, :] = value * gates[rows, :]
-
-        grade(0)
-        arrived(1, 3)
-        arrived(1, 4)
-        arrived(1, 7)
+        for slot in (3, 4, 7, 8, 9):
+            arrived(1, slot)
         tp_begin(0)
         for_sibling(0, sib, 0)
         for_sibling(0, sib, 1)
@@ -491,9 +497,9 @@
         y_go(0, 0, 2)
         for_self(0, sib, 2)
         y_go(0, 0, 3)
-        grade(-1)
-        grade(1)
-        grade(2)
+        value = lax.dot_general(both[1], out_w[...], (((1,), (1,)), ((), ())), preferred_element_type=f32)
+        grads[0, pl.ds(0, tokens), :] = value * query[...]
+        grads[1, pl.ds(0, tokens), :] = value * gates[...]
         go(("edge", 2), lambda: front_copy(0))
         y_pass(0, 0)
         for index in range(4, 8):
@@ -508,9 +514,21 @@
                 y_go(0, 1, 3)
         for_self(0, sib, 7)
 
+        def turn_tile(index):
+            rows = tile(index // steps, 128)
+            for kind in range(3):
+                cols = tile(kind * steps + index % steps, 128)
+                turned[cols, rows] = acts[rows, cols].T
+
         def backward(index, carry):
-            begin = pl.multiple_of((index // steps) * span, span)
-            cols = tile(index % steps, 128)
+            turn_tile(jnp.maximum(index - 1, 0))
+            for part_of in range(2):
+                backward_band((index // steps) * 2 + part_of, index % steps)
+            return carry
+
+        def backward_band(band, column):
+            begin = pl.multiple_of(band * span, span)
+            cols = tile(column, 128)
             rows = pl.ds(begin, wide)
             here_rows = pl.ds(begin, span)
 
@@ -535,10 +553,11 @@
                     moved = ahead(feat, lag)[:span]
                     summed = summed + short(lag, kind, cols) * moved
                     add_lag(lag * 3 + kind, moved * held)
-                acts[here_rows, tile(kind * steps + index % steps, 128)] = summed.astype(bf16)
-            return carry
-
-        lax.fori_loop(0, (bands - 1) * steps, backward, 0)
+                acts[here_rows, tile(kind * steps + column, 128)] = summed.astype(bf16)
+
+        tiles = (bands // 2) * steps
+        lax.fori_loop(0, tiles - steps, backward, 0)
+        y_pass(0, 1)
         front_copy(1).wait_recv()
         front_copy(0).wait_recv()
         grads[:, pl.ds(tokens, 8), :] = edges[...]
@@ -547,11 +566,10 @@
         def _():
             grads[pl.ds(0, 2), pl.ds(tokens, 8), :] = jnp.zeros((2, 8, chans), f32)
 
-        lax.fori_loop((bands - 1) * steps, bands * steps, backward, 0)
-        lax.fori_loop(0, 3 * steps, turn, 0)
+        lax.fori_loop(tiles - steps, tiles, backward, 0)
+        turn_tile(tiles - 1)
         lag_sum[0] = jnp.sum(lags[...], axis=1) * scale
         go(("lag", 0), lambda: lag_copy(0))
-        y_pass(0, 1)
         x_begin(0)
         for index in range(3):
             drained(("edge", index))
@@ -714,7 +732,7 @@
             pltpu.VMEM((2, 7, block, width), bf16),
             pltpu.VMEM((4, 16, chans), f32),
             pltpu.VMEM((4, 16, chans), f32),
-            dma((4,)), dma((2,)), dma((2, 8)), dma((2, 8)), dma((3,)), dma((3,)),
+            dma((4,)), dma((2,)), dma((2, 10)), dma((2, 10)), dma((3,)), dma((3,)),
             dma((2, 8)), dma((2, 8)), dma((2, 2, 6)), dma((2, 2, 6)), dma((2, 4)), dma((2, 4)),
             dma((2, 8)), dma((2, 8)), dma((4,)), dma((4,)),
         ],

time: 163 us -> 165 us (1.012); the launches traced: 163 us -> 163 us
  no operation moved by 1% of the time
where the time goes in v5:
time: 165 us; the launch traced here: 163 us
  Pallas kernels  162 us (98%)
    pallas_call x1, Pallas kernels, layer_results(): pl.pallas_call(body, out_shape=(jax.ShapeDtypeStruct((block, width), bf16...  158 us
    pallas_call x1, Pallas kernels, placed_results(): pl.pallas_call(place_kernel, out_shape=tuple((jax.ShapeDtypeStruct(array....  3.88 us

profile of v5, /device:TPU:0, one launch (start us, length us, event | category | flops | bytes accessed | tf_op | source)
XLA Modules:
  0.0 162.8 jit_solution(1627665571188305916)
XLA Ops:
  0.6 158.2 %whole_layer.1 = (bf16[64,4096]{1,0:T(8,128)(2,1)}, bf16[64,4096]{1,0:T(8,128)(2,1)}, bf16[3,256,512]{2,1,0:T(8,128)(2,1)}, bf16[512,256]{1,0:T(8,128)(2,1)}, f32[16,512]{1,0:T(8,128)}) custom-call(bf16[64,4096]{1,0:T(8,128)(2,1)} %refs_0_.1, bf16[64,4096]{1,0:T(8,128)(2,1)} %refs_1_.1, f32[1,4096]{1,0:T(1,128)} %bitcast.4, f32[3,3,512]{2,1,0:T(4,128)} %refs_3_.1, ...), custom_call_target="tpu_custom_call" | custom-call | tf_op jit(solution)/shard_map/whole_layer/pallas_call | solution.py:704
  158.8 3.9 %place_results.1 = (bf16[64,4096]{1,0:T(8,128)(2,1)}, bf16[64,4096]{1,0:T(8,128)(2,1)}, bf16[3,256,512]{2,1,0:T(8,128)(2,1)}, bf16[512,256]{1,0:T(8,128)(2,1)}, f32[3,3,512]{2,1,0:T(4,128)}, /*index=5*/f32[7,512]{1,0:T(8,128)}) custom-call(bf16[64,4096]{1,0:T(8,128)(2,1)} %get-tuple-element.17.layer, bf16[64,4096]{1,0:T(8,128)(2,1)} %get-tuple-element.18.grad, ...), custom_call_target="tpu_custom_call" | custom-call | tf_op jit(solution)/shard_map/place_results/pallas_call | solution.py:770

commit v6 on v5

--- a/solution.py
+++ b/solution.py
@@ -558,6 +558,8 @@
         tiles = (bands // 2) * steps
         lax.fori_loop(0, tiles - steps, backward, 0)
         y_pass(0, 1)
+        tp_halves(0)
+        tp_last(0)
         front_copy(1).wait_recv()
         front_copy(0).wait_recv()
         grads[:, pl.ds(tokens, 8), :] = edges[...]
@@ -608,8 +610,7 @@
         for_self(1, sib, 0)
         y_go(1, 0, 0)
         y_go(1, 0, 1)
-        tp_halves(0)
-        tp_last(0)
+        tp_direct(0)
         for_sibling(1, sib, 2)
         for_self(1, sib, 1)
         y_go(1, 0, 2)
@@ -618,7 +619,6 @@
         y_go(1, 0, 3)
         lag_step(0)
         x_on(0)
-        tp_direct(0)
         gnorm_product()
         tp_begin(1)
         y_pass(1, 0)
@@ -632,6 +632,7 @@
         y_go(1, 1, 0)
         y_go(1, 1, 1)
         tp_halves(1)
+        tp_last(1)
         lag_step(2)
         x_begin(1)
         drained(("y", 1, 0, 4))
@@ -647,6 +648,7 @@
             return carry
 
         lax.fori_loop(0, block // 16, layer_finish, 0)
+        tp_direct(1)
         for side in range(2):
             x_forward(0, side).wait_recv()
         y_done(0, 1)
@@ -655,8 +657,6 @@
         lag_step(3)
         y_pass(1, 1)
         x_on(1)
-        tp_last(1)
-        tp_direct(1)
         for slot in (5, 6, 7):
             tp_copy(1, slot).wait_recv()
 

time: 165 us -> 164 us (level)
  no operation moved by 1% of the time
where the time goes in v6:
time: 164 us; the launch traced here: 163 us
  Pallas kernels  162 us (99%)
    pallas_call x1, Pallas kernels, layer_results(): pl.pallas_call(body, out_shape=(jax.ShapeDtypeStruct((block, width), bf16...  159 us
    pallas_call x1, Pallas kernels, placed_results(): pl.pallas_call(place_kernel, out_shape=tuple((jax.ShapeDtypeStruct(array....  3.88 us

profile of v6, /device:TPU:0, one launch (start us, length us, event | category | flops | bytes accessed | tf_op | source)
XLA Modules:
  0.0 163.3 jit_solution(11378021127227744927)
XLA Ops:
  0.6 158.6 %whole_layer.1 = (bf16[64,4096]{1,0:T(8,128)(2,1)}, bf16[64,4096]{1,0:T(8,128)(2,1)}, bf16[3,256,512]{2,1,0:T(8,128)(2,1)}, bf16[512,256]{1,0:T(8,128)(2,1)}, f32[16,512]{1,0:T(8,128)}) custom-call(bf16[64,4096]{1,0:T(8,128)(2,1)} %refs_0_.1, bf16[64,4096]{1,0:T(8,128)(2,1)} %refs_1_.1, f32[1,4096]{1,0:T(1,128)} %bitcast.4, f32[3,3,512]{2,1,0:T(4,128)} %refs_3_.1, ...), custom_call_target="tpu_custom_call" | custom-call | tf_op jit(solution)/shard_map/whole_layer/pallas_call | solution.py:704
  159.2 3.9 %place_results.1 = (bf16[64,4096]{1,0:T(8,128)(2,1)}, bf16[64,4096]{1,0:T(8,128)(2,1)}, bf16[3,256,512]{2,1,0:T(8,128)(2,1)}, bf16[512,256]{1,0:T(8,128)(2,1)}, f32[3,3,512]{2,1,0:T(4,128)}, /*index=5*/f32[7,512]{1,0:T(8,128)}) custom-call(bf16[64,4096]{1,0:T(8,128)(2,1)} %get-tuple-element.17.layer, bf16[64,4096]{1,0:T(8,128)(2,1)} %get-tuple-element.18.grad, ...), custom_call_target="tpu_custom_call" | custom-call | tf_op jit(solution)/shard_map/place_results/pallas_call | solution.py:770

commit v7 on v6

--- a/solution.py
+++ b/solution.py
@@ -29,11 +29,27 @@
         x = (self.x_hi * 2 + self.x_lo + step) % 4
         return (self.y * 4 + (x // 2) * 2 + self.core, self.z * 2 + x % 2)
 
-    def along_ctx(self, step):
-        return ((self.ctx + step) % 16, self.tp)
+    def at(self, y, x, core):
+        return (y * 4 + (x // 2) * 2 + core, self.z * 2 + x % 2)
 
     def partner(self):
-        return (self.ctx, self.z * 2 + 1 - self.x_lo)
+        return self.along_x((1 - 2 * self.core) * (1 - 2 * self.x_lo))
+
+    def last_block(self):
+        x_hi, x_lo = self.x_hi, self.x_lo
+        return jnp.where(self.core == 1, x_hi * x_lo + (1 - x_hi) * (1 - x_lo), x_hi)
+
+    def following(self):
+        x_hi, x_lo, core = self.x_hi, self.x_lo, self.core
+        held = x_hi * x_lo + (1 - x_hi) * (1 - x_lo)
+        x = (1 - core) * ((2 * x_hi + 3 * x_lo) % 4) + core * ((1 - held) * 2 + x_lo)
+        return self.at((self.y + core * held) % 4, x, 1 - core)
+
+    def preceding(self):
+        x_hi, x_lo, core = self.x_hi, self.x_lo, self.core
+        held = x_hi * (1 - x_lo) + (1 - x_hi) * x_lo
+        x = core * (held * 2 + x_lo) + (1 - core) * (((1 - x_hi) * 2 + 2 - x_lo) % 4)
+        return self.at((self.y - (1 - core) * (1 - x_hi)) % 4, x, 1 - core)
 
     def block(self, step, same):
         x_lo = self.x_lo if same else 1 - self.x_lo
@@ -54,7 +70,7 @@
     scale, tokens,
     hidden, cot, gain, short_taps, inner_taps, in_w_hbm, out_w_hbm,
     layer_ref, input_ref, in_grad_ref, out_grad_ref, lag_ref,
-    both, out_w, proj, edges, lags, acts, turned, part,
+    both, out_w, proj, first_in, before_in, last_in, after_in, lags, acts, turned, part,
     sums_out, sums_in, y_out, y_in, pass_out, pass_in, x_out, x_in, tp_in, lag_sum, lag_got,
     load_sem, in_w_sem, send_sem, recv_sem, edge_send, edge_recv,
     sib_send, sib_recv, y_send, y_recv, x_send, x_recv, tp_send, tp_recv, lag_send, lag_recv,
@@ -69,14 +85,14 @@
     steps = chans // 128
     bands = tokens // span
     step_in = 512
-    x_cols = (width // 128 * 5 // 32) * 128
+    x_cols = (width // 128 * 3 // 4) * 128
     bf16, f32 = jnp.bfloat16, jnp.float32
 
     out_load = pltpu.make_async_copy(out_w_hbm, out_w, load_sem.at[3])
     barrier = pltpu.get_barrier_semaphore()
     devices = [
         here.sibling(), here.along_y(1), here.along_y(-1), here.along_y(2), here.along_z(1), here.along_z(-1),
-        here.along_x(1), here.along_x(-1), here.along_x(2), here.along_ctx(1), here.along_ctx(-1),
+        here.along_x(1), here.along_x(-1), here.along_x(2), here.following(), here.preceding(),
     ]
     for device in devices:
         pl.semaphore_signal(barrier, inc=1, device_id=device, device_id_type=MESH)
@@ -363,13 +379,17 @@
                 value = jnp.dot(
                     both[0, pl.ds(pl.multiple_of(begin, group), group), :], in_w[kind], preferred_element_type=f32
                 )
-                proj[kind, pl.ds(pl.multiple_of(8 + begin, 8), group), :] = value.astype(bf16).astype(f32)
+                value = value.astype(bf16).astype(f32)
+                for index in range(2):
+                    first = (begin // block + index) * wide + 8
+                    proj[kind, pl.ds(pl.multiple_of(first, 8), block), :] = value[index * block : (index + 1) * block]
                 return carry
 
             lax.fori_loop(0, 3, loop, 0)
 
         for slot in range(3):
             gather(0, slot)
+        gather(1, 0)
         arrived(0, 1)
         gather(0, 5)
         gather(0, 8)
@@ -379,8 +399,8 @@
         arrived(0, 0)
         gather(0, 3)
         gather(0, 4)
-        for slot in range(3):
-            gather(1, slot)
+        gather(1, 1)
+        gather(1, 2)
         for copy in loads:
             copy.wait()
         project(0)
@@ -399,28 +419,67 @@
         arrived(1, 2)
         gather(1, 6)
         gather(1, 9)
-        arrived(0, 7)
-        project(2)
-
-    def filter_phase(query, gates, prods, grads, sib):
-        def edge_copy():
-            return remote(
-                proj.at[:, pl.ds(tokens, 8), :], proj.at[:, pl.ds(0, 8), :], edge_send.at[0], edge_recv.at[0],
-                here.along_ctx(1))
-
-        def front_copy(which):
-            first = pl.ds((0, 2)[which], 2)
-            return remote(
-                grads.at[first, pl.ds(0, 8), :], edges.at[first], edge_send.at[1 + which], edge_recv.at[1 + which],
-                here.along_ctx(-1))
-
-        go(("edge", 0), edge_copy)
         arrived(1, 0)
         gather(1, 3)
         gather(1, 4)
+        arrived(0, 7)
+        project(2)
+
+    def filter_phase(query, gates, prods, grads, ends, heads, sib):
+        def first_copy():
+            return remote(
+                proj.at[:, pl.ds(7 * wide + span, 8), :], first_in, edge_send.at[0], edge_recv.at[0], here.following())
+
+        def before_copy():
+            return remote(ends, before_in, edge_send.at[1], edge_recv.at[1], here.along_x(2))
+
+        def last_copy(which):
+            kinds = pl.ds((0, 2)[which], 2)
+            return remote(
+                grads.at[kinds, pl.ds(0, 8), :], last_in.at[kinds], edge_send.at[2 + which], edge_recv.at[2 + which],
+                here.preceding())
+
+        def after_copy(which):
+            kinds = pl.ds((0, 2)[which], 2)
+            return remote(
+                heads.at[kinds], after_in.at[kinds], edge_send.at[4 + which], edge_recv.at[4 + which],
+                here.along_x(2))
+
+        def edge_rows(target, kinds, source, offset):
+            for kind in kinds:
+                for pair in range(4):
+                    rows = [source[kind, pl.ds((2 * pair + index) * wide + offset, 8), :] for index in range(2)]
+                    target[kind, pl.ds(pair * 16, 16), :] = jnp.concatenate(rows).astype(bf16)
+
+        def share(target, kinds, copy, source):
+            @pl.when(here.core == 1)
+            def _():
+                copy().wait_recv()
+
+            @pl.when(here.core == 0)
+            def _():
+                for kind in kinds:
+                    target[kind] = source[kind]
+
+        edge_rows(ends, range(3), proj, span)
+        go(("edge", 0), first_copy)
+
+        @pl.when(here.core == 1)
+        def _():
+            before_copy().start()
+
         arrived(1, 5)
         arrived(1, 6)
         gather(1, 7)
+        first_copy().wait_recv()
+        share(before_in, range(3), before_copy, ends)
+        for kind in range(3):
+            proj[kind, pl.ds(0, 8), :] = first_in[kind] * jnp.where(here.ctx == 0, 0.0, 1.0).astype(f32)
+            for pair in range(4):
+                rows = before_in[kind, pl.ds(pair * 16, 16), :].astype(f32)
+                proj[kind, pl.ds((2 * pair + 1) * wide, 8), :] = rows[:8]
+                if pair < 3:
+                    proj[kind, pl.ds((2 * pair + 2) * wide, 8), :] = rows[8:]
 
         def short(lag, kind, cols):
             return short_taps[lag, pl.ds(kind, 1), cols]
@@ -436,10 +495,11 @@
 
         def forward(index, carry):
             begin = pl.multiple_of((index // steps) * span, span)
+            first = pl.multiple_of((index // steps) * wide, 8)
             cols = tile(index % steps, 128)
             feats = []
             for kind in range(3):
-                held = proj[kind, pl.ds(begin, wide), cols]
+                held = proj[kind, pl.ds(first, wide), cols]
                 total = short(0, kind, cols) * held
                 for lag in (1, 2):
                     total = total + short(lag, kind, cols) * behind(held, lag)
@@ -450,22 +510,21 @@
                 total = total + inner(lag, cols) * behind(product, lag)
             rows = pl.ds(begin, span)
             query[rows, cols] = feats[0][8:]
-            grads[3, rows, cols] = feats[1][8:]
-            grads[2, rows, cols] = feats[2][8:]
+            grads[3, pl.ds(first, span), cols] = feats[1][8:]
+            grads[2, pl.ds(first, span), cols] = feats[2][8:]
             gates[rows, cols] = total[8:]
             prods[rows, cols] = product[8:]
             acts[rows, tile(3 * steps + index % steps, 128)] = (feats[0][8:] * total[8:]).astype(bf16)
             return carry
 
-        lax.fori_loop(steps, bands * steps, forward, 0)
-        edge_copy().wait_recv()
-
-        @pl.when(here.ctx == 0)
+        lax.fori_loop(0, bands * steps, forward, 0)
+        edge_rows(heads, (2, 3), grads, 0)
+        go(("edge", 3), lambda: last_copy(1))
+
+        @pl.when(here.core == 1)
         def _():
-            proj[:, pl.ds(0, 8), :] = jnp.zeros((3, 8, chans), f32)
-
-        lax.fori_loop(0, steps, forward, 0)
-        go(("edge", 1), lambda: front_copy(1))
+            after_copy(1).start()
+
         lags[...] = jnp.zeros_like(lags)
 
         def turn(index, carry):
@@ -498,9 +557,17 @@
         for_self(0, sib, 2)
         y_go(0, 0, 3)
         value = lax.dot_general(both[1], out_w[...], (((1,), (1,)), ((), ())), preferred_element_type=f32)
-        grads[0, pl.ds(0, tokens), :] = value * query[...]
-        grads[1, pl.ds(0, tokens), :] = value * gates[...]
-        go(("edge", 2), lambda: front_copy(0))
+        for index in range(8):
+            rows = pl.ds(index * span, span)
+            grads[0, pl.ds(index * wide, span), :] = value[index * span : (index + 1) * span] * query[rows, :]
+            grads[1, pl.ds(index * wide, span), :] = value[index * span : (index + 1) * span] * gates[rows, :]
+        edge_rows(heads, (0, 1), grads, 0)
+        go(("edge", 2), lambda: last_copy(0))
+
+        @pl.when(here.core == 1)
+        def _():
+            after_copy(0).start()
+
         y_pass(0, 0)
         for index in range(4, 8):
             for_sibling(0, sib, index)
@@ -513,6 +580,18 @@
             if index == 7:
                 y_go(0, 1, 3)
         for_self(0, sib, 7)
+        for which in range(2):
+            last_copy(which).wait_recv()
+            share(after_in, ((0, 1), (2, 3))[which], lambda which=which: after_copy(which), heads)
+        ended = (here.core == 1) & (here.y == 3) & (here.last_block() == 1)
+        for kind in range(4):
+            kept = jnp.where(ended, 0.0, 1.0).astype(f32) if kind < 2 else 1.0
+            grads[kind, pl.ds(7 * wide + span, 8), :] = last_in[kind] * kept
+            for pair in range(4):
+                rows = after_in[kind, pl.ds(pair * 16, 16), :].astype(f32)
+                if pair > 0:
+                    grads[kind, pl.ds((2 * pair - 1) * wide + span, 8), :] = rows[:8]
+                grads[kind, pl.ds(2 * pair * wide + span, 8), :] = rows[8:]
 
         def turn_tile(index):
             rows = tile(index // steps, 128)
@@ -528,8 +607,9 @@
 
         def backward_band(band, column):
             begin = pl.multiple_of(band * span, span)
+            first = pl.multiple_of(band * wide, 8)
             cols = tile(column, 128)
-            rows = pl.ds(begin, wide)
+            rows = pl.ds(first, wide)
             here_rows = pl.ds(begin, span)
 
             def add_lag(row, value):
@@ -546,7 +626,7 @@
             feats = (grads[1, rows, cols], total * grads[2, rows, cols], total * grads[3, rows, cols])
             for kind in range(3):
                 feat = feats[kind]
-                held = proj[kind, pl.ds(pl.multiple_of(begin + 8, 8), span), cols]
+                held = proj[kind, pl.ds(pl.multiple_of(first + 8, 8), span), cols]
                 summed = short(0, kind, cols) * feat[:span]
                 add_lag(kind, feat[:span] * held)
                 for lag in (1, 2):
@@ -560,21 +640,20 @@
         y_pass(0, 1)
         tp_halves(0)
         tp_last(0)
-        front_copy(1).wait_recv()
-        front_copy(0).wait_recv()
-        grads[:, pl.ds(tokens, 8), :] = edges[...]
-
-        @pl.when(here.ctx == 15)
-        def _():
-            grads[pl.ds(0, 2), pl.ds(tokens, 8), :] = jnp.zeros((2, 8, chans), f32)
-
         lax.fori_loop(tiles - steps, tiles, backward, 0)
         turn_tile(tiles - 1)
         lag_sum[0] = jnp.sum(lags[...], axis=1) * scale
         go(("lag", 0), lambda: lag_copy(0))
         x_begin(0)
-        for index in range(3):
+        for index in (0, 2, 3):
             drained(("edge", index))
+
+        @pl.when(here.core == 1)
+        def _():
+            before_copy().wait_send()
+            after_copy(0).wait_send()
+            after_copy(1).wait_send()
+
         for index in range(4, 8):
             drained(("sib", 0, index))
 
@@ -684,7 +763,9 @@
         pltpu.VMEM((tokens, chans), f32),
         pltpu.VMEM((tokens, chans), f32),
         pltpu.VMEM((tokens, chans), f32),
-        pltpu.VMEM((4, tokens + 8, chans), f32),
+        pltpu.VMEM((4, bands * wide, chans), f32),
+        pltpu.VMEM((3, bands * 8, chans), bf16),
+        pltpu.VMEM((4, bands * 8, chans), bf16),
         pltpu.VMEM((4, chans, cut), bf16),
     )
     pl.run_scoped(
@@ -715,8 +796,11 @@
         scratch_shapes=[
             pltpu.VMEM((2, tokens, width), bf16),
             pltpu.VMEM(out_weight.shape, bf16),
-            pltpu.VMEM((3, tokens + 8, chans), f32),
+            pltpu.VMEM((3, tokens + 64, chans), f32),
+            pltpu.VMEM((3, 8, chans), f32),
+            pltpu.VMEM((3, 64, chans), bf16),
             pltpu.VMEM((4, 8, chans), f32),
+            pltpu.VMEM((4, 64, chans), bf16),
             pltpu.VMEM((16, 8, chans), f32),
             pltpu.VMEM((tokens, 4 * chans), bf16),
             pltpu.VMEM((4 * chans, tokens), bf16),
@@ -732,7 +816,7 @@
             pltpu.VMEM((2, 7, block, width), bf16),
             pltpu.VMEM((4, 16, chans), f32),
             pltpu.VMEM((4, 16, chans), f32),
-            dma((4,)), dma((2,)), dma((2, 10)), dma((2, 10)), dma((3,)), dma((3,)),
+            dma((4,)), dma((2,)), dma((2, 10)), dma((2, 10)), dma((6,)), dma((6,)),
             dma((2, 8)), dma((2, 8)), dma((2, 2, 6)), dma((2, 2, 6)), dma((2, 4)), dma((2, 4)),
             dma((2, 8)), dma((2, 8)), dma((4,)), dma((4,)),
         ],

time: 164 us -> 152 us (0.927)
  Pallas kernels: 162 us -> 150 us
    pallas_call x1, Pallas kernels: 159 us -> 146 us  [layer_results(): pl.pallas_call(body, out_shape=(jax.ShapeDtypeStruct((block, width), bf16...]
where the time goes in v7:
time: 152 us; the launch traced here: 150 us
  Pallas kernels  150 us (99%)
    pallas_call x1, Pallas kernels, layer_results(): pl.pallas_call(body, out_shape=(jax.ShapeDtypeStruct((block, width), bf16...  146 us
    pallas_call x1, Pallas kernels, placed_results(): pl.pallas_call(place_kernel, out_shape=tuple((jax.ShapeDtypeStruct(array....  3.88 us

profile of v7, /device:TPU:0, one launch (start us, length us, event | category | flops | bytes accessed | tf_op | source)
XLA Modules:
  0.0 150.5 jit_solution(8159852924426093484)
XLA Ops:
  0.6 145.8 %whole_layer.1 = (bf16[64,4096]{1,0:T(8,128)(2,1)}, bf16[64,4096]{1,0:T(8,128)(2,1)}, bf16[3,256,512]{2,1,0:T(8,128)(2,1)}, bf16[512,256]{1,0:T(8,128)(2,1)}, f32[16,512]{1,0:T(8,128)}) custom-call(bf16[64,4096]{1,0:T(8,128)(2,1)} %refs_0_.1, bf16[64,4096]{1,0:T(8,128)(2,1)} %refs_1_.1, f32[1,4096]{1,0:T(1,128)} %bitcast.4, f32[3,3,512]{2,1,0:T(4,128)} %refs_3_.1, ...), custom_call_target="tpu_custom_call" | custom-call | tf_op jit(solution)/shard_map/whole_layer/pallas_call | solution.py:785
  146.4 3.9 %place_results.1 = (bf16[64,4096]{1,0:T(8,128)(2,1)}, bf16[64,4096]{1,0:T(8,128)(2,1)}, bf16[3,256,512]{2,1,0:T(8,128)(2,1)}, bf16[512,256]{1,0:T(8,128)(2,1)}, f32[3,3,512]{2,1,0:T(4,128)}, /*index=5*/f32[7,512]{1,0:T(8,128)}) custom-call(bf16[64,4096]{1,0:T(8,128)(2,1)} %get-tuple-element.17.layer, bf16[64,4096]{1,0:T(8,128)(2,1)} %get-tuple-element.18.grad, ...), custom_call_target="tpu_custom_call" | custom-call | tf_op jit(solution)/shard_map/place_results/pallas_call | solution.py:854

commit v8 on v7

--- a/solution.py
+++ b/solution.py
@@ -70,8 +70,9 @@
     scale, tokens,
     hidden, cot, gain, short_taps, inner_taps, in_w_hbm, out_w_hbm,
     layer_ref, input_ref, in_grad_ref, out_grad_ref, lag_ref,
-    both, out_w, proj, first_in, before_in, last_in, after_in, lags, acts, turned, part,
-    sums_out, sums_in, y_out, y_in, pass_out, pass_in, x_out, x_in, tp_in, lag_sum, lag_got,
+    both, out_w, proj, first_in, before_in, last_in, after_in, lags, acts, turned,
+    sums_out, sums_in, sums_val, y_out, y_in, y_val, pass_out, pass_in, pass_val, x_out, x_in, x_val,
+    tp_in, lag_sum, lag_got,
     load_sem, in_w_sem, send_sem, recv_sem, edge_send, edge_recv,
     sib_send, sib_recv, y_send, y_recv, x_send, x_recv, tp_send, tp_recv, lag_send, lag_recv,
 ):
@@ -151,7 +152,7 @@
         remote(held, held, send_sem.at[which, slot], recv_sem.at[which, slot], here.partner()).wait_recv()
 
 
-    parts = (part, out_w)
+    parts = [None, out_w]
 
     def tp_copy(which, slot):
         source, held = parts[which], tp_in.at[which]
@@ -218,10 +219,10 @@
         return at, total
 
 
-    sums = (sums_out, sums_in)
-    arriving = (y_out, y_in)
-    passing = (pass_out, pass_in)
-    crossing = (x_out, x_in)
+    sums = (sums_out, sums_in, sums_val)
+    arriving = (y_out, y_in, y_val)
+    passing = (pass_out, pass_in, pass_val)
+    crossing = (x_out, x_in, x_val)
 
     def halves(kind):
         size = sums[kind].shape[1] // 2
@@ -237,13 +238,13 @@
 
         def one(step, carry):
             rows = tile(step, chans)
-            first = 3 * chans if kind == 0 else 0
+            first = (3, 0, 2)[kind] * chans
             left = turned[pl.ds(pl.multiple_of(first + step * chans, chans), chans), :]
-            value = jnp.dot(left, both[1 - kind, :, cols], preferred_element_type=f32)
+            value = jnp.dot(left, both[(1, 0, 0)[kind], :, cols], preferred_element_type=f32)
             write(rows, value * scale)
             return carry
 
-        lax.fori_loop(0, (1, 3)[kind], one, 0)
+        lax.fori_loop(0, (1, 2, 1)[kind], one, 0)
 
     def sib_copy(kind, sib, index):
         return remote(
@@ -275,7 +276,7 @@
             (0, upper, 1), (0, lower, -1), (1, lower, 1), (2, upper, -1), (1, upper, 1), (2, lower, -1)
         )[slot]
         return remote(
-            sums[kind].at[far * 4 + index, rows], arriving[kind].at[far, slot],
+            sums[kind].at[far * 4 + index, rows], arriving[kind].at[far if kind < 2 else 0, slot],
             y_send.at[kind, far, slot], y_recv.at[kind, far, slot], here.along_y(step),
         )
 
@@ -285,10 +286,11 @@
     def y_pass(kind, far):
         size = halves(kind)[2]
         y_copy(kind, far, 0).wait_recv()
-        add_rows(sums[kind].at[far * 4 + 1], 0, size, [arriving[kind].at[far, 0]])
+        held = arriving[kind].at[far if kind < 2 else 0]
+        add_rows(sums[kind].at[far * 4 + 1], 0, size, [held.at[0]])
         y_go(kind, far, 4)
         y_copy(kind, far, 1).wait_recv()
-        add_rows(sums[kind].at[far * 4 + 2], size, size, [arriving[kind].at[far, 1]])
+        add_rows(sums[kind].at[far * 4 + 2], size, size, [held.at[1]])
         y_go(kind, far, 5)
 
     def y_done(kind, far):
@@ -297,8 +299,9 @@
 
     def x_copy(kind, side):
         rows = halves(kind)[side]
+        source = sums[kind].at[3, rows] if kind < 2 else sums[kind].at[pl.ds(0, 4), rows]
         return remote(
-            sums[kind].at[3, rows], passing[kind].at[side], x_send.at[kind, side], x_recv.at[kind, side],
+            source, passing[kind].at[side], x_send.at[kind, side], x_recv.at[kind, side],
             here.along_x((1, -1)[side]))
 
     def x_forward(kind, side):
@@ -325,16 +328,21 @@
     def last(kind, side):
         size = halves(kind)[2]
         begin = side * size
-        others = [arriving[kind].at[1, slot] for slot in ((3, 4), (2, 5))[side]] + [crossing[kind].at[side]]
+        slots = ((3, 4), (2, 5))[side]
+        if kind < 2:
+            others = [arriving[kind].at[1, slot] for slot in slots] + [crossing[kind].at[side]]
+        else:
+            others = [arriving[kind].at[0, slot] for slot in slots]
         for index in range(size // 128):
             row = begin + index * 128
             total = sums[kind][7, pl.ds(row, 128), :].astype(f32)
             for other in others:
                 total = total + other[pl.ds(index * 128, 128), :].astype(f32)
-            if kind == 1:
-                in_grad_ref[row // chans, :, pl.ds(row % chans, 128)] = total.T.astype(bf16)
+            if kind == 0:
+                out_grad_ref[pl.ds(row, 128), :] = total.astype(bf16)
             else:
-                out_grad_ref[pl.ds(row, 128), :] = total.astype(bf16)
+                to = row // chans if kind == 1 else 2
+                in_grad_ref[to, :, pl.ds(row % chans, 128)] = total.T.astype(bf16)
 
     def lag_copy(step):
         device = (
@@ -537,7 +545,7 @@
         def branch_product(index, carry):
             cols = tile(index, chans)
             value = jnp.dot(acts[:, pl.ds(3 * chans, chans)], out_w[:, cols], preferred_element_type=f32)
-            part[:, cols] = value.astype(bf16)
+            parts[0][:, cols] = value.astype(bf16)
             return carry
 
         lax.fori_loop(0, width // chans, branch_product, 0)
@@ -657,7 +665,7 @@
         for index in range(4, 8):
             drained(("sib", 0, index))
 
-    def reduce_phase(in_w, sib):
+    def reduce_phase(in_w, sib, sib_val):
         def in_load(step, slot):
             return pltpu.make_async_copy(in_w_hbm.at[:, tile(step, step_in), :], in_w.at[slot], in_w_sem.at[slot])
 
@@ -690,6 +698,13 @@
         y_go(1, 0, 0)
         y_go(1, 0, 1)
         tp_direct(0)
+        for_sibling(2, sib_val, 0)
+        for index in range(1, 4):
+            for_sibling(2, sib_val, index)
+            for_self(2, sib_val, index - 1)
+        for_self(2, sib_val, 3)
+        for side in range(2):
+            go(("x", 2, side), lambda side=side: x_copy(2, side))
         for_sibling(1, sib, 2)
         for_self(1, sib, 1)
         y_go(1, 0, 2)
@@ -702,6 +717,7 @@
         tp_begin(1)
         y_pass(1, 0)
         lag_step(1)
+        x_on(2)
         for index in range(4, 8):
             for_sibling(1, sib, index)
             for_self(1, sib, index - 1)
@@ -710,6 +726,11 @@
             drained(("y", 1, 0, slot))
         y_go(1, 1, 0)
         y_go(1, 1, 1)
+        for index in range(4, 8):
+            for_sibling(2, sib_val, index)
+            if index > 4:
+                for_self(2, sib_val, index - 1)
+        for_self(2, sib_val, 7)
         tp_halves(1)
         tp_last(1)
         lag_step(2)
@@ -735,7 +756,15 @@
         last(0, 1)
         lag_step(3)
         y_pass(1, 1)
+        size = halves(2)[2]
+        for side in range(2):
+            x_forward(2, side).wait_recv()
+            for index in range(4):
+                add_rows(sums_val.at[4 + index], side * size, size, [x_val.at[side, index]])
+        for slot in range(4):
+            y_go(2, 1, slot)
         x_on(1)
+        y_pass(2, 1)
         for slot in (5, 6, 7):
             tp_copy(1, slot).wait_recv()
 
@@ -754,23 +783,33 @@
         y_done(1, 1)
         last(1, 0)
         last(1, 1)
+        y_done(2, 1)
+        last(2, 0)
+        last(2, 1)
         for name in list(sends):
             drained(name)
 
+    def later_phases(part):
+        parts[0] = part
+        pl.run_scoped(
+            filter_phase,
+            pltpu.VMEM((tokens, chans), f32),
+            pltpu.VMEM((tokens, chans), f32),
+            pltpu.VMEM((tokens, chans), f32),
+            pltpu.VMEM((4, bands * wide, chans), f32),
+            pltpu.VMEM((3, bands * 8, chans), bf16),
+            pltpu.VMEM((4, bands * 8, chans), bf16),
+            pltpu.VMEM((4, chans, cut), bf16),
+        )
+        pl.run_scoped(
+            reduce_phase,
+            pltpu.VMEM((2, 3, step_in, chans), bf16),
+            pltpu.VMEM((4, 2 * chans, cut), bf16),
+            pltpu.VMEM((4, chans, cut), bf16),
+        )
+
     pl.run_scoped(gather_phase, pltpu.VMEM((3, width, chans), bf16))
-    pl.run_scoped(
-        filter_phase,
-        pltpu.VMEM((tokens, chans), f32),
-        pltpu.VMEM((tokens, chans), f32),
-        pltpu.VMEM((tokens, chans), f32),
-        pltpu.VMEM((4, bands * wide, chans), f32),
-        pltpu.VMEM((3, bands * 8, chans), bf16),
-        pltpu.VMEM((4, bands * 8, chans), bf16),
-        pltpu.VMEM((4, chans, cut), bf16),
-    )
-    pl.run_scoped(
-        reduce_phase, pltpu.VMEM((2, 3, step_in, chans), bf16), pltpu.VMEM((4, 3 * chans, cut), bf16)
-    )
+    pl.run_scoped(later_phases, pltpu.VMEM((tokens, width), bf16))
 
 
 def layer_results(hidden, cot, gain, short_taps, inner_taps, in_weight, out_weight, tokens, scale):
@@ -804,20 +843,23 @@
             pltpu.VMEM((16, 8, chans), f32),
             pltpu.VMEM((tokens, 4 * chans), bf16),
             pltpu.VMEM((4 * chans, tokens), bf16),
-            pltpu.VMEM((tokens, width), bf16),
             pltpu.VMEM((8, chans, cut), bf16),
-            pltpu.VMEM((8, 3 * chans, cut), bf16),
+            pltpu.VMEM((8, 2 * chans, cut), bf16),
+            pltpu.VMEM((8, chans, cut), bf16),
             pltpu.VMEM((2, 6, chans // 2, cut), bf16),
-            pltpu.VMEM((2, 6, 3 * chans // 2, cut), bf16),
+            pltpu.VMEM((2, 6, chans, cut), bf16),
+            pltpu.VMEM((1, 6, chans // 2, cut), bf16),
             pltpu.VMEM((2, chans // 2, cut), bf16),
-            pltpu.VMEM((2, 3 * chans // 2, cut), bf16),
+            pltpu.VMEM((2, chans, cut), bf16),
+            pltpu.VMEM((2, 4, chans // 2, cut), bf16),
             pltpu.VMEM((2, chans // 2, cut), bf16),
-            pltpu.VMEM((2, 3 * chans // 2, cut), bf16),
+            pltpu.VMEM((2, chans, cut), bf16),
+            pltpu.VMEM((2, 4, chans // 2, cut), bf16),
             pltpu.VMEM((2, 7, block, width), bf16),
             pltpu.VMEM((4, 16, chans), f32),
             pltpu.VMEM((4, 16, chans), f32),
             dma((4,)), dma((2,)), dma((2, 10)), dma((2, 10)), dma((6,)), dma((6,)),
-            dma((2, 8)), dma((2, 8)), dma((2, 2, 6)), dma((2, 2, 6)), dma((2, 4)), dma((2, 4)),
+            dma((3, 8)), dma((3, 8)), dma((3, 2, 6)), dma((3, 2, 6)), dma((3, 4)), dma((3, 4)),
             dma((2, 8)), dma((2, 8)), dma((4,)), dma((4,)),
         ],
         compiler_params=pltpu.CompilerParams(

time: 152 us -> 155 us (1.020)
  Pallas kernels: 150 us -> 153 us
    pallas_call x1, Pallas kernels: 146 us -> 149 us  [layer_results(): pl.pallas_call(body, out_shape=(jax.ShapeDtypeStruct((block, width), bf16...]
where the time goes in v8:
time: 155 us; the launch traced here: 154 us
  Pallas kernels  153 us (99%)
    pallas_call x1, Pallas kernels, layer_results(): pl.pallas_call(body, out_shape=(jax.ShapeDtypeStruct((block, width), bf16...  149 us
    pallas_call x1, Pallas kernels, placed_results(): pl.pallas_call(place_kernel, out_shape=tuple((jax.ShapeDtypeStruct(array....  3.88 us

profile of v8, /device:TPU:0, one launch (start us, length us, event | category | flops | bytes accessed | tf_op | source)
XLA Modules:
  0.0 153.7 jit_solution(17983180208184867775)
XLA Ops:
  0.6 149.0 %whole_layer.1 = (bf16[64,4096]{1,0:T(8,128)(2,1)}, bf16[64,4096]{1,0:T(8,128)(2,1)}, bf16[3,256,512]{2,1,0:T(8,128)(2,1)}, bf16[512,256]{1,0:T(8,128)(2,1)}, f32[16,512]{1,0:T(8,128)}) custom-call(bf16[64,4096]{1,0:T(8,128)(2,1)} %refs_0_.1, bf16[64,4096]{1,0:T(8,128)(2,1)} %refs_1_.1, f32[1,4096]{1,0:T(1,128)} %bitcast.4, f32[3,3,512]{2,1,0:T(4,128)} %refs_3_.1, ...), custom_call_target="tpu_custom_call" | custom-call | tf_op jit(solution)/shard_map/whole_layer/pallas_call | solution.py:824
  149.6 3.9 %place_results.1 = (bf16[64,4096]{1,0:T(8,128)(2,1)}, bf16[64,4096]{1,0:T(8,128)(2,1)}, bf16[3,256,512]{2,1,0:T(8,128)(2,1)}, bf16[512,256]{1,0:T(8,128)(2,1)}, f32[3,3,512]{2,1,0:T(4,128)}, /*index=5*/f32[7,512]{1,0:T(8,128)}) custom-call(bf16[64,4096]{1,0:T(8,128)(2,1)} %get-tuple-element.17.layer, bf16[64,4096]{1,0:T(8,128)(2,1)} %get-tuple-element.18.grad, ...), custom_call_target="tpu_custom_call" | custom-call | tf_op jit(solution)/shard_map/place_results/pallas_call | solution.py:896

commit v9 on v7

--- a/solution.py
+++ b/solution.py
@@ -68,11 +68,12 @@
 
 def layer_kernel(
     scale, tokens,
-    hidden, cot, gain, short_taps, inner_taps, in_w_hbm, out_w_hbm,
-    layer_ref, input_ref, in_grad_ref, out_grad_ref, lag_ref,
+    hidden_hbm, cot_hbm, gain_hbm, short_hbm, inner_hbm, in_w_hbm, out_w_hbm,
+    layer_hbm, input_hbm, in_grad_hbm, out_grad_hbm, lag_hbm,
+    hidden, cot, gain, short_taps, inner_taps, layer_ref, input_ref, in_grad_ref, out_grad_ref, lag_ref,
     both, out_w, proj, first_in, before_in, last_in, after_in, lags, acts, turned, part,
     sums_out, sums_in, y_out, y_in, pass_out, pass_in, x_out, x_in, tp_in, lag_sum, lag_got,
-    load_sem, in_w_sem, send_sem, recv_sem, edge_send, edge_recv,
+    load_sem, row_sem, result_sem, in_w_sem, send_sem, recv_sem, edge_send, edge_recv,
     sib_send, sib_recv, y_send, y_recv, x_send, x_recv, tp_send, tp_recv, lag_send, lag_recv,
 ):
     here = Place()
@@ -96,6 +97,20 @@
     ]
     for device in devices:
         pl.semaphore_signal(barrier, inc=1, device_id=device, device_id_type=MESH)
+    row_loads = [
+        pltpu.make_async_copy(source, target, row_sem.at[index])
+        for index, (source, target) in enumerate(
+            ((hidden_hbm, hidden), (cot_hbm, cot), (gain_hbm, gain), (short_hbm, short_taps), (inner_hbm, inner_taps)))
+    ]
+    for copy in row_loads:
+        copy.start()
+
+    def result(index):
+        source, target = (
+            (layer_ref, layer_hbm), (input_ref, input_hbm), (in_grad_ref, in_grad_hbm),
+            (out_grad_ref, out_grad_hbm), (lag_ref, lag_hbm),
+        )[index]
+        return pltpu.make_async_copy(source, target, result_sem.at[index])
 
     sends = {}
 
@@ -359,6 +374,8 @@
         for copy in loads:
             copy.start()
         out_load.start()
+        for copy in row_loads:
+            copy.wait()
 
         def normalise(index, carry):
             at = tile(index, 16)
@@ -658,31 +675,35 @@
             drained(("sib", 0, index))
 
     def reduce_phase(in_w, sib):
-        def in_load(step, slot):
-            return pltpu.make_async_copy(in_w_hbm.at[:, tile(step, step_in), :], in_w.at[slot], in_w_sem.at[slot])
-
-        in_load(0, 0).start()
-        in_load(1, 1).start()
-
-        def gnorm_product():
+        def in_loads(step, slot):
+            return [
+                pltpu.make_async_copy(
+                    in_w_hbm.at[kind, tile(step, step_in), :], in_w.at[slot, :, pl.ds(kind * chans, chans)],
+                    in_w_sem.at[slot, kind])
+                for kind in range(3)
+            ]
+
+        for step in range(2):
+            for copy in in_loads(step, step):
+                copy.start()
+
+        def gnorm_product(first, count):
             def loop(step, carry):
                 slot = step % 2
-                in_load(step, slot).wait()
-                value = jnp.zeros((tokens, step_in), f32)
-                for kind in range(3):
-                    value = value + lax.dot_general(
-                        acts[:, pl.ds(kind * chans, chans)], in_w[slot, kind],
-                        (((1,), (1,)), ((), ())), preferred_element_type=f32,
-                    )
+                for copy in in_loads(step, slot):
+                    copy.wait()
+                value = lax.dot_general(
+                    acts[:, pl.ds(0, 3 * chans)], in_w[slot], (((1,), (1,)), ((), ())), preferred_element_type=f32)
                 out_w[:, tile(step, step_in)] = value.astype(bf16)
 
                 @pl.when(step + 2 < width // step_in)
                 def _():
-                    in_load(step + 2, slot).start()
+                    for copy in in_loads(step + 2, slot):
+                        copy.start()
 
                 return carry
 
-            lax.fori_loop(0, width // step_in, loop, 0)
+            lax.fori_loop(first, first + count, loop, 0)
 
         for_sibling(1, sib, 0)
         for_sibling(1, sib, 1)
@@ -698,26 +719,29 @@
         y_go(1, 0, 3)
         lag_step(0)
         x_on(0)
-        gnorm_product()
+        in_steps = width // step_in
+        gnorm_product(0, in_steps // 2)
+        y_pass(1, 0)
+        gnorm_product(in_steps // 2, in_steps // 2)
         tp_begin(1)
-        y_pass(1, 0)
-        lag_step(1)
-        for index in range(4, 8):
-            for_sibling(1, sib, index)
-            for_self(1, sib, index - 1)
-        for_self(1, sib, 7)
-        for slot in range(4):
-            drained(("y", 1, 0, slot))
+        for_sibling(1, sib, 4)
+        for_sibling(1, sib, 5)
+        for_self(1, sib, 4)
         y_go(1, 1, 0)
         y_go(1, 1, 1)
+        lag_step(1)
+        for_sibling(1, sib, 6)
+        for_self(1, sib, 5)
+        y_go(1, 1, 2)
+        for_sibling(1, sib, 7)
+        for_self(1, sib, 6)
+        y_go(1, 1, 3)
+        for_self(1, sib, 3)
+        for_self(1, sib, 7)
         tp_halves(1)
         tp_last(1)
         lag_step(2)
         x_begin(1)
-        drained(("y", 1, 0, 4))
-        drained(("y", 1, 0, 5))
-        y_go(1, 1, 2)
-        y_go(1, 1, 3)
         for slot in (5, 6, 7):
             tp_copy(0, slot).wait_recv()
 
@@ -727,13 +751,16 @@
             return carry
 
         lax.fori_loop(0, block // 16, layer_finish, 0)
+        result(0).start()
         tp_direct(1)
         for side in range(2):
             x_forward(0, side).wait_recv()
         y_done(0, 1)
         last(0, 0)
         last(0, 1)
+        result(3).start()
         lag_step(3)
+        result(4).start()
         y_pass(1, 1)
         x_on(1)
         for slot in (5, 6, 7):
@@ -749,13 +776,17 @@
             return carry
 
         lax.fori_loop(0, block // 16, input_finish, 0)
+        result(1).start()
         for side in range(2):
             x_forward(1, side).wait_recv()
         y_done(1, 1)
         last(1, 0)
         last(1, 1)
+        result(2).start()
         for name in list(sends):
             drained(name)
+        for index in range(5):
+            result(index).wait()
 
     pl.run_scoped(gather_phase, pltpu.VMEM((3, width, chans), bf16))
     pl.run_scoped(
@@ -769,7 +800,7 @@
         pltpu.VMEM((4, chans, cut), bf16),
     )
     pl.run_scoped(
-        reduce_phase, pltpu.VMEM((2, 3, step_in, chans), bf16), pltpu.VMEM((4, 3 * chans, cut), bf16)
+        reduce_phase, pltpu.VMEM((2, step_in, 3 * chans), bf16), pltpu.VMEM((4, 3 * chans, cut), bf16)
     )
 
 
@@ -778,7 +809,6 @@
     chans = out_weight.shape[0]
     cut = width // 16
     any_space = pl.BlockSpec(memory_space=pl.ANY)
-    vmem_space = pl.BlockSpec(memory_space=pltpu.VMEM)
     bf16, f32 = jnp.bfloat16, jnp.float32
     dma = pltpu.SemaphoreType.DMA
     body = lambda *refs: layer_kernel(scale, tokens, *refs)
@@ -791,9 +821,19 @@
             jax.ShapeDtypeStruct((chans, cut), bf16),
             jax.ShapeDtypeStruct((16, chans), f32),
         ),
-        in_specs=[vmem_space] * 5 + [any_space] * 2,
-        out_specs=(vmem_space,) * 5,
+        in_specs=[any_space] * 7,
+        out_specs=(any_space,) * 5,
         scratch_shapes=[
+            pltpu.VMEM(hidden.shape, bf16),
+            pltpu.VMEM(cot.shape, bf16),
+            pltpu.VMEM(gain.shape, f32),
+            pltpu.VMEM(short_taps.shape, f32),
+            pltpu.VMEM(inner_taps.shape, f32),
+            pltpu.VMEM((block, width), bf16),
+            pltpu.VMEM((block, width), bf16),
+            pltpu.VMEM((3, cut, chans), bf16),
+            pltpu.VMEM((chans, cut), bf16),
+            pltpu.VMEM((16, chans), f32),
             pltpu.VMEM((2, tokens, width), bf16),
             pltpu.VMEM(out_weight.shape, bf16),
             pltpu.VMEM((3, tokens + 64, chans), f32),
@@ -816,7 +856,7 @@
             pltpu.VMEM((2, 7, block, width), bf16),
             pltpu.VMEM((4, 16, chans), f32),
             pltpu.VMEM((4, 16, chans), f32),
-            dma((4,)), dma((2,)), dma((2, 10)), dma((2, 10)), dma((6,)), dma((6,)),
+            dma((4,)), dma((5,)), dma((5,)), dma((2, 3)), dma((2, 10)), dma((2, 10)), dma((6,)), dma((6,)),
             dma((2, 8)), dma((2, 8)), dma((2, 2, 6)), dma((2, 2, 6)), dma((2, 4)), dma((2, 4)),
             dma((2, 8)), dma((2, 8)), dma((4,)), dma((4,)),
         ],
@@ -829,19 +869,25 @@
 
 def place_kernel(
     layer, grad, kinds, outer, lags, layer_to, grad_to, kinds_to, outer_to, short_to, inner_to,
-    layer_at, grad_at, kinds_at, outer_at, sems,
+    layer_at, grad_at, kinds_at, outer_at, lags_at, short_at, inner_at, read_sems, write_sems,
 ):
-    pairs = ((kinds, kinds_at, kinds_to), (layer, layer_at, layer_to), (grad, grad_at, grad_to), (outer, outer_at, outer_to))
-    reads = [pltpu.make_async_copy(pair[0], pair[1], sems.at[0, index]) for index, pair in enumerate(pairs)]
-    writes = [pltpu.make_async_copy(pair[1], pair[2], sems.at[1, index]) for index, pair in enumerate(pairs)]
+    ends = (
+        (lags, lags_at, None), (kinds, kinds_at, kinds_to), (layer, layer_at, layer_to), (grad, grad_at, grad_to),
+        (outer, outer_at, outer_to), (None, short_at, short_to), (None, inner_at, inner_to),
+    )
+    reads = [pltpu.make_async_copy(ends[index][0], ends[index][1], read_sems.at[index]) for index in range(5)]
+    writes = [pltpu.make_async_copy(ends[index][1], ends[index][2], write_sems.at[index - 1]) for index in range(1, 7)]
     for copy in reads:
         copy.start()
+    reads[0].wait()
     for lag in range(3):
-        short_to[lag] = lags[pl.ds(3 * lag, 3), :]
-    inner_to[...] = lags[pl.ds(9, 7), :]
-    for read, write in zip(reads, writes):
-        read.wait()
-        write.start()
+        short_at[lag] = lags_at[pl.ds(3 * lag, 3), :]
+    inner_at[...] = lags_at[pl.ds(9, 7), :]
+    writes[4].start()
+    writes[5].start()
+    for index in range(4):
+        reads[index + 1].wait()
+        writes[index].start()
     for copy in writes:
         copy.wait()
 
@@ -849,15 +895,17 @@
 def placed_results(layer, grad, kinds, outer, lags):
     chans = lags.shape[1]
     any_space = pl.BlockSpec(memory_space=pl.ANY)
-    vmem_space = pl.BlockSpec(memory_space=pltpu.VMEM)
     arrays = (layer, grad, kinds, outer)
+    ends = ((3, 3, chans), (7, chans))
     return pl.pallas_call(
         place_kernel,
         out_shape=tuple(jax.ShapeDtypeStruct(array.shape, array.dtype) for array in arrays)
-        + (jax.ShapeDtypeStruct((3, 3, chans), jnp.float32), jax.ShapeDtypeStruct((7, chans), jnp.float32)),
-        in_specs=[any_space] * 4 + [vmem_space],
-        out_specs=(any_space,) * 4 + (vmem_space,) * 2,
-        scratch_shapes=[pltpu.VMEM(array.shape, array.dtype) for array in arrays] + [pltpu.SemaphoreType.DMA((2, 4))],
+        + tuple(jax.ShapeDtypeStruct(shape, jnp.float32) for shape in ends),
+        in_specs=[any_space] * 5,
+        out_specs=(any_space,) * 6,
+        scratch_shapes=[pltpu.VMEM(array.shape, array.dtype) for array in (*arrays, lags)]
+        + [pltpu.VMEM(shape, jnp.float32) for shape in ends]
+        + [pltpu.SemaphoreType.DMA((5,)), pltpu.SemaphoreType.DMA((6,))],
         compiler_params=pltpu.CompilerParams(vmem_limit_bytes=60 * 2**20),
         name="place_results",
     )(layer, grad, kinds, outer, lags)

time: 152 us -> 151 us (level)
  no operation moved by 1% of the time
where the time goes in v9:
time: 151 us; the launch traced here: 150 us
  Pallas kernels  149 us (99%)
    pallas_call x1, Pallas kernels, layer_results(): pl.pallas_call(body, out_shape=(jax.ShapeDtypeStruct((block, width), bf16...  146 us

profile of v9, /device:TPU:0, one launch (start us, length us, event | category | flops | bytes accessed | tf_op | source)
XLA Modules:
  0.0 149.8 jit_solution(6364571910464072115)
XLA Ops:
  0.6 146.4 %whole_layer.1 = (bf16[64,4096]{1,0:T(8,128)(2,1)}, bf16[64,4096]{1,0:T(8,128)(2,1)}, bf16[3,256,512]{2,1,0:T(8,128)(2,1)}, bf16[512,256]{1,0:T(8,128)(2,1)}, f32[16,512]{1,0:T(8,128)}) custom-call(bf16[64,4096]{1,0:T(8,128)(2,1)} %refs_0_.1, bf16[64,4096]{1,0:T(8,128)(2,1)} %refs_1_.1, f32[1,4096]{1,0:T(1,128)} %bitcast.4, f32[3,3,512]{2,1,0:T(4,128)} %refs_3_.1, ...), custom_call_target="tpu_custom_call" | custom-call | tf_op jit(solution)/shard_map/whole_layer/pallas_call | solution.py:815
  147.0 2.6 %place_results.1 = (bf16[64,4096]{1,0:T(8,128)(2,1)}, bf16[64,4096]{1,0:T(8,128)(2,1)}, bf16[3,256,512]{2,1,0:T(8,128)(2,1)}, bf16[512,256]{1,0:T(8,128)(2,1)}, f32[3,3,512]{2,1,0:T(4,128)}, /*index=5*/f32[7,512]{1,0:T(8,128)}) custom-call(bf16[64,4096]{1,0:T(8,128)(2,1)} %get-tuple-element.17.layer, bf16[64,4096]{1,0:T(8,128)(2,1)} %get-tuple-element.18.grad, ...), custom_call_target="tpu_custom_call" | custom-call | tf_op jit(solution)/shard_map/place_results/pallas_call | solution.py:900

commit v10 on v9

--- a/solution.py
+++ b/solution.py
@@ -86,7 +86,7 @@
     steps = chans // 128
     bands = tokens // span
     step_in = 512
-    x_cols = (width // 128 * 3 // 4) * 128
+    x_cols = ((width // 128 * 3 // 4) * 128, (width // 128 // 2) * 128)
     bf16, f32 = jnp.bfloat16, jnp.float32
 
     out_load = pltpu.make_async_copy(out_w_hbm, out_w, load_sem.at[3])
@@ -126,9 +126,11 @@
         return pl.ds(pl.multiple_of(here.block(step, same) * block + begin, size), size)
 
     every = pl.ds(0, width)
-    by_x = pl.ds(0, x_cols)
-    by_z = pl.ds(x_cols, width - x_cols)
-    slot_cols = (every, every, every, by_z, by_z, every, every, every, by_x, by_x)
+
+    def slot_cols(which, slot):
+        by_x = pl.ds(0, x_cols[which])
+        by_z = pl.ds(x_cols[which], width - x_cols[which])
+        return (every, every, every, by_z, by_z, every, every, every, by_x, by_x)[slot]
 
     def gather_copy(which, slot):
         rows, device = (
@@ -143,7 +145,7 @@
             lambda: (rows_of(-1, True), here.partner()),
             lambda: (rows_of(1, True), here.partner()),
         )[slot]()
-        held = both.at[which, rows, slot_cols[slot]]
+        held = both.at[which, rows, slot_cols(which, slot)]
         return remote(held, held, send_sem.at[which, slot], recv_sem.at[which, slot], device)
 
     def gather(which, slot):
@@ -162,7 +164,7 @@
             lambda: rows_of(-1, False),
             lambda: rows_of(1, False),
         )[slot]()
-        held = both.at[which, rows, slot_cols[slot]]
+        held = both.at[which, rows, slot_cols(which, slot)]
         remote(held, held, send_sem.at[which, slot], recv_sem.at[which, slot], here.partner()).wait_recv()
 
 
@@ -416,20 +418,66 @@
         arrived(0, 0)
         gather(0, 3)
         gather(0, 4)
-        gather(1, 1)
-        gather(1, 2)
         for copy in loads:
             copy.wait()
         project(0)
         arrived(0, 5)
         arrived(0, 6)
         gather(0, 7)
+        gather(1, 1)
+        gather(1, 2)
         arrived(0, 3)
         arrived(0, 8)
         project(-1)
         arrived(0, 4)
         arrived(0, 9)
         project(1)
+        arrived(0, 7)
+        project(2)
+
+    def filter_phase(query, gates, prods, grads, ends, heads, sib):
+        def first_copy():
+            return remote(
+                proj.at[:, pl.ds(7 * wide + span, 8), :], first_in, edge_send.at[0], edge_recv.at[0], here.following())
+
+        def before_copy():
+            return remote(ends, before_in, edge_send.at[1], edge_recv.at[1], here.along_x(2))
+
+        def last_copy(which):
+            kinds = pl.ds((0, 2)[which], 2)
+            return remote(
+                grads.at[kinds, pl.ds(0, 8), :], last_in.at[kinds], edge_send.at[2 + which], edge_recv.at[2 + which],
+                here.preceding())
+
+        def after_copy(which):
+            kinds = pl.ds((0, 2)[which], 2)
+            return remote(
+                heads.at[kinds], after_in.at[kinds], edge_send.at[4 + which], edge_recv.at[4 + which],
+                here.along_x(2))
+
+        def edge_rows(target, kinds, source, offset):
+            for kind in kinds:
+                for pair in range(4):
+                    rows = [source[kind, pl.ds((2 * pair + index) * wide + offset, 8), :] for index in range(2)]
+                    target[kind, pl.ds(pair * 16, 16), :] = jnp.concatenate(rows).astype(bf16)
+
+        def share(target, kinds, copy, source):
+            @pl.when(here.core == 1)
+            def _():
+                copy().wait_recv()
+
+            @pl.when(here.core == 0)
+            def _():
+                for kind in kinds:
+                    target[kind] = source[kind]
+
+        edge_rows(ends, range(3), proj, span)
+        go(("edge", 0), first_copy)
+
+        @pl.when(here.core == 1)
+        def _():
+            before_copy().start()
+
         arrived(1, 1)
         gather(1, 5)
         gather(1, 8)
@@ -437,57 +485,11 @@
         gather(1, 6)
         gather(1, 9)
         arrived(1, 0)
-        gather(1, 3)
-        gather(1, 4)
-        arrived(0, 7)
-        project(2)
-
-    def filter_phase(query, gates, prods, grads, ends, heads, sib):
-        def first_copy():
-            return remote(
-                proj.at[:, pl.ds(7 * wide + span, 8), :], first_in, edge_send.at[0], edge_recv.at[0], here.following())
-
-        def before_copy():
-            return remote(ends, before_in, edge_send.at[1], edge_recv.at[1], here.along_x(2))
-
-        def last_copy(which):
-            kinds = pl.ds((0, 2)[which], 2)
-            return remote(
-                grads.at[kinds, pl.ds(0, 8), :], last_in.at[kinds], edge_send.at[2 + which], edge_recv.at[2 + which],
-                here.preceding())
-
-        def after_copy(which):
-            kinds = pl.ds((0, 2)[which], 2)
-            return remote(
-                heads.at[kinds], after_in.at[kinds], edge_send.at[4 + which], edge_recv.at[4 + which],
-                here.along_x(2))
-
-        def edge_rows(target, kinds, source, offset):
-            for kind in kinds:
-                for pair in range(4):
-                    rows = [source[kind, pl.ds((2 * pair + index) * wide + offset, 8), :] for index in range(2)]
-                    target[kind, pl.ds(pair * 16, 16), :] = jnp.concatenate(rows).astype(bf16)
-
-        def share(target, kinds, copy, source):
-            @pl.when(here.core == 1)
-            def _():
-                copy().wait_recv()
-
-            @pl.when(here.core == 0)
-            def _():
-                for kind in kinds:
-                    target[kind] = source[kind]
-
-        edge_rows(ends, range(3), proj, span)
-        go(("edge", 0), first_copy)
-
-        @pl.when(here.core == 1)
-        def _():
-            before_copy().start()
-
         arrived(1, 5)
         arrived(1, 6)
         gather(1, 7)
+        gather(1, 3)
+        gather(1, 4)
         first_copy().wait_recv()
         share(before_in, range(3), before_copy, ends)
         for kind in range(3):

time: 151 us -> 146 us (0.967)
  Pallas kernels: 149 us -> 145 us
    pallas_call x1, Pallas kernels: 146 us -> 143 us  [layer_results(): pl.pallas_call(body, out_shape=(jax.ShapeDtypeStruct((block, width), bf16...]
where the time goes in v10:
time: 146 us
  Pallas kernels  145 us (99%)
    pallas_call x1, Pallas kernels, layer_results(): pl.pallas_call(body, out_shape=(jax.ShapeDtypeStruct((block, width), bf16...  143 us

profile of v10, /device:TPU:0, one launch (start us, length us, event | category | flops | bytes accessed | tf_op | source)
XLA Modules:
  0.0 146.2 jit_solution(7090254481935678580)
XLA Ops:
  0.6 142.8 %whole_layer.1 = (bf16[64,4096]{1,0:T(8,128)(2,1)}, bf16[64,4096]{1,0:T(8,128)(2,1)}, bf16[3,256,512]{2,1,0:T(8,128)(2,1)}, bf16[512,256]{1,0:T(8,128)(2,1)}, f32[16,512]{1,0:T(8,128)}) custom-call(bf16[64,4096]{1,0:T(8,128)(2,1)} %refs_0_.1, bf16[64,4096]{1,0:T(8,128)(2,1)} %refs_1_.1, f32[1,4096]{1,0:T(1,128)} %bitcast.4, f32[3,3,512]{2,1,0:T(4,128)} %refs_3_.1, ...), custom_call_target="tpu_custom_call" | custom-call | tf_op jit(solution)/shard_map/whole_layer/pallas_call | solution.py:817
  143.4 2.6 %place_results.1 = (bf16[64,4096]{1,0:T(8,128)(2,1)}, bf16[64,4096]{1,0:T(8,128)(2,1)}, bf16[3,256,512]{2,1,0:T(8,128)(2,1)}, bf16[512,256]{1,0:T(8,128)(2,1)}, f32[3,3,512]{2,1,0:T(4,128)}, /*index=5*/f32[7,512]{1,0:T(8,128)}) custom-call(bf16[64,4096]{1,0:T(8,128)(2,1)} %get-tuple-element.17.layer, bf16[64,4096]{1,0:T(8,128)(2,1)} %get-tuple-element.18.grad, ...), custom_call_target="tpu_custom_call" | custom-call | tf_op jit(solution)/shard_map/place_results/pallas_call | solution.py:902

commit v11 on v10

--- a/solution.py
+++ b/solution.py
@@ -86,7 +86,7 @@
     steps = chans // 128
     bands = tokens // span
     step_in = 512
-    x_cols = ((width // 128 * 3 // 4) * 128, (width // 128 // 2) * 128)
+    x_cols = ((width // 128 * 15 // 16) * 128, (width // 128 // 2) * 128)
     bf16, f32 = jnp.bfloat16, jnp.float32
 
     out_load = pltpu.make_async_copy(out_w_hbm, out_w, load_sem.at[3])
@@ -559,11 +559,8 @@
             part[:, cols] = value.astype(bf16)
             return carry
 
-        lax.fori_loop(0, width // chans, branch_product, 0)
-
         for slot in (3, 4, 7, 8, 9):
             arrived(1, slot)
-        tp_begin(0)
         for_sibling(0, sib, 0)
         for_sibling(0, sib, 1)
         for_sibling(0, sib, 2)
@@ -575,6 +572,8 @@
         y_go(0, 0, 2)
         for_self(0, sib, 2)
         y_go(0, 0, 3)
+        lax.fori_loop(0, width // chans, branch_product, 0)
+        tp_begin(0)
         value = lax.dot_general(both[1], out_w[...], (((1,), (1,)), ((), ())), preferred_element_type=f32)
         for index in range(8):
             rows = pl.ds(index * span, span)
@@ -657,8 +656,6 @@
         tiles = (bands // 2) * steps
         lax.fori_loop(0, tiles - steps, backward, 0)
         y_pass(0, 1)
-        tp_halves(0)
-        tp_last(0)
         lax.fori_loop(tiles - steps, tiles, backward, 0)
         turn_tile(tiles - 1)
         lag_sum[0] = jnp.sum(lags[...], axis=1) * scale
@@ -712,7 +709,8 @@
         for_self(1, sib, 0)
         y_go(1, 0, 0)
         y_go(1, 0, 1)
-        tp_direct(0)
+        tp_halves(0)
+        tp_last(0)
         for_sibling(1, sib, 2)
         for_self(1, sib, 1)
         y_go(1, 0, 2)
@@ -721,6 +719,7 @@
         y_go(1, 0, 3)
         lag_step(0)
         x_on(0)
+        tp_direct(0)
         in_steps = width // step_in
         gnorm_product(0, in_steps // 2)
         y_pass(1, 0)

time: 146 us -> 151 us (1.034); the launches traced: 146 us -> 148 us
  Pallas kernels: 145 us -> 147 us
    pallas_call x1, Pallas kernels: 143 us -> 145 us  [layer_results(): pl.pallas_call(body, out_shape=(jax.ShapeDtypeStruct((block, width), bf16...]
where the time goes in v11:
time: 151 us; the launch traced here: 148 us
  Pallas kernels  147 us (97%)
    pallas_call x1, Pallas kernels, layer_results(): pl.pallas_call(body, out_shape=(jax.ShapeDtypeStruct((block, width), bf16...  145 us

profile of v11, /device:TPU:0, one launch (start us, length us, event | category | flops | bytes accessed | tf_op | source)
XLA Modules:
  0.0 148.2 jit_solution(4133056167554100980)
XLA Ops:
  0.6 144.9 %whole_layer.1 = (bf16[64,4096]{1,0:T(8,128)(2,1)}, bf16[64,4096]{1,0:T(8,128)(2,1)}, bf16[3,256,512]{2,1,0:T(8,128)(2,1)}, bf16[512,256]{1,0:T(8,128)(2,1)}, f32[16,512]{1,0:T(8,128)}) custom-call(bf16[64,4096]{1,0:T(8,128)(2,1)} %refs_0_.1, bf16[64,4096]{1,0:T(8,128)(2,1)} %refs_1_.1, f32[1,4096]{1,0:T(1,128)} %bitcast.4, f32[3,3,512]{2,1,0:T(4,128)} %refs_3_.1, ...), custom_call_target="tpu_custom_call" | custom-call | tf_op jit(solution)/shard_map/whole_layer/pallas_call | solution.py:816
  145.5 2.6 %place_results.1 = (bf16[64,4096]{1,0:T(8,128)(2,1)}, bf16[64,4096]{1,0:T(8,128)(2,1)}, bf16[3,256,512]{2,1,0:T(8,128)(2,1)}, bf16[512,256]{1,0:T(8,128)(2,1)}, f32[3,3,512]{2,1,0:T(4,128)}, /*index=5*/f32[7,512]{1,0:T(8,128)}) custom-call(bf16[64,4096]{1,0:T(8,128)(2,1)} %get-tuple-element.17.layer, bf16[64,4096]{1,0:T(8,128)(2,1)} %get-tuple-element.18.grad, ...), custom_call_target="tpu_custom_call" | custom-call | tf_op jit(solution)/shard_map/place_results/pallas_call | solution.py:901
